TPU v7x, 32 devices: a whole 2x2x4 slice. The times are simulated.
32 devices in a mesh: sec: 8 (over z, x), row: 4 (over y, core).
Axes of the slice: x: 2, y: 2, z: 4, core: 2. Of those that a mesh axis runs over, the one named last changes fastest.
Arguments:
- corner_ul: bfloat16 [8, 1024, 1024], P('sec', 'row'), may hold values from -6 to 6
- corner_ur: bfloat16 [8, 1024, 1024], P('sec'), may hold values from -0.1875 to 0.1875
- corner_dl: bfloat16 [8, 1024, 1024], P('sec', 'row'), may hold values from -6 to 6
- corner_dr: bfloat16 [8, 1024, 1024], P('sec'), may hold values from -0.1875 to 0.1875
- left_factor: bfloat16 [8, 1024, 16], P('sec', 'row'), may hold values from -0.1875 to 0.1875
- right_factor: bfloat16 [8, 1024, 16], P('sec', 'row'), may hold values from -0.1875 to 0.1875
- singular: float32 [8, 16], P('sec'), may hold values from 0.25 to 4
- states: int32 [8], P('sec'), may hold values from 8 to 16, as said below
- kept: int32 [8], P('sec'), may hold values from 8 to 16, as said below
- joining_map: int32 [8, 16], P('sec'), may hold values from 0 to 15, each once within a row
Outputs:
- proj_tilde: bfloat16 [8, 1024, 16], P('sec', 'row')
- proj: bfloat16 [8, 1024, 16], P('sec', 'row')
- intersection: float32 [8, 16, 16], P('sec')
Inputs may be any that keep to these rules, and one draw needn't show every extreme that they name: `states`: at least half of 16; some sector has all 16. `kept`: at least half of 16; some sector keeps all 16. `joining_map`: each row is a permutation of 0 to 15.
All inputs are finite; a program needn't handle non-finite values.
Results may differ from a plain program's by a relative error of at most 0.0051.
Values may be sent and summed in bfloat16 or wider, within the bound.
No kernel may reach another device: no remote copies, remote signals or barrier semaphores. Data moves between devices by JAX's collectives and lax.ppermute only.
A program may use at most 64 MiB of HBM per device.

v0:
```python
import jax
import jax.numpy as jnp
from jax import lax
from jax.sharding import PartitionSpec as P


def passed_along(value, axis, steps):
    count = lax.axis_size(axis)
    pairs = [(source, (source + steps) % count) for source in range(count)]
    return lax.ppermute(value, axis, pairs)


def local(
    corner_ul,
    corner_ur,
    corner_dl,
    corner_dr,
    left_factor,
    right_factor,
    singular,
    states,
    kept,
    joining_map,
):
    rows_here = corner_ul.shape[1]
    width = corner_ul.shape[2]
    states_here = joining_map.shape[1]
    bonds = width // states_here
    keep_cols = left_factor.shape[2]
    row_index = lax.axis_index("row")
    positions = row_index * rows_here + jnp.arange(rows_here, dtype=jnp.int32)
    live_rows = (positions % states_here < states[0]).astype(jnp.float32)
    live_cols = (jnp.arange(width, dtype=jnp.int32) % states_here < states[0]).astype(jnp.float32)

    def half(left, right):
        full = jnp.dot(left[0], right[0], preferred_element_type=jnp.float32)
        return (full * live_rows[:, None] * live_cols[None, :]).astype(jnp.bfloat16)

    upper = half(corner_ul, corner_ur)
    lower = half(corner_dl, corner_dr)
    picker = (joining_map[0][:, None] == jnp.arange(states_here, dtype=jnp.int32)[None, :]).astype(
        jnp.bfloat16
    )

    def permute(factor):
        three = factor[0].reshape(rows_here // states_here, states_here, keep_cols)
        moved = jnp.einsum("xz,qxk->qzk", picker, three, preferred_element_type=jnp.float32)
        return moved.astype(jnp.bfloat16).reshape(rows_here, keep_cols)

    u_moved = permute(left_factor)
    v_moved = permute(right_factor)
    u_there = passed_along(u_moved, "sec", -1)
    v_there = passed_along(v_moved, "sec", 1)
    whole_u, whole_v = (
        lax.all_gather(u_there, "row", axis=0, tiled=True),
        lax.all_gather(v_there, "row", axis=0, tiled=True),
    )

    def apply_rows(block, factor):
        block4 = block.reshape(rows_here // states_here, states_here, bonds, states_here)
        factor3 = factor.reshape(bonds, states_here, keep_cols)
        result = jnp.einsum("pzqy,qzk->pyk", block4, factor3, preferred_element_type=jnp.float32)
        return result.reshape(rows_here, keep_cols)

    a_far = apply_rows(upper, whole_u)
    b_far = apply_rows(lower, whole_v)
    a_part = passed_along(a_far, "sec", 1)
    b_part = passed_along(b_far, "sec", -1)
    columns = jnp.arange(keep_cols, dtype=jnp.int32)
    weight = jnp.where(columns < kept[0], 1.0 / jnp.sqrt(singular[0]), 0.0)
    scaled_a = a_part * weight[None, :]
    scaled_b = b_part * weight[None, :]
    partial_intersection = jnp.dot(
        scaled_a.T, scaled_b, precision=lax.Precision.HIGHEST, preferred_element_type=jnp.float32
    )
    intersection = lax.psum(partial_intersection, "row") / jnp.sqrt(jnp.float32(width))
    return (
        scaled_a.astype(jnp.bfloat16)[None],
        scaled_b.astype(jnp.bfloat16)[None],
        intersection[None],
    )


def solution(mesh):
    placed = (
        P("sec", "row", None),
        P("sec", None, None),
        P("sec", "row", None),
        P("sec", None, None),
        P("sec", "row", None),
        P("sec", "row", None),
        P("sec", None),
        P("sec"),
        P("sec"),
        P("sec", None),
    )
    return jax.shard_map(
        local,
        mesh=mesh,
        in_specs=placed,
        out_specs=(P("sec", "row", None), P("sec", "row", None), P("sec", None, None)),
        check_vma=False,
    )
```

profile of v0, /device:TPU:0, one launch (start us, length us, event | category | flops | bytes accessed | tf_op | source)
XLA Modules:
  0.0 59.7 jit_solution(7328211177463114116)
XLA Ops:
  0.6 0.0 copy-start
  0.6 1.0 %copy.27 = bf16[1,256,16]{2,1,0:T(8,128)(2,1)S(1)} copy(bf16[1,256,16]{1,2,0:T(8,128)(2,1)} %param.14) | data formatting | bytes 16384 | tf_op jit(solution)/shard_map/reshape;squeeze | solution.py:46
  1.6 0.8 %convolution_convert_fusion.1 = bf16[16,16,16]{2,0,1:T(8,128)(2,1)S(1)} fusion(bf16[16,16,16]{2,1,0:T(8,128)(2,1)S(1)} %bitcast.76, s32[16]{0:T(128)} %bitcast.78), kind=kOutput, calls=%fused_computation.11 | convolution fusion | flops 135424 | bytes 16448 | tf_op jit(solution)/shard_map/xz,qxk->qzk/dot_general | solution.py:47
  2.4 0.1 copy.19
  2.5 6.0 %collective-permute-start = (bf16[256,16]{0,1:T(8,128)(2,1)S(1)}, bf16[256,16]{0,1:T(8,128)(2,1)S(1)}, u32[]{:S(2)}, u32[]{:S(2)}) collective-permute-start(bf16[256,16]{0,1:T(8,128)(2,1)S(1)} %copy.19), channel_id=1, source_target_pairs={{0,28},{4,0},{8,4},{12,8},{16,12},{20,16},{24,20},{28,24},{1,29},{... | collective-permute-start | bytes 24584 | tf_op jit(solution)/shard_map/ppermute | solution.py:10
  8.5 0.8 %copy.28 = bf16[1,256,16]{2,1,0:T(8,128)(2,1)S(1)} copy(bf16[1,256,16]{1,2,0:T(8,128)(2,1)} %param.15) | data formatting | bytes 16384 | tf_op jit(solution)/shard_map/reshape;squeeze | solution.py:46
  9.3 0.8 %convolution_convert_fusion = bf16[16,16,16]{2,0,1:T(8,128)(2,1)S(1)} fusion(bf16[16,16,16]{2,1,0:T(8,128)(2,1)S(1)} %bitcast.77, s32[16]{0:T(128)} %bitcast.79), kind=kOutput, calls=%fused_computation.10 | convolution fusion | flops 135424 | bytes 16448 | tf_op jit(solution)/shard_map/xz,qxk->qzk/dot_general | solution.py:47
  10.1 0.1 copy.24
  10.1 0.0 collective-permute-start.2
  10.9 0.0 copy-start.1
  10.9 0.0 copy-done
  10.9 1.9 %fusion.19 = bf16[256,1024]{1,0:T(8,128)(2,1)S(1)} fusion(bf16[1,1024,1024]{2,1,0:T(8,128)(2,1)S(1)} %copy-done, bf16[1,256,1024]{2,1,0:T(8,128)(2,1)} %param.10, f32[1024]{0:T(1024)S(1)} %fusion.39, f32[256]{0:T(256)S(1)} %compare_convert_fusion), kind=kOutput, calls=%fused_computation.9 | convolution fusion | flops 537657344 | bytes 3150848 | tf_op jit(solution)/shard_map/dot_general | solution.py:36
  12.8 0.0 copy-done.1
  12.8 1.8 %fusion.16 = bf16[256,1024]{1,0:T(8,128)(2,1)S(1)} fusion(bf16[1,1024,1024]{2,1,0:T(8,128)(2,1)S(1)} %copy-done.1, bf16[1,256,1024]{2,1,0:T(8,128)(2,1)} %param.12, f32[1024]{0:T(1024)S(1)} %fusion.39, f32[256]{0:T(256)S(1)} %compare_convert_fusion), kind=kOutput, calls=%fused_computation.8 | convolution fusion | flops 537657344 | bytes 3150848 | tf_op jit(solution)/shard_map/dot_general | solution.py:36
  14.6 4.5 %reshape.64 = bf16[16,16,64,16]{3,2,1,0:T(8,128)(2,1)} reshape(bf16[256,1024]{1,0:T(8,128)(2,1)S(1)} %fusion.19) | data formatting | bytes 1048576 | tf_op jit(solution)/shard_map/reshape | solution.py:60
  19.1 4.6 %copy.29 = bf16[16,16,64,16]{2,1,0,3:T(8,128)(2,1)} copy(bf16[16,16,64,16]{1,2,3,0:T(8,128)(2,1)} %bitcast.70) | data formatting | bytes 1048576 | tf_op jit(solution)/shard_map/pzqy,qzk->pyk/dot_general | solution.py:62
  23.7 4.5 %reshape.67 = bf16[16,16,64,16]{3,2,1,0:T(8,128)(2,1)} reshape(bf16[256,1024]{1,0:T(8,128)(2,1)S(1)} %fusion.16) | data formatting | bytes 1048576 | tf_op jit(solution)/shard_map/reshape | solution.py:60
  28.2 3.6 %copy.30 = bf16[16,16,64,16]{2,1,0,3:T(8,128)(2,1)S(1)} copy(bf16[16,16,64,16]{1,2,3,0:T(8,128)(2,1)} %bitcast.71) | data formatting | bytes 1048576 | tf_op jit(solution)/shard_map/pzqy,qzk->pyk/dot_general | solution.py:62
  31.8 0.0 copy-start.2
  32.5 0.0 collective-permute-done
  32.5 5.2 %all_gather.6 = bf16[1024,16]{0,1:T(8,128)(2,1)S(1)} all-gather(bf16[256,16]{0,1:T(8,128)(2,1)S(1)} %collective-permute-done), channel_id=1, replica_groups=mesh['sec'=8,'row'=4] {'row'}, dimensions={0}, use_global_device_ids=true | all-gather | bytes 40960 | tf_op jit(solution)/shard_map/all_gather | solution.py:55
  37.7 0.2 reshape.66
  37.9 0.1 copy.21
  38.1 1.6 %convolution_bitcast_fusion.1 = f32[256,16]{0,1:T(8,128)S(1)} fusion(bf16[64,16,16]{0,2,1:T(8,128)(2,1)S(1)} %copy.21, bf16[256,64,16]{1,0,2:T(8,128)(2,1)} %bitcast.73), kind=kOutput, calls=%fused_computation.13 | convolution fusion | flops 8388608 | bytes 573440 | tf_op jit(solution)/shard_map/pzqy,qzk->pyk/dot_general | solution.py:62
  39.7 0.0 collective-permute-start.1
  39.7 0.0 collective-permute-done.2
  39.7 5.2 %all_gather.7 = bf16[1024,16]{0,1:T(8,128)(2,1)S(1)} all-gather(bf16[256,16]{0,1:T(8,128)(2,1)S(1)} %collective-permute-done.2), channel_id=1, replica_groups=mesh['sec'=8,'row'=4] {'row'}, dimensions={0}, use_global_device_ids=true | all-gather | bytes 40960 | tf_op jit(solution)/shard_map/all_gather | solution.py:56
  44.9 0.2 reshape.69
  45.1 0.1 copy.26
  45.3 0.4 convolution_bitcast_fusion
  45.6 4.7 %collective-permute-start.3 = (f32[256,16]{0,1:T(8,128)S(1)}, f32[256,16]{0,1:T(8,128)S(1)}, u32[]{:S(2)}, u32[]{:S(2)}) collective-permute-start(f32[256,16]{0,1:T(8,128)S(1)} %convolution_bitcast_fusion), channel_id=1, source_target_pairs={{0,28},{4,0},{8,4},{12,8},{16,12},{20,16},{24,20},{28,24},{1,29},{... | collective-permute-start | bytes 49160 | tf_op jit(solution)/shard_map/ppermute | solution.py:10
  50.4 0.0 copy-done.2
  50.4 0.0 collective-permute-done.1
  50.4 1.4 %collective-permute-done.3 = f32[256,16]{0,1:T(8,128)S(1)} collective-permute-done((f32[256,16]{0,1:T(8,128)S(1)}, f32[256,16]{0,1:T(8,128)S(1)}, u32[]{:S(2)}, u32[]{:S(2)}) %collective-permute-start.3) | collective-permute-done | bytes 16416 | tf_op jit(solution)/shard_map/ppermute | solution.py:10
  51.8 0.2 fusion.24
  52.0 6.4 %psum.7 = f32[16,16]{1,0:T(8,128)S(1)} all-reduce(f32[16,16]{1,0:T(8,128)S(1)} %fusion.24), channel_id=1, replica_groups=mesh['sec'=8,'row'=4] {'row'}, use_global_device_ids=true, to_apply=%region_0.1 | all-reduce | flops 256 | bytes 2048 | tf_op jit(solution)/shard_map/psum | solution.py:76
  58.4 0.6 %multiply_bitcast_fusion = f32[1,16,16]{2,1,0:T(8,128)} fusion(f32[16,16]{1,0:T(8,128)S(1)} %psum.7), kind=kLoop, calls=%fused_computation.23 | loop fusion | flops 256 | bytes 2048 | tf_op jit(solution)/shard_map/broadcast_in_dim | solution.py:80
  59.0 0.7 %fusion.28 = (bf16[1,256,16]{1,2,0:T(8,128)(2,1)}, bf16[1,256,16]{1,2,0:T(8,128)(2,1)}) fusion(f32[256,16]{0,1:T(8,128)S(1)} %collective-permute-done.3, f32[16]{0:T(128)S(1)} %fusion.41, f32[256,16]{0,1:T(8,128)S(1)} %collective-permute-done.1), kind=kLoop, calls=%fused_computation.22 | loop fusion | flops 16384 | bytes 49216 | tf_op jit(solution)/shard_map/broadcast_in_dim | solution.py:79
  (3 shorter events, 0.0 us)
Async XLA Ops:
  0.6 10.3 %copy-start = (bf16[1,1024,1024]{2,1,0:T(8,128)(2,1)S(1)}, bf16[1,1024,1024]{2,1,0:T(8,128)(2,1)}, u32[]{:S(2)}) copy-start(bf16[1,1024,1024]{2,1,0:T(8,128)(2,1)} %param.11) | copy-start | bytes 6291460
  2.5 30.0 %collective-permute-start = (bf16[256,16]{0,1:T(8,128)(2,1)S(1)}, bf16[256,16]{0,1:T(8,128)(2,1)S(1)}, u32[]{:S(2)}, u32[]{:S(2)}) collective-permute-start(bf16[256,16]{0,1:T(8,128)(2,1)S(1)} %copy.19), channel_id=1, source_target_pairs={{0,28},{4,0},{8,4},{12,8},{16,12},{20,16},{24,20},{28,24},{1,29},{... | collective-permute-start | bytes 24584 | tf_op jit(solution)/shard_map/ppermute | solution.py:10
  10.1 29.6 %collective-permute-start.2 = (bf16[256,16]{0,1:T(8,128)(2,1)S(1)}, bf16[256,16]{0,1:T(8,128)(2,1)S(1)}, u32[]{:S(2)}, u32[]{:S(2)}) collective-permute-start(bf16[256,16]{0,1:T(8,128)(2,1)S(1)} %copy.24), channel_id=1, source_target_pairs={{0,4},{4,8},{8,12},{12,16},{16,20},{20,24},{24,28},{28,0},{1,5},{5... | collective-permute-start | bytes 24584 | tf_op jit(solution)/shard_map/ppermute | solution.py:10
  10.9 1.9 %copy-start.1 = (bf16[1,1024,1024]{2,1,0:T(8,128)(2,1)S(1)}, bf16[1,1024,1024]{2,1,0:T(8,128)(2,1)}, u32[]{:S(2)}) copy-start(bf16[1,1024,1024]{2,1,0:T(8,128)(2,1)} %param.13) | copy-start | bytes 6291460
  31.8 18.6 %copy-start.2 = (f32[1,16]{1,0:T(1,128)S(1)}, f32[1,16]{1,0:T(1,128)}, u32[]{:S(2)}) copy-start(f32[1,16]{1,0:T(1,128)} %param.16) | copy-start | bytes 196
  39.7 10.7 %collective-permute-start.1 = (f32[256,16]{0,1:T(8,128)S(1)}, f32[256,16]{0,1:T(8,128)S(1)}, u32[]{:S(2)}, u32[]{:S(2)}) collective-permute-start(f32[256,16]{0,1:T(8,128)S(1)} %convolution_bitcast_fusion.1), channel_id=1, source_target_pairs={{0,4},{4,8},{8,12},{12,16},{16,20},{20,24},{24,28},{28,0},{1,5},{5... | collective-permute-start | bytes 49160 | tf_op jit(solution)/shard_map/ppermute | solution.py:10
  45.6 6.2 %collective-permute-start.3 = (f32[256,16]{0,1:T(8,128)S(1)}, f32[256,16]{0,1:T(8,128)S(1)}, u32[]{:S(2)}, u32[]{:S(2)}) collective-permute-start(f32[256,16]{0,1:T(8,128)S(1)} %convolution_bitcast_fusion), channel_id=1, source_target_pairs={{0,28},{4,0},{8,4},{12,8},{16,12},{20,16},{24,20},{28,24},{1,29},{... | collective-permute-start | bytes 49160 | tf_op jit(solution)/shard_map/ppermute | solution.py:10
where the time goes:
time: 60.2 us; the launch traced here: 59.7 us
  local copies, waits for them, and re-layouts  19.9 us (33%)
  blocking collectives  16.8 us (28%)
  starting transfers between devices  10.8 us (18%)
  matrix products  7.38 us (12%)
  between operations  2.09 us (3%)
  waiting for transfers between devices  1.47 us (2%)
  other arithmetic  1.3 us (2%)
    ppermute x4, starting transfers between devices, passed_along(): return lax.ppermute(value, axis, pairs)  10.8 us
    reshape x2, local copies, waits for them, and re-layouts, apply_rows(): block.reshape(rows_here // states_here, states_here, bonds, states_here)  9.06 us
    dot_general x2, local copies, waits for them, and re-layouts, apply_rows(): jnp.einsum('pzqy,qzk->pyk', block4, factor3, preferred_element_type=jnp.f...  8.2 us
    psum x1, blocking collectives, local(): lax.psum(partial_intersection, 'row') / jnp.sqrt(jnp.float32(width))  6.36 us
    all_gather x1, blocking collectives, local(): lax.all_gather(v_there, 'row', axis=0, tiled=True)  5.19 us
    all_gather x1, blocking collectives, local(): lax.all_gather(u_there, 'row', axis=0, tiled=True)  5.19 us
    dot_general x2, matrix products, half(): full = jnp.dot(left[0], right[0], preferred_element_type=jnp.float32)  3.66 us
    dot_general x2, matrix products, apply_rows(): jnp.einsum('pzqy,qzk->pyk', block4, factor3, preferred_element_type=jnp.f...  1.94 us
  transfers between devices with their start and end apart: 4, of which 1 were waited for; matrix products, arithmetic and copies ran while one was open for 42% of the time, Pallas kernels for 0%

commit v1 on v0

v1 whole, which is shorter than its diff:
```python
import functools

import jax
import jax.numpy as jnp
from jax import lax
from jax.experimental import pallas as pl
from jax.experimental.pallas import tpu as pltpu
from jax.sharding import PartitionSpec as P

LANES = 128
F32, BF16 = jnp.float32, jnp.bfloat16
VMEM_BYTES = 24 * 1024 * 1024


def iota(shape, dim):
    return lax.broadcasted_iota(jnp.int32, shape, dim)


def is_upper():
    return lax.axis_index("row") % 2 == 1


def order_kernel(map_ref, u_ref, u_got_ref, v_ref, v_got_ref, out_ref):
    states_here = map_ref.shape[1]
    lane = iota((LANES, LANES), 1)
    row = iota((LANES, LANES), 0)
    wanted = jnp.zeros((LANES, LANES), jnp.int32)
    for x in range(states_here):
        wanted = jnp.where(lane % states_here == map_ref[0, x], x, wanted)
    same_bond = row // states_here == lane // states_here
    mover = jnp.where(same_bond & (row % states_here == wanted), 1.0, 0.0).astype(BF16)
    mine = is_upper()
    first = jnp.where(mine, u_got_ref[...], v_ref[...])
    second = jnp.where(mine, u_ref[...], v_got_ref[...])
    both = jnp.concatenate([first, second], axis=1)
    for start in range(0, both.shape[1], LANES):
        moved = jnp.dot(both[:, start : start + LANES], mover, preferred_element_type=F32)
        out_ref[:, start : start + LANES] = moved.astype(BF16)


def half_kernel(states_ref, ul, ul_got, ur, dl, dl_got, dr, out_ref, left, right, sems, *, parts, states_here):
    rows, width = ul.shape
    step = width // parts
    mine = is_upper()

    def copies(first, second, matrix):
        todo = [
            pltpu.make_async_copy(first, left.at[pl.ds(0, rows)], sems.at[0]),
            pltpu.make_async_copy(second, left.at[pl.ds(rows, rows)], sems.at[1]),
        ]
        for n in range(parts):
            columns = pl.ds(n * step, step)
            todo.append(pltpu.make_async_copy(matrix.at[:, columns], right.at[:, columns], sems.at[2 + n]))
        return todo

    @pl.when(mine)
    def _():
        for copy in copies(ul_got, ul, ur):
            copy.start()

    @pl.when(jnp.logical_not(mine))
    def _():
        for copy in copies(dl, dl_got, dr):
            copy.start()

    waits = copies(ul, ul, ur)
    group = LANES // states_here
    live_states = states_ref[0]
    lane = iota((1, LANES), 1)
    live = (iota((states_here, LANES), 0) < live_states) & (
        iota((states_here, LANES), 1) % states_here < live_states
    )
    waits[0].wait()
    waits[1].wait()
    for n in range(parts):
        waits[2 + n].wait()
        full = jnp.dot(left[...], right[:, n * step : (n + 1) * step], preferred_element_type=F32)
        for p in range(0, 2 * rows, LANES):
            for q in range(0, step, LANES):
                block = full[p : p + LANES, q : q + LANES]
                distance = 1
                while distance < group:
                    four = block.reshape(group // (2 * distance), 2, distance * states_here, LANES)
                    size = group // 2 * states_here
                    low = four[:, 0].reshape(size, LANES)
                    high = four[:, 1].reshape(size, LANES)
                    odd = (lane // states_here // distance) % 2 == 1
                    shift = distance * states_here
                    new_low = jnp.where(odd, pltpu.roll(high, shift, 1), low)
                    new_high = jnp.where(odd, high, pltpu.roll(low, LANES - shift, 1))
                    shape = (group // (2 * distance), 1, distance * states_here, LANES)
                    block = jnp.concatenate([new_low.reshape(shape), new_high.reshape(shape)], axis=1)
                    block = block.reshape(LANES, LANES)
                    distance *= 2
                three = jnp.where(live[None], block.reshape(group, states_here, LANES), 0.0)
                out_ref[n * step + q : n * step + q + LANES, p : p + LANES] = three.reshape(
                    LANES, LANES
                ).astype(BF16)


def apply_kernel(*refs):
    *factors, half_ref, out_ref = refs
    chips = len(factors)
    chip = lax.axis_index("row") // 2
    depth = factors[0].shape[1]
    total = jnp.zeros(out_ref.shape, F32)
    for away in range(chips):
        source = lax.rem(chip - away + chips, chips)
        part = half_ref[pl.ds(pl.multiple_of(source * depth, depth), depth), :]
        total += jnp.dot(factors[away][...], part, preferred_element_type=F32)
    out_ref[...] = total.astype(BF16)


def finish_kernel(kept_ref, singular_ref, *refs, width):
    *parts, tilde_ref, proj_ref, inter_ref = refs
    chips = len(parts) // 2
    mine, got = parts[:chips], parts[chips:]
    keep_cols, rows = tilde_ref.shape
    core = lax.axis_index("row") % 2
    chip = lax.axis_index("row") // 2
    upper = is_upper()
    column = iota((1, keep_cols), 1)
    weight = jnp.where(column < kept_ref[0], 1.0 / jnp.sqrt(singular_ref[...]), 0.0)
    square = (keep_cols, keep_cols)
    diagonal = iota(square, 0) == iota(square, 1)
    weight_rows = jnp.sum(jnp.where(diagonal, weight, 0.0), axis=1, keepdims=True)
    products = []
    for away in range(chips):
        a = jnp.where(upper, mine[away][...], got[away][...])
        b = jnp.where(upper, got[away][...], mine[away][...])
        if away == 0:
            for whole, ref in ((a, tilde_ref), (b, proj_ref)):
                own = jnp.where(core == 0, whole[:, :rows], whole[:, rows:])
                ref[...] = (own.astype(F32) * weight_rows).astype(BF16)
        products.append(lax.dot_general(a, b, (((1,), (1,)), ((), ())), preferred_element_type=F32))
    total = jnp.zeros(square, F32)
    for source in range(chips):
        for away in range(chips):
            here = lax.rem(chip - away + chips, chips) == source
            total += jnp.where(here, products[away], 0.0)
    inter_ref[...] = total * weight_rows * weight / jnp.sqrt(jnp.float32(width))


def in_vmem():
    return pl.BlockSpec(memory_space=pltpu.VMEM)


def in_smem():
    return pl.BlockSpec(memory_space=pltpu.SMEM)


def local(
    sectors,
    row_devices,
    corner_ul,
    corner_ur,
    corner_dl,
    corner_dr,
    left_factor,
    right_factor,
    singular,
    states,
    kept,
    joining_map,
):
    rows, width = corner_ul.shape[1:]
    states_here = joining_map.shape[1]
    keep_cols = left_factor.shape[2]
    chips = row_devices // 2

    def other_core(value):
        return lax.ppermute(value, "row", [(i, i ^ 1) for i in range(row_devices)])

    def to_sector(value, upper_step, away):
        pairs = []
        for s in range(sectors):
            for r in range(row_devices):
                t = (s + (upper_step if r % 2 else -upper_step)) % sectors
                pairs.append((s * row_devices + r, t * row_devices + (r + 2 * away) % row_devices))
        return lax.ppermute(value, ("sec", "row"), pairs)

    u, v = left_factor[0].T, right_factor[0].T
    u_got, v_got = other_core(u), other_core(v)
    ul, dl = corner_ul[0], corner_dl[0]
    ul_got, dl_got = other_core(ul), other_core(dl)

    ordered = pl.pallas_call(
        order_kernel,
        out_shape=jax.ShapeDtypeStruct((keep_cols, 2 * rows), BF16),
        in_specs=[in_smem()] + [in_vmem()] * 4,
        out_specs=in_vmem(),
        name="order_factor",
    )(joining_map, u, u_got, v, v_got)
    factors = [to_sector(ordered, -1, away) for away in range(chips)]

    parts = width // (2 * LANES)
    anywhere = pl.BlockSpec(memory_space=pl.ANY)
    half = pl.pallas_call(
        functools.partial(half_kernel, parts=parts, states_here=states_here),
        out_shape=jax.ShapeDtypeStruct((width, 2 * rows), BF16),
        in_specs=[in_smem()] + [anywhere] * 6,
        out_specs=in_vmem(),
        scratch_shapes=[
            pltpu.VMEM((2 * rows, width), BF16),
            pltpu.VMEM((width, width), BF16),
            pltpu.SemaphoreType.DMA((2 + parts,)),
        ],
        compiler_params=pltpu.CompilerParams(vmem_limit_bytes=VMEM_BYTES),
        cost_estimate=pl.CostEstimate(
            flops=4 * rows * width * width, bytes_accessed=2 * width * (width + 4 * rows), transcendentals=0
        ),
        name="half_product",
    )(states, ul, ul_got, corner_ur[0], dl, dl_got, corner_dr[0])

    applied = pl.pallas_call(
        apply_kernel,
        out_shape=jax.ShapeDtypeStruct((keep_cols, 2 * rows), BF16),
        in_specs=[in_vmem()] * (chips + 1),
        out_specs=in_vmem(),
        compiler_params=pltpu.CompilerParams(vmem_limit_bytes=VMEM_BYTES),
        name="apply_factor",
    )(*factors, half)
    mine = [to_sector(applied, 1, away) for away in range(chips)]
    got = [other_core(value) for value in mine]

    tilde, proj, inter = pl.pallas_call(
        functools.partial(finish_kernel, width=width),
        out_shape=(
            jax.ShapeDtypeStruct((keep_cols, rows), BF16),
            jax.ShapeDtypeStruct((keep_cols, rows), BF16),
            jax.ShapeDtypeStruct((keep_cols, keep_cols), F32),
        ),
        in_specs=[in_smem()] + [in_vmem()] * (2 * chips + 1),
        out_specs=(in_vmem(), in_vmem(), in_vmem()),
        name="finish",
    )(kept, singular, *mine, *got)
    return tilde.T[None], proj.T[None], inter[None]


def solution(mesh):
    placed = (
        P("sec", "row", None),
        P("sec", None, None),
        P("sec", "row", None),
        P("sec", None, None),
        P("sec", "row", None),
        P("sec", "row", None),
        P("sec", None),
        P("sec"),
        P("sec"),
        P("sec", None),
    )
    return jax.shard_map(
        functools.partial(local, mesh.shape["sec"], mesh.shape["row"]),
        mesh=mesh,
        in_specs=placed,
        out_specs=(P("sec", "row", None), P("sec", "row", None), P("sec", None, None)),
        check_vma=False,
    )
```

time: 60.2 us -> 34.2 us (0.57)
  blocking collectives: 16.8 us -> 0 us
  local copies, waits for them, and re-layouts: 19.9 us -> 7.47 us
  Pallas kernels: 0 us -> 7.44 us
  matrix products: 7.38 us -> 0 us
  starting transfers between devices: 10.8 us -> 13.5 us
  waiting for transfers between devices: 1.47 us -> 3.47 us
  other arithmetic: 1.3 us -> 0 us
    all_gather x2 -> x0, blocking collectives: 10.4 us -> none  [the longest x1 5.19 us: local(): lax.all_gather(v_there, 'row', axis=0, tiled=True)]
    reshape x8 -> x0, local copies, waits for them, and re-layouts: 9.91 us -> none  [the longest x2 9.06 us: apply_rows(): block.reshape(rows_here // states_here, states_here, bonds, states_here)]
    dot_general x2 -> x0, local copies, waits for them, and re-layouts: 8.2 us -> none  [apply_rows(): jnp.einsum('pzqy,qzk->pyk', block4, factor3, preferred_element_type=jnp.f...]
    unnamed x6 -> x20, local copies, waits for them, and re-layouts: 0.02 us -> 7.47 us
    pallas_call x0 -> x4, Pallas kernels: none -> 7.44 us  [the longest x1 4.09 us: local(): pl.pallas_call(functools.partial(half_kernel, parts=parts, states_here=st...]
    dot_general x7 -> x0, matrix products: 7.38 us -> none  [the longest x2 3.66 us: half(): full = jnp.dot(left[0], right[0], preferred_element_type=jnp.float32)]
    psum x1 -> x0, blocking collectives: 6.36 us -> none  [local(): lax.psum(partial_intersection, 'row') / jnp.sqrt(jnp.float32(width))]
    ppermute x4 -> x10, starting transfers between devices: 10.8 us -> 13.5 us  [the longest x4 8.9 us: to_sector(): return lax.ppermute(value, ('sec', 'row'), pairs)]
  transfers between devices with their start and end apart: 4 -> 10, of which waited for: 1 -> 4; matrix products, arithmetic and copies ran while one was open for 42% -> 0% of each run, Pallas kernels for 0% -> 17%
where the time goes in v1:
time: 34.2 us; the launch traced here: 33.8 us
  starting transfers between devices  13.5 us (39%)
  local copies, waits for them, and re-layouts  7.47 us (22%)
  Pallas kernels  7.44 us (22%)
  waiting for transfers between devices  3.47 us (10%)
  between operations  2 us (6%)
    ppermute x4, starting transfers between devices, to_sector(): return lax.ppermute(value, ('sec', 'row'), pairs)  8.9 us
    unnamed x20, local copies, waits for them, and re-layouts  7.47 us
    ppermute x6, starting transfers between devices, other_core(): return lax.ppermute(value, 'row', [(i, i ^ 1) for i in range(row_devices)])  4.57 us
    pallas_call x1, Pallas kernels, local(): pl.pallas_call(functools.partial(half_kernel, parts=parts, states_here=st...  4.09 us
    ppermute x4, waiting for transfers between devices, to_sector(): return lax.ppermute(value, ('sec', 'row'), pairs)  2.02 us
    pallas_call x1, Pallas kernels, local(): pl.pallas_call(order_kernel, out_shape=jax.ShapeDtypeStruct((keep_cols, 2...  1.56 us
    pallas_call x1, Pallas kernels, local(): pl.pallas_call(functools.partial(finish_kernel, width=width), out_shape=(...  1.53 us
    ppermute x6, waiting for transfers between devices, other_core(): return lax.ppermute(value, 'row', [(i, i ^ 1) for i in range(row_devices)])  1.45 us
  transfers between devices with their start and end apart: 10, of which 4 were waited for; matrix products, arithmetic and copies ran while one was open for 0% of the time, Pallas kernels for 17%

profile of v1, /device:TPU:0, one launch (start us, length us, event | category | flops | bytes accessed | tf_op | source)
XLA Modules:
  0.0 33.8 jit_solution(4440237554756021678)
XLA Ops:
  0.6 0.5 %collective-permute-start.4 = (bf16[256,1024]{1,0:T(8,128)(2,1)}, bf16[256,1024]{1,0:T(8,128)(2,1)S(1)}, u32[]{:S(2)}, u32[]{:S(2)}) collective-permute-start(bf16[256,1024]{1,0:T(8,128)(2,1)} %bitcast.19), channel_id=1, source_target_pairs={{0,1},{1,0},{2,3},{3,2},{4,5},{5,4},{6,7},{7,6},{8,9},{9,8},{10,11... | collective-permute-start | bytes 1572872 | tf_op jit(solution)/shard_map/ppermute | solution.py:172
  1.1 0.1 collective-permute-start.5
  1.2 0.4 %collective-permute-start = (bf16[16,256]{1,0:T(8,128)(2,1)}, bf16[16,256]{1,0:T(8,128)(2,1)S(1)}, u32[]{:S(2)}, u32[]{:S(2)}) collective-permute-start(bf16[16,256]{1,0:T(8,128)(2,1)} %bitcast.23), channel_id=1, source_target_pairs={{0,1},{1,0},{2,3},{3,2},{4,5},{5,4},{6,7},{7,6},{8,9},{9,8},{10,11... | collective-permute-start | bytes 24584 | tf_op jit(solution)/shard_map/ppermute | solution.py:172
  1.7 0.1 collective-permute-start.1
  2.4 1.3 %collective-permute-done.u_got_ref = bf16[16,256]{1,0:T(8,128)(2,1)S(1)} collective-permute-done((bf16[16,256]{1,0:T(8,128)(2,1)}, bf16[16,256]{1,0:T(8,128)(2,1)S(1)}, u32[]{:S(2)}, u32[]{:S(2)}) %collective-permute-start) | collective-permute-done | bytes 8224 | tf_op jit(solution)/shard_map/ppermute | solution.py:172
  3.7 0.0 copy-start.8
  3.7 0.0 collective-permute-done.1.v_got_ref
  3.7 0.6 %copy-done.8 = bf16[16,256]{1,0:T(8,128)(2,1)} copy-done((bf16[16,256]{1,0:T(8,128)(2,1)}, bf16[16,256]{1,0:T(8,128)(2,1)S(1)}, u32[]{:S(2)}) %copy-start.8) | copy-done | bytes 8216
  4.3 0.0 copy-start.9
  4.3 0.6 %copy-done.9 = bf16[16,256]{1,0:T(8,128)(2,1)} copy-done((bf16[16,256]{1,0:T(8,128)(2,1)}, bf16[16,256]{1,0:T(8,128)(2,1)S(1)}, u32[]{:S(2)}) %copy-start.9) | copy-done | bytes 8216
  4.9 1.6 %order_factor.1 = bf16[16,512]{1,0:T(8,128)(2,1)} custom-call(s32[1,16]{1,0:T(1,128)} %map_ref.1, bf16[16,256]{1,0:T(8,128)(2,1)} %bitcast.24, bf16[16,256]{1,0:T(8,128)(2,1)} %copy-done.8, bf16[16,256]{1,0:T(8,128)(2,1)} %bitcast.26, bf16[16,256]{1,0:T(8,128)(2,1)} %copy-done.9), custom_call_target="tpu_custom_call" | custom-call | tf_op jit(solution)/shard_map/order_factor/pallas_call | solution.py:187
  6.4 2.9 %collective-permute-start.2 = (bf16[16,512]{1,0:T(8,128)(2,1)}, bf16[16,512]{1,0:T(8,128)(2,1)S(1)}, u32[]{:S(2)}, u32[]{:S(2)}) collective-permute-start(bf16[16,512]{1,0:T(8,128)(2,1)} %order_factor.1), channel_id=1, source_target_pairs={{0,4},{1,29},{2,6},{3,31},{4,8},{5,1},{6,10},{7,3},{8,12},{9,5},{1... | collective-permute-start | bytes 49160 | tf_op jit(solution)/shard_map/ppermute | solution.py:180
  9.3 2.5 %collective-permute-start.3 = (bf16[16,512]{1,0:T(8,128)(2,1)}, bf16[16,512]{1,0:T(8,128)(2,1)S(1)}, u32[]{:S(2)}, u32[]{:S(2)}) collective-permute-start(bf16[16,512]{1,0:T(8,128)(2,1)} %order_factor.1), channel_id=1, source_target_pairs={{0,6},{1,31},{2,4},{3,29},{4,10},{5,3},{6,8},{7,1},{8,14},{9,7},{1... | collective-permute-start | bytes 49160 | tf_op jit(solution)/shard_map/ppermute | solution.py:180
  11.8 0.0 collective-permute-done.4.ul_got
  11.8 0.0 collective-permute-done.5.dl_got
  11.8 0.0 copy-start
  11.8 1.6 %copy-done = bf16[1,1024,1024]{2,1,0:T(8,128)(2,1)S(1)} copy-done((bf16[1,1024,1024]{2,1,0:T(8,128)(2,1)S(1)}, bf16[1,1024,1024]{2,1,0:T(8,128)(2,1)}, u32[]{:S(2)}) %copy-start) | copy-done | bytes 2097176
  13.4 0.0 copy-start.1
  13.4 1.6 %copy-done.1 = bf16[1,1024,1024]{2,1,0:T(8,128)(2,1)S(1)} copy-done((bf16[1,1024,1024]{2,1,0:T(8,128)(2,1)S(1)}, bf16[1,1024,1024]{2,1,0:T(8,128)(2,1)}, u32[]{:S(2)}) %copy-start.1) | copy-done | bytes 2097176
  15.0 0.0 copy-start.2
  15.0 1.0 %copy-done.2 = bf16[1,256,1024]{2,1,0:T(8,128)(2,1)S(1)} copy-done((bf16[1,256,1024]{2,1,0:T(8,128)(2,1)S(1)}, bf16[1,256,1024]{2,1,0:T(8,128)(2,1)}, u32[]{:S(2)}) %copy-start.2) | copy-done | bytes 524312
  16.0 0.0 copy-start.3
  16.0 1.0 %copy-done.3 = bf16[1,256,1024]{2,1,0:T(8,128)(2,1)S(1)} copy-done((bf16[1,256,1024]{2,1,0:T(8,128)(2,1)S(1)}, bf16[1,256,1024]{2,1,0:T(8,128)(2,1)}, u32[]{:S(2)}) %copy-start.3) | copy-done | bytes 524312
  17.1 4.1 %half_product.1.refs_2_ = bf16[1024,512]{1,0:T(8,128)(2,1)S(1)} custom-call(s32[1]{0:T(128)S(6)} %copy.13.states_ref, bf16[256,1024]{1,0:T(8,128)(2,1)S(1)} %bitcast.20, bf16[256,1024]{1,0:T(8,128)(2,1)S(1)} %collective-permute-done.4.ul_got, bf16[1024,1024]{1,0:T(8,128)(2,1)S(1)} %bitcast.17, bf16[256,1024]{1,0:T(8,128)(2,1)S(1)} %bitcast.22, ...), custom_call_target="tpu_custom_call" | custom-call | flops 1073741824 | bytes 4194304 | tf_op jit(solution)/shard_map/half_product/pallas_call | solution.py:198
  21.2 0.0 collective-permute-done.2.refs_0_
  21.2 0.0 collective-permute-done.3.refs_1_
  21.2 0.3 apply_factor.1
  21.4 3.2 %collective-permute-start.6 = (bf16[16,512]{1,0:T(8,128)(2,1)S(1)}, bf16[16,512]{1,0:T(8,128)(2,1)S(1)}, u32[]{:S(2)}, u32[]{:S(2)}) collective-permute-start(bf16[16,512]{1,0:T(8,128)(2,1)S(1)} %apply_factor.1), channel_id=1, source_target_pairs={{0,28},{1,5},{2,30},{3,7},{4,0},{5,9},{6,2},{7,11},{8,4},{9,13},{1... | collective-permute-start | bytes 49160 | tf_op jit(solution)/shard_map/ppermute | solution.py:180
  24.6 0.3 %collective-permute-start.7 = (bf16[16,512]{1,0:T(8,128)(2,1)S(1)}, bf16[16,512]{1,0:T(8,128)(2,1)S(1)}, u32[]{:S(2)}, u32[]{:S(2)}) collective-permute-start(bf16[16,512]{1,0:T(8,128)(2,1)S(1)} %apply_factor.1), channel_id=1, source_target_pairs={{0,30},{1,7},{2,28},{3,5},{4,2},{5,11},{6,0},{7,9},{8,6},{9,15},{1... | collective-permute-start | bytes 49160 | tf_op jit(solution)/shard_map/ppermute | solution.py:180
  25.0 1.1 %collective-permute-done.6.refs_0_ = bf16[16,512]{1,0:T(8,128)(2,1)S(1)} collective-permute-done((bf16[16,512]{1,0:T(8,128)(2,1)S(1)}, bf16[16,512]{1,0:T(8,128)(2,1)S(1)}, u32[]{:S(2)}, u32[]{:S(2)}) %collective-permute-start.6) | collective-permute-done | bytes 16416 | tf_op jit(solution)/shard_map/ppermute | solution.py:180
  26.1 0.0 copy-start.4
  26.1 2.3 %collective-permute-start.8 = (bf16[16,512]{1,0:T(8,128)(2,1)S(1)}, bf16[16,512]{1,0:T(8,128)(2,1)S(1)}, u32[]{:S(2)}, u32[]{:S(2)}) collective-permute-start(bf16[16,512]{1,0:T(8,128)(2,1)S(1)} %collective-permute-done.6.refs_0_), channel_id=1, source_target_pairs={{0,1},{1,0},{2,3},{3,2},{4,5},{5,4},{6,7},{7,6},{8,9},{9,8},{10,11... | collective-permute-start | bytes 49160 | tf_op jit(solution)/shard_map/ppermute | solution.py:172
  28.3 0.9 %collective-permute-done.7.refs_1_ = bf16[16,512]{1,0:T(8,128)(2,1)S(1)} collective-permute-done((bf16[16,512]{1,0:T(8,128)(2,1)S(1)}, bf16[16,512]{1,0:T(8,128)(2,1)S(1)}, u32[]{:S(2)}, u32[]{:S(2)}) %collective-permute-start.7) | collective-permute-done | bytes 16416 | tf_op jit(solution)/shard_map/ppermute | solution.py:180
  29.3 0.0 copy-start.5
  29.3 1.2 %collective-permute-start.9 = (bf16[16,512]{1,0:T(8,128)(2,1)S(1)}, bf16[16,512]{1,0:T(8,128)(2,1)S(1)}, u32[]{:S(2)}, u32[]{:S(2)}) collective-permute-start(bf16[16,512]{1,0:T(8,128)(2,1)S(1)} %collective-permute-done.7.refs_1_), channel_id=1, source_target_pairs={{0,1},{1,0},{2,3},{3,2},{4,5},{5,4},{6,7},{7,6},{8,9},{9,8},{10,11... | collective-permute-start | bytes 49160 | tf_op jit(solution)/shard_map/ppermute | solution.py:172
  31.1 0.0 collective-permute-done.8.refs_2_
  31.1 0.0 copy-start.6
  31.1 0.2 collective-permute-done.9.refs_3_
  31.3 0.0 copy-done.4
  31.3 0.0 copy-done.5
  31.3 0.4 %copy-done.6 = bf16[16,512]{1,0:T(8,128)(2,1)} copy-done((bf16[16,512]{1,0:T(8,128)(2,1)}, bf16[16,512]{1,0:T(8,128)(2,1)S(1)}, u32[]{:S(2)}) %copy-start.6) | copy-done | bytes 16408
  31.7 0.0 copy-start.7
  31.7 0.6 %copy-done.7 = bf16[16,512]{1,0:T(8,128)(2,1)} copy-done((bf16[16,512]{1,0:T(8,128)(2,1)}, bf16[16,512]{1,0:T(8,128)(2,1)S(1)}, u32[]{:S(2)}) %copy-start.7) | copy-done | bytes 16408
  32.3 1.5 %finish.1 = (bf16[16,256]{1,0:T(8,128)(2,1)}, bf16[16,256]{1,0:T(8,128)(2,1)}, f32[16,16]{1,0:T(8,128)}) custom-call(s32[1]{0:T(128)S(6)} %copy.14.kept_ref, f32[1,16]{1,0:T(1,128)} %singular_ref.1, bf16[16,512]{1,0:T(8,128)(2,1)} %copy-done.4, bf16[16,512]{1,0:T(8,128)(2,1)} %copy-done.5, bf16[16,512]{1,0:T(8,128)(2,1)} %copy-done.6, bf16[16,512]{1,0:T(8,128)(2,1)} %copy-done.7), custom_call_target="tpu_custom_call" | custom-call | tf_op jit(solution)/shard_map/finish/pallas_call | solution.py:226
Async XLA Ops:
  0.6 11.2 %collective-permute-start.4 = (bf16[256,1024]{1,0:T(8,128)(2,1)}, bf16[256,1024]{1,0:T(8,128)(2,1)S(1)}, u32[]{:S(2)}, u32[]{:S(2)}) collective-permute-start(bf16[256,1024]{1,0:T(8,128)(2,1)} %bitcast.19), channel_id=1, source_target_pairs={{0,1},{1,0},{2,3},{3,2},{4,5},{5,4},{6,7},{7,6},{8,9},{9,8},{10,11... | collective-permute-start | bytes 1572872 | tf_op jit(solution)/shard_map/ppermute | solution.py:172
  1.1 10.6 %collective-permute-start.5 = (bf16[256,1024]{1,0:T(8,128)(2,1)}, bf16[256,1024]{1,0:T(8,128)(2,1)S(1)}, u32[]{:S(2)}, u32[]{:S(2)}) collective-permute-start(bf16[256,1024]{1,0:T(8,128)(2,1)} %bitcast.21), channel_id=1, source_target_pairs={{0,1},{1,0},{2,3},{3,2},{4,5},{5,4},{6,7},{7,6},{8,9},{9,8},{10,11... | collective-permute-start | bytes 1572872 | tf_op jit(solution)/shard_map/ppermute | solution.py:172
  1.2 2.4 %collective-permute-start = (bf16[16,256]{1,0:T(8,128)(2,1)}, bf16[16,256]{1,0:T(8,128)(2,1)S(1)}, u32[]{:S(2)}, u32[]{:S(2)}) collective-permute-start(bf16[16,256]{1,0:T(8,128)(2,1)} %bitcast.23), channel_id=1, source_target_pairs={{0,1},{1,0},{2,3},{3,2},{4,5},{5,4},{6,7},{7,6},{8,9},{9,8},{10,11... | collective-permute-start | bytes 24584 | tf_op jit(solution)/shard_map/ppermute | solution.py:172
  1.7 2.0 %collective-permute-start.1 = (bf16[16,256]{1,0:T(8,128)(2,1)}, bf16[16,256]{1,0:T(8,128)(2,1)S(1)}, u32[]{:S(2)}, u32[]{:S(2)}) collective-permute-start(bf16[16,256]{1,0:T(8,128)(2,1)} %bitcast.25), channel_id=1, source_target_pairs={{0,1},{1,0},{2,3},{3,2},{4,5},{5,4},{6,7},{7,6},{8,9},{9,8},{10,11... | collective-permute-start | bytes 24584 | tf_op jit(solution)/shard_map/ppermute | solution.py:172
  3.7 0.6 %copy-start.8 = (bf16[16,256]{1,0:T(8,128)(2,1)}, bf16[16,256]{1,0:T(8,128)(2,1)S(1)}, u32[]{:S(2)}) copy-start(bf16[16,256]{1,0:T(8,128)(2,1)S(1)} %collective-permute-done.u_got_ref) | copy-start | bytes 24580
  4.3 0.6 %copy-start.9 = (bf16[16,256]{1,0:T(8,128)(2,1)}, bf16[16,256]{1,0:T(8,128)(2,1)S(1)}, u32[]{:S(2)}) copy-start(bf16[16,256]{1,0:T(8,128)(2,1)S(1)} %collective-permute-done.1.v_got_ref) | copy-start | bytes 24580
  6.4 14.7 %collective-permute-start.2 = (bf16[16,512]{1,0:T(8,128)(2,1)}, bf16[16,512]{1,0:T(8,128)(2,1)S(1)}, u32[]{:S(2)}, u32[]{:S(2)}) collective-permute-start(bf16[16,512]{1,0:T(8,128)(2,1)} %order_factor.1), channel_id=1, source_target_pairs={{0,4},{1,29},{2,6},{3,31},{4,8},{5,1},{6,10},{7,3},{8,12},{9,5},{1... | collective-permute-start | bytes 49160 | tf_op jit(solution)/shard_map/ppermute | solution.py:180
  9.3 11.9 %collective-permute-start.3 = (bf16[16,512]{1,0:T(8,128)(2,1)}, bf16[16,512]{1,0:T(8,128)(2,1)S(1)}, u32[]{:S(2)}, u32[]{:S(2)}) collective-permute-start(bf16[16,512]{1,0:T(8,128)(2,1)} %order_factor.1), channel_id=1, source_target_pairs={{0,6},{1,31},{2,4},{3,29},{4,10},{5,3},{6,8},{7,1},{8,14},{9,7},{1... | collective-permute-start | bytes 49160 | tf_op jit(solution)/shard_map/ppermute | solution.py:180
  11.8 1.6 %copy-start = (bf16[1,1024,1024]{2,1,0:T(8,128)(2,1)S(1)}, bf16[1,1024,1024]{2,1,0:T(8,128)(2,1)}, u32[]{:S(2)}) copy-start(bf16[1,1024,1024]{2,1,0:T(8,128)(2,1)} %param.11) | copy-start | bytes 6291460
  13.4 1.6 %copy-start.1 = (bf16[1,1024,1024]{2,1,0:T(8,128)(2,1)S(1)}, bf16[1,1024,1024]{2,1,0:T(8,128)(2,1)}, u32[]{:S(2)}) copy-start(bf16[1,1024,1024]{2,1,0:T(8,128)(2,1)} %param.13) | copy-start | bytes 6291460
  15.0 1.0 %copy-start.2 = (bf16[1,256,1024]{2,1,0:T(8,128)(2,1)S(1)}, bf16[1,256,1024]{2,1,0:T(8,128)(2,1)}, u32[]{:S(2)}) copy-start(bf16[1,256,1024]{2,1,0:T(8,128)(2,1)} %param.10) | copy-start | bytes 1572868
  16.0 1.0 %copy-start.3 = (bf16[1,256,1024]{2,1,0:T(8,128)(2,1)S(1)}, bf16[1,256,1024]{2,1,0:T(8,128)(2,1)}, u32[]{:S(2)}) copy-start(bf16[1,256,1024]{2,1,0:T(8,128)(2,1)} %param.12) | copy-start | bytes 1572868
  21.4 4.6 %collective-permute-start.6 = (bf16[16,512]{1,0:T(8,128)(2,1)S(1)}, bf16[16,512]{1,0:T(8,128)(2,1)S(1)}, u32[]{:S(2)}, u32[]{:S(2)}) collective-permute-start(bf16[16,512]{1,0:T(8,128)(2,1)S(1)} %apply_factor.1), channel_id=1, source_target_pairs={{0,28},{1,5},{2,30},{3,7},{4,0},{5,9},{6,2},{7,11},{8,4},{9,13},{1... | collective-permute-start | bytes 49160 | tf_op jit(solution)/shard_map/ppermute | solution.py:180
  24.6 4.6 %collective-permute-start.7 = (bf16[16,512]{1,0:T(8,128)(2,1)S(1)}, bf16[16,512]{1,0:T(8,128)(2,1)S(1)}, u32[]{:S(2)}, u32[]{:S(2)}) collective-permute-start(bf16[16,512]{1,0:T(8,128)(2,1)S(1)} %apply_factor.1), channel_id=1, source_target_pairs={{0,30},{1,7},{2,28},{3,5},{4,2},{5,11},{6,0},{7,9},{8,6},{9,15},{1... | collective-permute-start | bytes 49160 | tf_op jit(solution)/shard_map/ppermute | solution.py:180
  26.1 5.2 %copy-start.4 = (bf16[16,512]{1,0:T(8,128)(2,1)}, bf16[16,512]{1,0:T(8,128)(2,1)S(1)}, u32[]{:S(2)}) copy-start(bf16[16,512]{1,0:T(8,128)(2,1)S(1)} %collective-permute-done.6.refs_0_) | copy-start | bytes 49156
  26.1 5.0 %collective-permute-start.8 = (bf16[16,512]{1,0:T(8,128)(2,1)S(1)}, bf16[16,512]{1,0:T(8,128)(2,1)S(1)}, u32[]{:S(2)}, u32[]{:S(2)}) collective-permute-start(bf16[16,512]{1,0:T(8,128)(2,1)S(1)} %collective-permute-done.6.refs_0_), channel_id=1, source_target_pairs={{0,1},{1,0},{2,3},{3,2},{4,5},{5,4},{6,7},{7,6},{8,9},{9,8},{10,11... | collective-permute-start | bytes 49160 | tf_op jit(solution)/shard_map/ppermute | solution.py:172
  29.3 2.0 %copy-start.5 = (bf16[16,512]{1,0:T(8,128)(2,1)}, bf16[16,512]{1,0:T(8,128)(2,1)S(1)}, u32[]{:S(2)}) copy-start(bf16[16,512]{1,0:T(8,128)(2,1)S(1)} %collective-permute-done.7.refs_1_) | copy-start | bytes 49156
  29.3 2.0 %collective-permute-start.9 = (bf16[16,512]{1,0:T(8,128)(2,1)S(1)}, bf16[16,512]{1,0:T(8,128)(2,1)S(1)}, u32[]{:S(2)}, u32[]{:S(2)}) collective-permute-start(bf16[16,512]{1,0:T(8,128)(2,1)S(1)} %collective-permute-done.7.refs_1_), channel_id=1, source_target_pairs={{0,1},{1,0},{2,3},{3,2},{4,5},{5,4},{6,7},{7,6},{8,9},{9,8},{10,11... | collective-permute-start | bytes 49160 | tf_op jit(solution)/shard_map/ppermute | solution.py:172
  31.1 0.6 %copy-start.6 = (bf16[16,512]{1,0:T(8,128)(2,1)}, bf16[16,512]{1,0:T(8,128)(2,1)S(1)}, u32[]{:S(2)}) copy-start(bf16[16,512]{1,0:T(8,128)(2,1)S(1)} %collective-permute-done.8.refs_2_) | copy-start | bytes 49156
  31.7 0.6 %copy-start.7 = (bf16[16,512]{1,0:T(8,128)(2,1)}, bf16[16,512]{1,0:T(8,128)(2,1)S(1)}, u32[]{:S(2)}) copy-start(bf16[16,512]{1,0:T(8,128)(2,1)S(1)} %collective-permute-done.9.refs_3_) | copy-start | bytes 49156

commit v2 on v1

v2 whole, which is shorter than its diff:
```python
import functools

import jax
import jax.numpy as jnp
from jax import lax
from jax.experimental import pallas as pl
from jax.experimental.pallas import tpu as pltpu
from jax.sharding import PartitionSpec as P

LANES = 128
F32, BF16 = jnp.float32, jnp.bfloat16
MIB = 1024 * 1024
JOIN_FLOPS = 10**10


def iota(shape, dim):
    return lax.broadcasted_iota(jnp.int32, shape, dim)


def is_upper():
    return lax.axis_index("row") % 2 == 1


def join_kernel(own_ref, u_got_ref, v_got_ref, out_ref, *, states_here):
    keep_cols, rows = u_got_ref.shape
    upper = is_upper()
    own = own_ref[:keep_cols, :rows]
    got = jnp.where(upper, u_got_ref[...], v_got_ref[...])
    both = jnp.concatenate([jnp.where(upper, got, own), jnp.where(upper, own, got)], axis=1)
    lane = iota((1, LANES), 1)
    order = own_ref[keep_cols : keep_cols + 1, :LANES].astype(F32)
    order = jnp.where(lane < states_here, order, 0.0)
    distance = states_here
    while distance < LANES:
        order += pltpu.roll(order, distance, 1)
        distance *= 2
    wanted = order.astype(jnp.int32) + lane // states_here * states_here
    mover = jnp.where(iota((LANES, LANES), 0) == wanted, 1.0, 0.0).astype(BF16)
    for start in range(0, 2 * rows, LANES):
        moved = lax.dot_general(
            both[:, start : start + LANES], mover, (((1,), (1,)), ((), ())), preferred_element_type=F32
        )
        out_ref[:, start : start + LANES] = moved.astype(BF16)


def half_kernel(ul, ul_got, ur, dl, dl_got, dr, out_ref, *, states_here):
    rows, width = ul.shape
    step = 2 * LANES
    group = LANES // states_here
    lane = iota((1, LANES), 1)
    odd = {distance: (lane // states_here // distance) % 2 == 1 for distance in range(1, group)}

    def regroup(block):
        chunks = [block[i * states_here : (i + 1) * states_here] for i in range(group)]
        distance = 1
        while distance < group:
            shift = distance * states_here
            moved = list(chunks)
            for i in range(group):
                if i & distance == 0:
                    low, high = chunks[i], chunks[i + distance]
                    moved[i] = jnp.where(odd[distance], pltpu.roll(high, shift, 1), low)
                    moved[i + distance] = jnp.where(odd[distance], high, pltpu.roll(low, LANES - shift, 1))
            chunks = moved
            distance *= 2
        return chunks

    def work(first, second, matrix):
        if rows % LANES:
            lefts = [(0, jnp.concatenate([first[...], second[...]], axis=0))]
        else:
            lefts = [(0, first[...]), (rows, second[...])]
        for column in range(0, width, step):
            for base, left in lefts:
                full = jnp.dot(left, matrix[:, column : column + step], preferred_element_type=F32)
                for p in range(0, left.shape[0], LANES):
                    for q in range(0, step, LANES):
                        for i, chunk in enumerate(regroup(full[p : p + LANES, q : q + LANES])):
                            at = column + q + i * states_here
                            out_ref[at : at + states_here, base + p : base + p + LANES] = chunk.astype(BF16)

    upper = is_upper()

    @pl.when(upper)
    def _():
        work(ul_got, ul, ur)

    @pl.when(jnp.logical_not(upper))
    def _():
        work(dl, dl_got, dr)


def apply_kernel(states_ref, *refs, states_here):
    *factors, half_ref, out_ref = refs
    chips = len(factors)
    chip = lax.axis_index("row") // 2
    depth = factors[0].shape[1]
    live = iota((1, depth), 1) % states_here < states_ref[...]
    total = jnp.zeros(out_ref.shape, F32)
    for away in range(chips):
        source = lax.rem(chip - away + chips, chips)
        part = half_ref[pl.ds(pl.multiple_of(source * depth, depth), depth), :]
        factor = jnp.where(live, factors[away][...], jnp.zeros((), BF16))
        total += jnp.dot(factor, part, preferred_element_type=F32)
    out_ref[...] = jnp.where(live, total, 0.0).astype(BF16)


def finish_kernel(weight_ref, *refs, width):
    *parts, tilde_ref, proj_ref, inter_ref = refs
    chips = len(parts) // 2
    mine, got = parts[:chips], parts[chips:]
    keep_cols, rows = tilde_ref.shape
    core = lax.axis_index("row") % 2
    chip = lax.axis_index("row") // 2
    upper = is_upper()
    weight = weight_ref[...]
    square = (keep_cols, keep_cols)
    diagonal = iota(square, 0) == iota(square, 1)
    weight_rows = jnp.sum(jnp.where(diagonal, weight, 0.0), axis=1, keepdims=True)
    products = []
    for away in range(chips):
        a = jnp.where(upper, mine[away][...], got[away][...])
        b = jnp.where(upper, got[away][...], mine[away][...])
        if away == 0:
            for whole, ref in ((a, tilde_ref), (b, proj_ref)):
                own = jnp.where(core == 0, whole[:, :rows], whole[:, rows:])
                ref[...] = (own.astype(F32) * weight_rows).astype(BF16)
        products.append(lax.dot_general(a, b, (((1,), (1,)), ((), ())), preferred_element_type=F32))
    total = jnp.zeros(square, F32)
    for source in range(chips):
        for away in range(chips):
            here = lax.rem(chip - away + chips, chips) == source
            total += jnp.where(here, products[away], 0.0)
    inter_ref[...] = total * weight_rows * weight / jnp.sqrt(jnp.float32(width))


def in_vmem():
    return pl.BlockSpec(memory_space=pltpu.VMEM)


def local(
    sectors,
    row_devices,
    corner_ul,
    corner_ur,
    corner_dl,
    corner_dr,
    left_factor,
    right_factor,
    singular,
    states,
    kept,
    joining_map,
):
    rows, width = corner_ul.shape[1:]
    states_here = joining_map.shape[1]
    keep_cols = left_factor.shape[2]
    chips = row_devices // 2

    def other_core(value):
        return lax.ppermute(value, "row", [(i, i ^ 1) for i in range(row_devices)])

    def to_sector(value, upper_step, away):
        pairs = []
        for s in range(sectors):
            for r in range(row_devices):
                t = (s + (upper_step if r % 2 else -upper_step)) % sectors
                pairs.append((s * row_devices + r, t * row_devices + (r + 2 * away) % row_devices))
        return lax.ppermute(value, ("sec", "row"), pairs)

    block = jax.ShapeDtypeStruct((keep_cols, rows), BF16)
    whole = jax.ShapeDtypeStruct((keep_cols, 2 * rows), BF16)
    u, v = left_factor[0].T, right_factor[0].T
    u_got, v_got = other_core(u), other_core(v)
    own = jnp.where(is_upper(), u, v)
    own_width = max(rows, LANES)
    own = jnp.concatenate(
        [
            jnp.pad(own, ((0, 0), (0, own_width - rows))),
            jnp.pad(joining_map.astype(BF16), ((0, keep_cols - 1), (0, own_width - states_here))),
        ],
        axis=0,
    )
    joined = pl.pallas_call(
        functools.partial(join_kernel, states_here=states_here),
        out_shape=whole,
        in_specs=[in_vmem()] * 3,
        out_specs=in_vmem(),
        compiler_params=pltpu.CompilerParams(vmem_limit_bytes=MIB),
        cost_estimate=pl.CostEstimate(flops=JOIN_FLOPS, bytes_accessed=0, transcendentals=0),
        name="join_factor",
    )(own, u_got, v_got)
    factors = [to_sector(joined, -1, away) for away in range(chips)]

    ul, dl = corner_ul[0], corner_dl[0]
    ul_got, dl_got = other_core(ul), other_core(dl)
    half = pl.pallas_call(
        functools.partial(half_kernel, states_here=states_here),
        out_shape=jax.ShapeDtypeStruct((width, 2 * rows), BF16),
        in_specs=[in_vmem()] * 6,
        out_specs=in_vmem(),
        compiler_params=pltpu.CompilerParams(vmem_limit_bytes=16 * MIB),
        cost_estimate=pl.CostEstimate(
            flops=4 * rows * width * width, bytes_accessed=2 * width * (width + 4 * rows), transcendentals=0
        ),
        name="half_product",
    )(ul, ul_got, corner_ur[0], dl, dl_got, corner_dr[0])

    applied = pl.pallas_call(
        functools.partial(apply_kernel, states_here=states_here),
        out_shape=whole,
        in_specs=[in_vmem()] * (chips + 2),
        out_specs=in_vmem(),
        compiler_params=pltpu.CompilerParams(vmem_limit_bytes=4 * MIB),
        name="apply_factor",
    )(states[None], *factors, half)
    mine = [to_sector(applied, 1, away) for away in range(chips)]
    theirs = [other_core(value) for value in mine]

    columns = jnp.arange(keep_cols, dtype=jnp.int32)
    weight = jnp.where(columns < kept[0], 1.0 / jnp.sqrt(singular), 0.0)
    tilde, proj, inter = pl.pallas_call(
        functools.partial(finish_kernel, width=width),
        out_shape=(block, block, jax.ShapeDtypeStruct((keep_cols, keep_cols), F32)),
        in_specs=[in_vmem()] * (2 * chips + 1),
        out_specs=(in_vmem(), in_vmem(), in_vmem()),
        compiler_params=pltpu.CompilerParams(vmem_limit_bytes=MIB),
        name="finish",
    )(weight, *mine, *theirs)
    return tilde.T[None], proj.T[None], inter[None]


def solution(mesh):
    placed = (
        P("sec", "row", None),
        P("sec", None, None),
        P("sec", "row", None),
        P("sec", None, None),
        P("sec", "row", None),
        P("sec", "row", None),
        P("sec", None),
        P("sec"),
        P("sec"),
        P("sec", None),
    )
    return jax.shard_map(
        functools.partial(local, mesh.shape["sec"], mesh.shape["row"]),
        mesh=mesh,
        in_specs=placed,
        out_specs=(P("sec", "row", None), P("sec", "row", None), P("sec", None, None)),
        check_vma=False,
    )
```

time: 34.2 us -> 22.7 us (0.66)
  local copies, waits for them, and re-layouts: 7.47 us -> 0.03 us
  Pallas kernels: 7.44 us -> 2.91 us
  starting transfers between devices: 13.5 us -> 10.9 us
  waiting for transfers between devices: 3.47 us -> 5.09 us
  other arithmetic: 0 us -> 1.39 us
    unnamed x20 -> x10, local copies, waits for them, and re-layouts: 7.47 us -> 0.03 us
    pallas_call x3, Pallas kernels: 5.9 us -> 2.17 us  [the longest x1 1.52 us: local(): pl.pallas_call(functools.partial(half_kernel, states_here=states_here), o...]
    ppermute x6, starting transfers between devices: 4.57 us -> 1.23 us  [other_core(): return lax.ppermute(value, 'row', [(i, i ^ 1) for i in range(row_devices)])]
    ppermute x4, waiting for transfers between devices: 2.02 us -> 3.96 us  [to_sector(): return lax.ppermute(value, ('sec', 'row'), pairs)]
    pallas_call x1, Pallas kernels: 1.53 us -> 0.74 us  [local(): pl.pallas_call(functools.partial(finish_kernel, width=width), out_shape=(...]
    ppermute x4, starting transfers between devices: 8.9 us -> 9.68 us  [to_sector(): return lax.ppermute(value, ('sec', 'row'), pairs)]
    select_n x0 -> x2, other arithmetic: none -> 0.72 us  [the longest x1 0.72 us: local(): own = jnp.where(is_upper(), u, v)]
    convert_element_type x0 -> x1, other arithmetic: none -> 0.66 us  [local(): joining_map.astype(BF16)]
  transfers between devices with their start and end apart: 10 -> 10, of which waited for: 4 -> 5; matrix products, arithmetic and copies ran while one was open for 0% -> 6% of each run, Pallas kernels for 17% -> 8%
where the time goes in v2:
time: 22.7 us; the launch traced here: 22.4 us
  starting transfers between devices  10.9 us (48%)
  waiting for transfers between devices  5.09 us (22%)
  Pallas kernels  2.91 us (13%)
  between operations  2.05 us (9%)
  other arithmetic  1.39 us (6%)
    ppermute x4, starting transfers between devices, to_sector(): return lax.ppermute(value, ('sec', 'row'), pairs)  9.68 us
    ppermute x4, waiting for transfers between devices, to_sector(): return lax.ppermute(value, ('sec', 'row'), pairs)  3.96 us
    pallas_call x1, Pallas kernels, local(): pl.pallas_call(functools.partial(half_kernel, states_here=states_here), o...  1.52 us
    ppermute x6, starting transfers between devices, other_core(): return lax.ppermute(value, 'row', [(i, i ^ 1) for i in range(row_devices)])  1.23 us
    ppermute x6, waiting for transfers between devices, other_core(): return lax.ppermute(value, 'row', [(i, i ^ 1) for i in range(row_devices)])  1.13 us
    pallas_call x1, Pallas kernels, local(): pl.pallas_call(functools.partial(finish_kernel, width=width), out_shape=(...  0.74 us
    select_n x1, other arithmetic, local(): own = jnp.where(is_upper(), u, v)  0.72 us
    convert_element_type x1, other arithmetic, local(): joining_map.astype(BF16)  0.66 us
  transfers between devices with their start and end apart: 10, of which 5 were waited for; matrix products, arithmetic and copies ran while one was open for 6% of the time, Pallas kernels for 8%

profile of v2, /device:TPU:0, one launch (start us, length us, event | category | flops | bytes accessed | tf_op | source)
XLA Modules:
  0.0 22.4 jit_solution(4589614832113434294)
XLA Ops:
  0.6 0.5 %collective-permute-start = (bf16[16,256]{1,0:T(8,128)(2,1)}, bf16[16,256]{1,0:T(8,128)(2,1)S(1)}, u32[]{:S(2)}, u32[]{:S(2)}) collective-permute-start(bf16[16,256]{1,0:T(8,128)(2,1)} %bitcast.29), channel_id=1, source_target_pairs={{0,1},{1,0},{2,3},{3,2},{4,5},{5,4},{6,7},{7,6},{8,9},{9,8},{10,11... | collective-permute-start | bytes 24584 | tf_op jit(solution)/shard_map/ppermute | solution.py:161
  1.1 0.1 collective-permute-start.1
  1.2 0.4 %collective-permute-start.4 = (bf16[256,1024]{1,0:T(8,128)(2,1)}, bf16[256,1024]{1,0:T(8,128)(2,1)S(1)}, u32[]{:S(2)}, u32[]{:S(2)}) collective-permute-start(bf16[256,1024]{1,0:T(8,128)(2,1)} %bitcast.25), channel_id=1, source_target_pairs={{0,1},{1,0},{2,3},{3,2},{4,5},{5,4},{6,7},{7,6},{8,9},{9,8},{10,11... | collective-permute-start | bytes 1572872 | tf_op jit(solution)/shard_map/ppermute | solution.py:161
  1.7 0.1 collective-permute-start.5
  1.7 0.7 %broadcast_select_fusion = bf16[16,256]{1,0:T(8,128)(2,1)S(1)} fusion(pred[]{:T(512)S(6)} %eq.5, bf16[1,256,16]{1,2,0:T(8,128)(2,1)} %param.15, bf16[1,256,16]{1,2,0:T(8,128)(2,1)} %param.14), kind=kLoop, calls=%fused_computation.3 | loop fusion | flops 4096 | bytes 24577 | tf_op jit(solution)/shard_map/jit(_where)/select_n | solution.py:175
  2.5 0.7 %convert_element_type.5 = bf16[1,16]{1,0:T(2,128)(2,1)S(1)} convert(s32[1,16]{1,0:T(1,128)} %param.19) | non-fusion elementwise | flops 16 | bytes 96 | tf_op jit(solution)/shard_map/convert_element_type | solution.py:180
  3.8 0.0 copy-start
  3.8 0.0 copy-start.1
  3.8 0.0 copy-start.2
  3.8 0.0 copy-start.3
  3.8 0.0 collective-permute-done.u_got_ref
  3.8 0.0 collective-permute-done.1.v_got_ref
  3.8 0.4 %join_factor.1 = bf16[16,512]{1,0:T(8,128)(2,1)S(1)} custom-call(bf16[32,256]{1,0:T(8,128)(2,1)S(1)} %fusion.1.own_ref, bf16[16,256]{1,0:T(8,128)(2,1)S(1)} %collective-permute-done.u_got_ref, bf16[16,256]{1,0:T(8,128)(2,1)S(1)} %collective-permute-done.1.v_got_ref), custom_call_target="tpu_custom_call" | custom-call | flops 10000000000 | tf_op jit(solution)/shard_map/join_factor/pallas_call | solution.py:184
  4.2 3.0 %collective-permute-start.2 = (bf16[16,512]{1,0:T(8,128)(2,1)S(1)}, bf16[16,512]{1,0:T(8,128)(2,1)S(1)}, u32[]{:S(2)}, u32[]{:S(2)}) collective-permute-start(bf16[16,512]{1,0:T(8,128)(2,1)S(1)} %join_factor.1), channel_id=1, source_target_pairs={{0,4},{1,29},{2,6},{3,31},{4,8},{5,1},{6,10},{7,3},{8,12},{9,5},{1... | collective-permute-start | bytes 49160 | tf_op jit(solution)/shard_map/ppermute | solution.py:169
  7.2 2.5 %collective-permute-start.3 = (bf16[16,512]{1,0:T(8,128)(2,1)S(1)}, bf16[16,512]{1,0:T(8,128)(2,1)S(1)}, u32[]{:S(2)}, u32[]{:S(2)}) collective-permute-start(bf16[16,512]{1,0:T(8,128)(2,1)S(1)} %join_factor.1), channel_id=1, source_target_pairs={{0,6},{1,31},{2,4},{3,29},{4,10},{5,3},{6,8},{7,1},{8,14},{9,7},{1... | collective-permute-start | bytes 49160 | tf_op jit(solution)/shard_map/ppermute | solution.py:169
  9.7 0.0 collective-permute-done.4.ul_got
  9.7 0.0 collective-permute-done.5.dl_got
  9.7 0.0 copy-done
  9.7 0.0 copy-done.1
  9.7 0.0 copy-done.2
  9.7 0.0 copy-done.3
  9.7 0.0 copy-start.4
  9.7 1.5 %half_product.1.refs_2_ = bf16[1024,512]{1,0:T(8,128)(2,1)S(1)} custom-call(bf16[256,1024]{1,0:T(8,128)(2,1)S(1)} %bitcast.26, bf16[256,1024]{1,0:T(8,128)(2,1)S(1)} %collective-permute-done.4.ul_got, bf16[1024,1024]{1,0:T(8,128)(2,1)S(1)} %bitcast.23, bf16[256,1024]{1,0:T(8,128)(2,1)S(1)} %bitcast.28, bf16[256,1024]{1,0:T(8,128)(2,1)S(1)} %collective-permute-done.5.dl_got, ...), custom_call_target="tpu_custom_call" | custom-call | flops 1073741824 | bytes 4194304 | tf_op jit(solution)/shard_map/half_product/pallas_call | solution.py:197
  11.2 0.7 %collective-permute-done.2.refs_0_ = bf16[16,512]{1,0:T(8,128)(2,1)S(1)} collective-permute-done((bf16[16,512]{1,0:T(8,128)(2,1)S(1)}, bf16[16,512]{1,0:T(8,128)(2,1)S(1)}, u32[]{:S(2)}, u32[]{:S(2)}) %collective-permute-start.2) | collective-permute-done | bytes 16416 | tf_op jit(solution)/shard_map/ppermute | solution.py:169
  11.9 2.6 %collective-permute-done.3.refs_1_ = bf16[16,512]{1,0:T(8,128)(2,1)S(1)} collective-permute-done((bf16[16,512]{1,0:T(8,128)(2,1)S(1)}, bf16[16,512]{1,0:T(8,128)(2,1)S(1)}, u32[]{:S(2)}, u32[]{:S(2)}) %collective-permute-start.3) | collective-permute-done | bytes 16416 | tf_op jit(solution)/shard_map/ppermute | solution.py:169
  14.5 0.3 %apply_factor.1 = bf16[16,512]{1,0:T(8,128)(2,1)S(1)} custom-call(s32[1,1]{1,0:T(1,128)} %bitcast.21.states_ref, bf16[16,512]{1,0:T(8,128)(2,1)S(1)} %collective-permute-done.2.refs_0_, bf16[16,512]{1,0:T(8,128)(2,1)S(1)} %collective-permute-done.3.refs_1_, bf16[1024,512]{1,0:T(8,128)(2,1)S(1)} %half_product.1.refs_2_), custom_call_target="tpu_custom_call" | custom-call | tf_op jit(solution)/shard_map/apply_factor/pallas_call | solution.py:209
  14.8 0.6 %collective-permute-start.6 = (bf16[16,512]{1,0:T(8,128)(2,1)S(1)}, bf16[16,512]{1,0:T(8,128)(2,1)S(1)}, u32[]{:S(2)}, u32[]{:S(2)}) collective-permute-start(bf16[16,512]{1,0:T(8,128)(2,1)S(1)} %apply_factor.1), channel_id=1, source_target_pairs={{0,28},{1,5},{2,30},{3,7},{4,0},{5,9},{6,2},{7,11},{8,4},{9,13},{1... | collective-permute-start | bytes 49160 | tf_op jit(solution)/shard_map/ppermute | solution.py:169
  15.4 3.6 %collective-permute-start.7 = (bf16[16,512]{1,0:T(8,128)(2,1)S(1)}, bf16[16,512]{1,0:T(8,128)(2,1)S(1)}, u32[]{:S(2)}, u32[]{:S(2)}) collective-permute-start(bf16[16,512]{1,0:T(8,128)(2,1)S(1)} %apply_factor.1), channel_id=1, source_target_pairs={{0,30},{1,7},{2,28},{3,5},{4,2},{5,11},{6,0},{7,9},{8,6},{9,15},{1... | collective-permute-start | bytes 49160 | tf_op jit(solution)/shard_map/ppermute | solution.py:169
  19.7 0.0 collective-permute-done.6.refs_0_
  19.7 0.1 collective-permute-start.8
  19.8 0.7 %collective-permute-done.7.refs_1_ = bf16[16,512]{1,0:T(8,128)(2,1)S(1)} collective-permute-done((bf16[16,512]{1,0:T(8,128)(2,1)S(1)}, bf16[16,512]{1,0:T(8,128)(2,1)S(1)}, u32[]{:S(2)}, u32[]{:S(2)}) %collective-permute-start.7) | collective-permute-done | bytes 16416 | tf_op jit(solution)/shard_map/ppermute | solution.py:169
  20.5 0.1 collective-permute-start.9
  20.5 0.0 copy-done.4
  20.5 0.4 %collective-permute-done.8.refs_2_ = bf16[16,512]{1,0:T(8,128)(2,1)S(1)} collective-permute-done((bf16[16,512]{1,0:T(8,128)(2,1)S(1)}, bf16[16,512]{1,0:T(8,128)(2,1)S(1)}, u32[]{:S(2)}, u32[]{:S(2)}) %collective-permute-start.8) | collective-permute-done | bytes 16416 | tf_op jit(solution)/shard_map/ppermute | solution.py:161
  20.9 0.7 %collective-permute-done.9.refs_3_ = bf16[16,512]{1,0:T(8,128)(2,1)S(1)} collective-permute-done((bf16[16,512]{1,0:T(8,128)(2,1)S(1)}, bf16[16,512]{1,0:T(8,128)(2,1)S(1)}, u32[]{:S(2)}, u32[]{:S(2)}) %collective-permute-start.9) | collective-permute-done | bytes 16416 | tf_op jit(solution)/shard_map/ppermute | solution.py:161
  21.6 0.7 %finish.1 = (bf16[16,256]{1,0:T(8,128)(2,1)}, bf16[16,256]{1,0:T(8,128)(2,1)}, f32[16,16]{1,0:T(8,128)}) custom-call(f32[1,16]{1,0:T(1,128)S(1)} %compare_select_fusion.weight_ref, bf16[16,512]{1,0:T(8,128)(2,1)S(1)} %collective-permute-done.6.refs_0_, bf16[16,512]{1,0:T(8,128)(2,1)S(1)} %collective-permute-done.7.refs_1_, ...), custom_call_target="tpu_custom_call" | custom-call | tf_op jit(solution)/shard_map/finish/pallas_call | solution.py:222
  (2 shorter events, 0.0 us)
Async XLA Ops:
  0.6 3.2 %collective-permute-start = (bf16[16,256]{1,0:T(8,128)(2,1)}, bf16[16,256]{1,0:T(8,128)(2,1)S(1)}, u32[]{:S(2)}, u32[]{:S(2)}) collective-permute-start(bf16[16,256]{1,0:T(8,128)(2,1)} %bitcast.29), channel_id=1, source_target_pairs={{0,1},{1,0},{2,3},{3,2},{4,5},{5,4},{6,7},{7,6},{8,9},{9,8},{10,11... | collective-permute-start | bytes 24584 | tf_op jit(solution)/shard_map/ppermute | solution.py:161
  1.1 2.7 %collective-permute-start.1 = (bf16[16,256]{1,0:T(8,128)(2,1)}, bf16[16,256]{1,0:T(8,128)(2,1)S(1)}, u32[]{:S(2)}, u32[]{:S(2)}) collective-permute-start(bf16[16,256]{1,0:T(8,128)(2,1)} %bitcast.30), channel_id=1, source_target_pairs={{0,1},{1,0},{2,3},{3,2},{4,5},{5,4},{6,7},{7,6},{8,9},{9,8},{10,11... | collective-permute-start | bytes 24584 | tf_op jit(solution)/shard_map/ppermute | solution.py:161
  1.2 8.4 %collective-permute-start.4 = (bf16[256,1024]{1,0:T(8,128)(2,1)}, bf16[256,1024]{1,0:T(8,128)(2,1)S(1)}, u32[]{:S(2)}, u32[]{:S(2)}) collective-permute-start(bf16[256,1024]{1,0:T(8,128)(2,1)} %bitcast.25), channel_id=1, source_target_pairs={{0,1},{1,0},{2,3},{3,2},{4,5},{5,4},{6,7},{7,6},{8,9},{9,8},{10,11... | collective-permute-start | bytes 1572872 | tf_op jit(solution)/shard_map/ppermute | solution.py:161
  1.7 8.0 %collective-permute-start.5 = (bf16[256,1024]{1,0:T(8,128)(2,1)}, bf16[256,1024]{1,0:T(8,128)(2,1)S(1)}, u32[]{:S(2)}, u32[]{:S(2)}) collective-permute-start(bf16[256,1024]{1,0:T(8,128)(2,1)} %bitcast.27), channel_id=1, source_target_pairs={{0,1},{1,0},{2,3},{3,2},{4,5},{5,4},{6,7},{7,6},{8,9},{9,8},{10,11... | collective-permute-start | bytes 1572872 | tf_op jit(solution)/shard_map/ppermute | solution.py:161
  3.8 5.9 %copy-start = (bf16[1,1024,1024]{2,1,0:T(8,128)(2,1)S(1)}, bf16[1,1024,1024]{2,1,0:T(8,128)(2,1)}, u32[]{:S(2)}) copy-start(bf16[1,1024,1024]{2,1,0:T(8,128)(2,1)} %param.11) | copy-start | bytes 6291460
  3.8 5.9 %copy-start.1 = (bf16[1,1024,1024]{2,1,0:T(8,128)(2,1)S(1)}, bf16[1,1024,1024]{2,1,0:T(8,128)(2,1)}, u32[]{:S(2)}) copy-start(bf16[1,1024,1024]{2,1,0:T(8,128)(2,1)} %param.13) | copy-start | bytes 6291460
  3.8 5.9 %copy-start.2 = (bf16[1,256,1024]{2,1,0:T(8,128)(2,1)S(1)}, bf16[1,256,1024]{2,1,0:T(8,128)(2,1)}, u32[]{:S(2)}) copy-start(bf16[1,256,1024]{2,1,0:T(8,128)(2,1)} %param.10) | copy-start | bytes 1572868
  3.8 5.9 %copy-start.3 = (bf16[1,256,1024]{2,1,0:T(8,128)(2,1)S(1)}, bf16[1,256,1024]{2,1,0:T(8,128)(2,1)}, u32[]{:S(2)}) copy-start(bf16[1,256,1024]{2,1,0:T(8,128)(2,1)} %param.12) | copy-start | bytes 1572868
  4.2 7.7 %collective-permute-start.2 = (bf16[16,512]{1,0:T(8,128)(2,1)S(1)}, bf16[16,512]{1,0:T(8,128)(2,1)S(1)}, u32[]{:S(2)}, u32[]{:S(2)}) collective-permute-start(bf16[16,512]{1,0:T(8,128)(2,1)S(1)} %join_factor.1), channel_id=1, source_target_pairs={{0,4},{1,29},{2,6},{3,31},{4,8},{5,1},{6,10},{7,3},{8,12},{9,5},{1... | collective-permute-start | bytes 49160 | tf_op jit(solution)/shard_map/ppermute | solution.py:169
  7.2 7.3 %collective-permute-start.3 = (bf16[16,512]{1,0:T(8,128)(2,1)S(1)}, bf16[16,512]{1,0:T(8,128)(2,1)S(1)}, u32[]{:S(2)}, u32[]{:S(2)}) collective-permute-start(bf16[16,512]{1,0:T(8,128)(2,1)S(1)} %join_factor.1), channel_id=1, source_target_pairs={{0,6},{1,31},{2,4},{3,29},{4,10},{5,3},{6,8},{7,1},{8,14},{9,7},{1... | collective-permute-start | bytes 49160 | tf_op jit(solution)/shard_map/ppermute | solution.py:169
  9.7 10.8 %copy-start.4 = (f32[1,16]{1,0:T(1,128)S(1)}, f32[1,16]{1,0:T(1,128)}, u32[]{:S(2)}) copy-start(f32[1,16]{1,0:T(1,128)} %param.16) | copy-start | bytes 196
  14.8 4.9 %collective-permute-start.6 = (bf16[16,512]{1,0:T(8,128)(2,1)S(1)}, bf16[16,512]{1,0:T(8,128)(2,1)S(1)}, u32[]{:S(2)}, u32[]{:S(2)}) collective-permute-start(bf16[16,512]{1,0:T(8,128)(2,1)S(1)} %apply_factor.1), channel_id=1, source_target_pairs={{0,28},{1,5},{2,30},{3,7},{4,0},{5,9},{6,2},{7,11},{8,4},{9,13},{1... | collective-permute-start | bytes 49160 | tf_op jit(solution)/shard_map/ppermute | solution.py:169
  15.4 5.1 %collective-permute-start.7 = (bf16[16,512]{1,0:T(8,128)(2,1)S(1)}, bf16[16,512]{1,0:T(8,128)(2,1)S(1)}, u32[]{:S(2)}, u32[]{:S(2)}) collective-permute-start(bf16[16,512]{1,0:T(8,128)(2,1)S(1)} %apply_factor.1), channel_id=1, source_target_pairs={{0,30},{1,7},{2,28},{3,5},{4,2},{5,11},{6,0},{7,9},{8,6},{9,15},{1... | collective-permute-start | bytes 49160 | tf_op jit(solution)/shard_map/ppermute | solution.py:169
  19.7 1.2 %collective-permute-start.8 = (bf16[16,512]{1,0:T(8,128)(2,1)S(1)}, bf16[16,512]{1,0:T(8,128)(2,1)S(1)}, u32[]{:S(2)}, u32[]{:S(2)}) collective-permute-start(bf16[16,512]{1,0:T(8,128)(2,1)S(1)} %collective-permute-done.6.refs_0_), channel_id=1, source_target_pairs={{0,1},{1,0},{2,3},{3,2},{4,5},{5,4},{6,7},{7,6},{8,9},{9,8},{10,11... | collective-permute-start | bytes 49160 | tf_op jit(solution)/shard_map/ppermute | solution.py:161
  20.5 1.2 %collective-permute-start.9 = (bf16[16,512]{1,0:T(8,128)(2,1)S(1)}, bf16[16,512]{1,0:T(8,128)(2,1)S(1)}, u32[]{:S(2)}, u32[]{:S(2)}) collective-permute-start(bf16[16,512]{1,0:T(8,128)(2,1)S(1)} %collective-permute-done.7.refs_1_), channel_id=1, source_target_pairs={{0,1},{1,0},{2,3},{3,2},{4,5},{5,4},{6,7},{7,6},{8,9},{9,8},{10,11... | collective-permute-start | bytes 49160 | tf_op jit(solution)/shard_map/ppermute | solution.py:161

commit v3 on v2

--- a/solution.py
+++ b/solution.py
@@ -11,6 +11,8 @@
 F32, BF16 = jnp.float32, jnp.bfloat16
 MIB = 1024 * 1024
 JOIN_FLOPS = 10**10
+FACTOR_FIRST = (1, 1)
+RESULT_FIRST = (1, 1)
 
 
 def iota(shape, dim):
@@ -18,17 +20,17 @@
 
 
 def is_upper():
-    return lax.axis_index("row") % 2 == 1
+    return lax.axis_index("row") & 1 == 1
 
 
 def join_kernel(own_ref, u_got_ref, v_got_ref, out_ref, *, states_here):
     keep_cols, rows = u_got_ref.shape
     upper = is_upper()
-    own = own_ref[:keep_cols, :rows]
+    own = own_ref[:keep_cols, :rows].astype(BF16)
     got = jnp.where(upper, u_got_ref[...], v_got_ref[...])
     both = jnp.concatenate([jnp.where(upper, got, own), jnp.where(upper, own, got)], axis=1)
     lane = iota((1, LANES), 1)
-    order = own_ref[keep_cols : keep_cols + 1, :LANES].astype(F32)
+    order = own_ref[keep_cols : keep_cols + 1, :LANES]
     order = jnp.where(lane < states_here, order, 0.0)
     distance = states_here
     while distance < LANES:
@@ -97,10 +99,11 @@
     depth = factors[0].shape[1]
     live = iota((1, depth), 1) % states_here < states_ref[...]
     total = jnp.zeros(out_ref.shape, F32)
-    for away in range(chips):
-        source = lax.rem(chip - away + chips, chips)
+    first = jnp.where(is_upper(), FACTOR_FIRST[1], FACTOR_FIRST[0])
+    for turn in range(chips):
+        source = lax.rem(chip - turn - first + 2 * chips, chips)
         part = half_ref[pl.ds(pl.multiple_of(source * depth, depth), depth), :]
-        factor = jnp.where(live, factors[away][...], jnp.zeros((), BF16))
+        factor = jnp.where(live, factors[turn][...], jnp.zeros((), BF16))
         total += jnp.dot(factor, part, preferred_element_type=F32)
     out_ref[...] = jnp.where(live, total, 0.0).astype(BF16)
 
@@ -117,15 +120,17 @@
     square = (keep_cols, keep_cols)
     diagonal = iota(square, 0) == iota(square, 1)
     weight_rows = jnp.sum(jnp.where(diagonal, weight, 0.0), axis=1, keepdims=True)
-    products = []
-    for away in range(chips):
-        a = jnp.where(upper, mine[away][...], got[away][...])
-        b = jnp.where(upper, got[away][...], mine[away][...])
-        if away == 0:
-            for whole, ref in ((a, tilde_ref), (b, proj_ref)):
-                own = jnp.where(core == 0, whole[:, :rows], whole[:, rows:])
-                ref[...] = (own.astype(F32) * weight_rows).astype(BF16)
-        products.append(lax.dot_general(a, b, (((1,), (1,)), ((), ())), preferred_element_type=F32))
+    lower_parts = [jnp.where(upper, got[turn][...], mine[turn][...]) for turn in range(chips)]
+    upper_parts = [jnp.where(upper, mine[turn][...], got[turn][...]) for turn in range(chips)]
+    lower_parts = [lower_parts[(away - RESULT_FIRST[0]) % chips] for away in range(chips)]
+    upper_parts = [upper_parts[(away - RESULT_FIRST[1]) % chips] for away in range(chips)]
+    for whole, ref in ((upper_parts[0], tilde_ref), (lower_parts[0], proj_ref)):
+        own = jnp.where(core == 0, whole[:, :rows], whole[:, rows:])
+        ref[...] = (own.astype(F32) * weight_rows).astype(BF16)
+    products = [
+        lax.dot_general(a, b, (((1,), (1,)), ((), ())), preferred_element_type=F32)
+        for a, b in zip(upper_parts, lower_parts)
+    ]
     total = jnp.zeros(square, F32)
     for source in range(chips):
         for away in range(chips):
@@ -160,11 +165,12 @@
     def other_core(value):
         return lax.ppermute(value, "row", [(i, i ^ 1) for i in range(row_devices)])
 
-    def to_sector(value, upper_step, away):
+    def to_sector(value, upper_step, turn, first):
         pairs = []
         for s in range(sectors):
             for r in range(row_devices):
                 t = (s + (upper_step if r % 2 else -upper_step)) % sectors
+                away = (turn + first[r % 2]) % chips
                 pairs.append((s * row_devices + r, t * row_devices + (r + 2 * away) % row_devices))
         return lax.ppermute(value, ("sec", "row"), pairs)
 
@@ -172,15 +178,15 @@
     whole = jax.ShapeDtypeStruct((keep_cols, 2 * rows), BF16)
     u, v = left_factor[0].T, right_factor[0].T
     u_got, v_got = other_core(u), other_core(v)
-    own = jnp.where(is_upper(), u, v)
-    own_width = max(rows, LANES)
-    own = jnp.concatenate(
-        [
-            jnp.pad(own, ((0, 0), (0, own_width - rows))),
-            jnp.pad(joining_map.astype(BF16), ((0, keep_cols - 1), (0, own_width - states_here))),
-        ],
-        axis=0,
-    )
+    own_shape = (2 * keep_cols, max(rows, LANES))
+
+    def placed(value, row):
+        height, across = value.shape
+        spare = (row, own_shape[0] - row - height, 0), (0, own_shape[1] - across, 0)
+        return lax.pad(value, jnp.zeros((), value.dtype), spare)
+
+    own = jnp.where(is_upper(), placed(u, 0), placed(v, 0)).astype(F32)
+    own = jnp.where(iota(own_shape, 0) < keep_cols, own, placed(joining_map, keep_cols).astype(F32))
     joined = pl.pallas_call(
         functools.partial(join_kernel, states_here=states_here),
         out_shape=whole,
@@ -190,10 +196,11 @@
         cost_estimate=pl.CostEstimate(flops=JOIN_FLOPS, bytes_accessed=0, transcendentals=0),
         name="join_factor",
     )(own, u_got, v_got)
-    factors = [to_sector(joined, -1, away) for away in range(chips)]
+    factors = [to_sector(joined, -1, turn, FACTOR_FIRST) for turn in range(chips)]
 
     ul, dl = corner_ul[0], corner_dl[0]
-    ul_got, dl_got = other_core(ul), other_core(dl)
+    ul_later, dl_later, _ = lax.optimization_barrier((ul, dl, own))
+    ul_got, dl_got = other_core(ul_later), other_core(dl_later)
     half = pl.pallas_call(
         functools.partial(half_kernel, states_here=states_here),
         out_shape=jax.ShapeDtypeStruct((width, 2 * rows), BF16),
@@ -201,7 +208,7 @@
         out_specs=in_vmem(),
         compiler_params=pltpu.CompilerParams(vmem_limit_bytes=16 * MIB),
         cost_estimate=pl.CostEstimate(
-            flops=4 * rows * width * width, bytes_accessed=2 * width * (width + 4 * rows), transcendentals=0
+            flops=rows * width, bytes_accessed=rows, transcendentals=0
         ),
         name="half_product",
     )(ul, ul_got, corner_ur[0], dl, dl_got, corner_dr[0])
@@ -214,7 +221,7 @@
         compiler_params=pltpu.CompilerParams(vmem_limit_bytes=4 * MIB),
         name="apply_factor",
     )(states[None], *factors, half)
-    mine = [to_sector(applied, 1, away) for away in range(chips)]
+    mine = [to_sector(applied, 1, turn, RESULT_FIRST) for turn in range(chips)]
     theirs = [other_core(value) for value in mine]
 
     columns = jnp.arange(keep_cols, dtype=jnp.int32)

time: 22.7 us -> 21.3 us (0.938)
  other arithmetic: 1.39 us -> 0.81 us
  waiting for transfers between devices: 5.09 us -> 4.59 us
    ppermute x4, starting transfers between devices: 9.68 us -> 8.67 us  [to_sector(): return lax.ppermute(value, ('sec', 'row'), pairs)]
    ppermute x6, starting transfers between devices: 1.23 us -> 2.01 us  [other_core(): return lax.ppermute(value, 'row', [(i, i ^ 1) for i in range(row_devices)])]
    convert_element_type x1 -> x0, other arithmetic: 0.66 us -> none  [local(): joining_map.astype(BF16)]
    ppermute x4, waiting for transfers between devices: 3.96 us -> 3.41 us  [to_sector(): return lax.ppermute(value, ('sec', 'row'), pairs)]
  transfers between devices with their start and end apart: 10 -> 10, of which waited for: 5 -> 5; matrix products, arithmetic and copies ran while one was open for 6% -> 4% of each run, Pallas kernels for 8% -> 9%
where the time goes in v3:
time: 21.3 us; the launch traced here: 21.1 us
  starting transfers between devices  10.7 us (50%)
  waiting for transfers between devices  4.59 us (22%)
  Pallas kernels  2.92 us (14%)
  between operations  2.03 us (10%)
  other arithmetic  0.81 us (4%)
    ppermute x4, starting transfers between devices, to_sector(): return lax.ppermute(value, ('sec', 'row'), pairs)  8.67 us
    ppermute x4, waiting for transfers between devices, to_sector(): return lax.ppermute(value, ('sec', 'row'), pairs)  3.41 us
    ppermute x6, starting transfers between devices, other_core(): return lax.ppermute(value, 'row', [(i, i ^ 1) for i in range(row_devices)])  2.01 us
    pallas_call x1, Pallas kernels, local(): pl.pallas_call(functools.partial(half_kernel, states_here=states_here), o...  1.52 us
    ppermute x6, waiting for transfers between devices, other_core(): return lax.ppermute(value, 'row', [(i, i ^ 1) for i in range(row_devices)])  1.17 us
    select_n x1, other arithmetic, local(): jnp.where(iota(own_shape, 0) < keep_cols, own, placed(joining_map, keep_c...  0.8 us
    pallas_call x1, Pallas kernels, local(): pl.pallas_call(functools.partial(finish_kernel, width=width), out_shape=(...  0.74 us
  transfers between devices with their start and end apart: 10, of which 5 were waited for; matrix products, arithmetic and copies ran while one was open for 4% of the time, Pallas kernels for 9%

profile of v3, /device:TPU:0, one launch (start us, length us, event | category | flops | bytes accessed | tf_op | source)
XLA Modules:
  0.0 21.1 jit_solution(571796602951111568)
XLA Ops:
  0.6 0.5 %collective-permute-start = (bf16[16,256]{1,0:T(8,128)(2,1)}, bf16[16,256]{1,0:T(8,128)(2,1)S(1)}, u32[]{:S(2)}, u32[]{:S(2)}) collective-permute-start(bf16[16,256]{1,0:T(8,128)(2,1)} %bitcast.27), channel_id=1, source_target_pairs={{0,1},{1,0},{2,3},{3,2},{4,5},{5,4},{6,7},{7,6},{8,9},{9,8},{10,11... | collective-permute-start | bytes 24584 | tf_op jit(solution)/shard_map/ppermute | solution.py:166
  1.1 0.1 collective-permute-start.1
  1.2 0.8 %convert_select_fusion.own_ref = f32[32,256]{1,0:T(8,128)S(1)} fusion(s32[1,16]{1,0:T(1,128)} %param.19, bf16[16,256]{1,0:T(8,128)(2,1)} %bitcast.30, bf16[16,256]{1,0:T(8,128)(2,1)} %bitcast.28, pred[32]{0:T(512)(128)(4,1)S(1)} %iota_compare_fusion, pred[]{:T(512)S(6)} %eq.3), kind=kLoop, calls=%fused_computation | loop fusion | flops 32768 | bytes 49249 | tf_op jit(solution)/shard_map/jit(_where)/select_n | solution.py:189
  2.0 0.0 copy-start
  2.0 0.0 copy-start.1
  2.0 0.0 copy-start.2
  2.0 0.0 copy-start.3
  2.1 0.5 %collective-permute-start.4 = (bf16[256,1024]{1,0:T(8,128)(2,1)}, bf16[256,1024]{1,0:T(8,128)(2,1)S(1)}, u32[]{:S(2)}, u32[]{:S(2)}) collective-permute-start(bf16[256,1024]{1,0:T(8,128)(2,1)} %bitcast.23), channel_id=1, source_target_pairs={{0,1},{1,0},{2,3},{3,2},{4,5},{5,4},{6,7},{7,6},{8,9},{9,8},{10,11... | collective-permute-start | bytes 1572872 | tf_op jit(solution)/shard_map/ppermute | solution.py:166
  2.6 0.1 collective-permute-start.5
  2.6 0.0 collective-permute-done.u_got_ref
  2.6 0.0 collective-permute-done.1.v_got_ref
  2.6 0.4 %join_factor.1 = bf16[16,512]{1,0:T(8,128)(2,1)S(1)} custom-call(f32[32,256]{1,0:T(8,128)S(1)} %convert_select_fusion.own_ref, bf16[16,256]{1,0:T(8,128)(2,1)S(1)} %collective-permute-done.u_got_ref, bf16[16,256]{1,0:T(8,128)(2,1)S(1)} %collective-permute-done.1.v_got_ref), custom_call_target="tpu_custom_call" | custom-call | flops 10000000000 | tf_op jit(solution)/shard_map/join_factor/pallas_call | solution.py:190
  3.0 3.9 %collective-permute-start.2 = (bf16[16,512]{1,0:T(8,128)(2,1)S(1)}, bf16[16,512]{1,0:T(8,128)(2,1)S(1)}, u32[]{:S(2)}, u32[]{:S(2)}) collective-permute-start(bf16[16,512]{1,0:T(8,128)(2,1)S(1)} %join_factor.1), channel_id=1, source_target_pairs={{0,6},{1,31},{2,4},{3,29},{4,10},{5,3},{6,8},{7,1},{8,14},{9,7},{1... | collective-permute-start | bytes 49160 | tf_op jit(solution)/shard_map/ppermute | solution.py:175
  6.9 1.5 %collective-permute-start.3 = (bf16[16,512]{1,0:T(8,128)(2,1)S(1)}, bf16[16,512]{1,0:T(8,128)(2,1)S(1)}, u32[]{:S(2)}, u32[]{:S(2)}) collective-permute-start(bf16[16,512]{1,0:T(8,128)(2,1)S(1)} %join_factor.1), channel_id=1, source_target_pairs={{0,4},{1,29},{2,6},{3,31},{4,8},{5,1},{6,10},{7,3},{8,12},{9,5},{1... | collective-permute-start | bytes 49160 | tf_op jit(solution)/shard_map/ppermute | solution.py:175
  9.1 0.0 collective-permute-done.4.ul_got
  9.1 0.0 collective-permute-done.5.dl_got
  9.1 0.0 copy-done
  9.1 0.0 copy-done.1
  9.2 0.0 copy-done.2
  9.2 0.0 copy-done.3
  9.2 0.0 copy-start.4
  9.2 1.5 %half_product.1.refs_2_ = bf16[1024,512]{1,0:T(8,128)(2,1)S(1)} custom-call(bf16[256,1024]{1,0:T(8,128)(2,1)S(1)} %bitcast.24, bf16[256,1024]{1,0:T(8,128)(2,1)S(1)} %collective-permute-done.4.ul_got, bf16[1024,1024]{1,0:T(8,128)(2,1)S(1)} %bitcast.21, bf16[256,1024]{1,0:T(8,128)(2,1)S(1)} %bitcast.26, bf16[256,1024]{1,0:T(8,128)(2,1)S(1)} %collective-permute-done.5.dl_got, ...), custom_call_target="tpu_custom_call" | custom-call | flops 262144 | bytes 256 | tf_op jit(solution)/shard_map/half_product/pallas_call | solution.py:204
  10.7 1.0 %collective-permute-done.2.refs_0_ = bf16[16,512]{1,0:T(8,128)(2,1)S(1)} collective-permute-done((bf16[16,512]{1,0:T(8,128)(2,1)S(1)}, bf16[16,512]{1,0:T(8,128)(2,1)S(1)}, u32[]{:S(2)}, u32[]{:S(2)}) %collective-permute-start.2) | collective-permute-done | bytes 16416 | tf_op jit(solution)/shard_map/ppermute | solution.py:175
  11.7 1.7 %collective-permute-done.3.refs_1_ = bf16[16,512]{1,0:T(8,128)(2,1)S(1)} collective-permute-done((bf16[16,512]{1,0:T(8,128)(2,1)S(1)}, bf16[16,512]{1,0:T(8,128)(2,1)S(1)}, u32[]{:S(2)}, u32[]{:S(2)}) %collective-permute-start.3) | collective-permute-done | bytes 16416 | tf_op jit(solution)/shard_map/ppermute | solution.py:175
  13.4 0.3 %apply_factor.1 = bf16[16,512]{1,0:T(8,128)(2,1)S(1)} custom-call(s32[1,1]{1,0:T(1,128)} %bitcast.19.states_ref, bf16[16,512]{1,0:T(8,128)(2,1)S(1)} %collective-permute-done.2.refs_0_, bf16[16,512]{1,0:T(8,128)(2,1)S(1)} %collective-permute-done.3.refs_1_, bf16[1024,512]{1,0:T(8,128)(2,1)S(1)} %half_product.1.refs_2_), custom_call_target="tpu_custom_call" | custom-call | tf_op jit(solution)/shard_map/apply_factor/pallas_call | solution.py:216
  13.6 1.3 %collective-permute-start.6 = (bf16[16,512]{1,0:T(8,128)(2,1)S(1)}, bf16[16,512]{1,0:T(8,128)(2,1)S(1)}, u32[]{:S(2)}, u32[]{:S(2)}) collective-permute-start(bf16[16,512]{1,0:T(8,128)(2,1)S(1)} %apply_factor.1), channel_id=1, source_target_pairs={{0,30},{1,7},{2,28},{3,5},{4,2},{5,11},{6,0},{7,9},{8,6},{9,15},{1... | collective-permute-start | bytes 49160 | tf_op jit(solution)/shard_map/ppermute | solution.py:175
  14.9 2.0 %collective-permute-start.7 = (bf16[16,512]{1,0:T(8,128)(2,1)S(1)}, bf16[16,512]{1,0:T(8,128)(2,1)S(1)}, u32[]{:S(2)}, u32[]{:S(2)}) collective-permute-start(bf16[16,512]{1,0:T(8,128)(2,1)S(1)} %apply_factor.1), channel_id=1, source_target_pairs={{0,28},{1,5},{2,30},{3,7},{4,0},{5,9},{6,2},{7,11},{8,4},{9,13},{1... | collective-permute-start | bytes 49160 | tf_op jit(solution)/shard_map/ppermute | solution.py:175
  17.5 0.8 %collective-permute-done.6.refs_0_ = bf16[16,512]{1,0:T(8,128)(2,1)S(1)} collective-permute-done((bf16[16,512]{1,0:T(8,128)(2,1)S(1)}, bf16[16,512]{1,0:T(8,128)(2,1)S(1)}, u32[]{:S(2)}, u32[]{:S(2)}) %collective-permute-start.6) | collective-permute-done | bytes 16416 | tf_op jit(solution)/shard_map/ppermute | solution.py:175
  18.3 0.8 %collective-permute-start.8 = (bf16[16,512]{1,0:T(8,128)(2,1)S(1)}, bf16[16,512]{1,0:T(8,128)(2,1)S(1)}, u32[]{:S(2)}, u32[]{:S(2)}) collective-permute-start(bf16[16,512]{1,0:T(8,128)(2,1)S(1)} %collective-permute-done.6.refs_0_), channel_id=1, source_target_pairs={{0,1},{1,0},{2,3},{3,2},{4,5},{5,4},{6,7},{7,6},{8,9},{9,8},{10,11... | collective-permute-start | bytes 49160 | tf_op jit(solution)/shard_map/ppermute | solution.py:166
  19.1 0.0 collective-permute-done.7.refs_1_
  19.1 0.0 collective-permute-start.9
  19.1 0.0 copy-done.4
  19.1 0.8 %collective-permute-done.8.refs_2_ = bf16[16,512]{1,0:T(8,128)(2,1)S(1)} collective-permute-done((bf16[16,512]{1,0:T(8,128)(2,1)S(1)}, bf16[16,512]{1,0:T(8,128)(2,1)S(1)}, u32[]{:S(2)}, u32[]{:S(2)}) %collective-permute-start.8) | collective-permute-done | bytes 16416 | tf_op jit(solution)/shard_map/ppermute | solution.py:166
  20.0 0.3 %collective-permute-done.9.refs_3_ = bf16[16,512]{1,0:T(8,128)(2,1)S(1)} collective-permute-done((bf16[16,512]{1,0:T(8,128)(2,1)S(1)}, bf16[16,512]{1,0:T(8,128)(2,1)S(1)}, u32[]{:S(2)}, u32[]{:S(2)}) %collective-permute-start.9) | collective-permute-done | bytes 16416 | tf_op jit(solution)/shard_map/ppermute | solution.py:166
  20.3 0.7 %finish.1 = (bf16[16,256]{1,0:T(8,128)(2,1)}, bf16[16,256]{1,0:T(8,128)(2,1)}, f32[16,16]{1,0:T(8,128)}) custom-call(f32[1,16]{1,0:T(1,128)S(1)} %compare_select_fusion.weight_ref, bf16[16,512]{1,0:T(8,128)(2,1)S(1)} %collective-permute-done.6.refs_0_, bf16[16,512]{1,0:T(8,128)(2,1)S(1)} %collective-permute-done.7.refs_1_, ...), custom_call_target="tpu_custom_call" | custom-call | tf_op jit(solution)/shard_map/finish/pallas_call | solution.py:229
  (2 shorter events, 0.0 us)
Async XLA Ops:
  0.6 2.0 %collective-permute-start = (bf16[16,256]{1,0:T(8,128)(2,1)}, bf16[16,256]{1,0:T(8,128)(2,1)S(1)}, u32[]{:S(2)}, u32[]{:S(2)}) collective-permute-start(bf16[16,256]{1,0:T(8,128)(2,1)} %bitcast.27), channel_id=1, source_target_pairs={{0,1},{1,0},{2,3},{3,2},{4,5},{5,4},{6,7},{7,6},{8,9},{9,8},{10,11... | collective-permute-start | bytes 24584 | tf_op jit(solution)/shard_map/ppermute | solution.py:166
  1.1 1.5 %collective-permute-start.1 = (bf16[16,256]{1,0:T(8,128)(2,1)}, bf16[16,256]{1,0:T(8,128)(2,1)S(1)}, u32[]{:S(2)}, u32[]{:S(2)}) collective-permute-start(bf16[16,256]{1,0:T(8,128)(2,1)} %bitcast.29), channel_id=1, source_target_pairs={{0,1},{1,0},{2,3},{3,2},{4,5},{5,4},{6,7},{7,6},{8,9},{9,8},{10,11... | collective-permute-start | bytes 24584 | tf_op jit(solution)/shard_map/ppermute | solution.py:166
  2.0 7.1 %copy-start = (bf16[1,1024,1024]{2,1,0:T(8,128)(2,1)S(1)}, bf16[1,1024,1024]{2,1,0:T(8,128)(2,1)}, u32[]{:S(2)}) copy-start(bf16[1,1024,1024]{2,1,0:T(8,128)(2,1)} %param.11) | copy-start | bytes 6291460
  2.0 7.1 %copy-start.1 = (bf16[1,1024,1024]{2,1,0:T(8,128)(2,1)S(1)}, bf16[1,1024,1024]{2,1,0:T(8,128)(2,1)}, u32[]{:S(2)}) copy-start(bf16[1,1024,1024]{2,1,0:T(8,128)(2,1)} %param.13) | copy-start | bytes 6291460
  2.0 7.1 %copy-start.2 = (bf16[1,256,1024]{2,1,0:T(8,128)(2,1)S(1)}, bf16[1,256,1024]{2,1,0:T(8,128)(2,1)}, u32[]{:S(2)}) copy-start(bf16[1,256,1024]{2,1,0:T(8,128)(2,1)} %param.10) | copy-start | bytes 1572868
  2.0 7.1 %copy-start.3 = (bf16[1,256,1024]{2,1,0:T(8,128)(2,1)S(1)}, bf16[1,256,1024]{2,1,0:T(8,128)(2,1)}, u32[]{:S(2)}) copy-start(bf16[1,256,1024]{2,1,0:T(8,128)(2,1)} %param.12) | copy-start | bytes 1572868
  2.1 7.1 %collective-permute-start.4 = (bf16[256,1024]{1,0:T(8,128)(2,1)}, bf16[256,1024]{1,0:T(8,128)(2,1)S(1)}, u32[]{:S(2)}, u32[]{:S(2)}) collective-permute-start(bf16[256,1024]{1,0:T(8,128)(2,1)} %bitcast.23), channel_id=1, source_target_pairs={{0,1},{1,0},{2,3},{3,2},{4,5},{5,4},{6,7},{7,6},{8,9},{9,8},{10,11... | collective-permute-start | bytes 1572872 | tf_op jit(solution)/shard_map/ppermute | solution.py:166
  2.6 6.6 %collective-permute-start.5 = (bf16[256,1024]{1,0:T(8,128)(2,1)}, bf16[256,1024]{1,0:T(8,128)(2,1)S(1)}, u32[]{:S(2)}, u32[]{:S(2)}) collective-permute-start(bf16[256,1024]{1,0:T(8,128)(2,1)} %bitcast.25), channel_id=1, source_target_pairs={{0,1},{1,0},{2,3},{3,2},{4,5},{5,4},{6,7},{7,6},{8,9},{9,8},{10,11... | collective-permute-start | bytes 1572872 | tf_op jit(solution)/shard_map/ppermute | solution.py:166
  3.0 8.7 %collective-permute-start.2 = (bf16[16,512]{1,0:T(8,128)(2,1)S(1)}, bf16[16,512]{1,0:T(8,128)(2,1)S(1)}, u32[]{:S(2)}, u32[]{:S(2)}) collective-permute-start(bf16[16,512]{1,0:T(8,128)(2,1)S(1)} %join_factor.1), channel_id=1, source_target_pairs={{0,6},{1,31},{2,4},{3,29},{4,10},{5,3},{6,8},{7,1},{8,14},{9,7},{1... | collective-permute-start | bytes 49160 | tf_op jit(solution)/shard_map/ppermute | solution.py:175
  6.9 6.4 %collective-permute-start.3 = (bf16[16,512]{1,0:T(8,128)(2,1)S(1)}, bf16[16,512]{1,0:T(8,128)(2,1)S(1)}, u32[]{:S(2)}, u32[]{:S(2)}) collective-permute-start(bf16[16,512]{1,0:T(8,128)(2,1)S(1)} %join_factor.1), channel_id=1, source_target_pairs={{0,4},{1,29},{2,6},{3,31},{4,8},{5,1},{6,10},{7,3},{8,12},{9,5},{1... | collective-permute-start | bytes 49160 | tf_op jit(solution)/shard_map/ppermute | solution.py:175
  9.2 10.0 %copy-start.4 = (f32[1,16]{1,0:T(1,128)S(1)}, f32[1,16]{1,0:T(1,128)}, u32[]{:S(2)}) copy-start(f32[1,16]{1,0:T(1,128)} %param.16) | copy-start | bytes 196
  13.6 4.6 %collective-permute-start.6 = (bf16[16,512]{1,0:T(8,128)(2,1)S(1)}, bf16[16,512]{1,0:T(8,128)(2,1)S(1)}, u32[]{:S(2)}, u32[]{:S(2)}) collective-permute-start(bf16[16,512]{1,0:T(8,128)(2,1)S(1)} %apply_factor.1), channel_id=1, source_target_pairs={{0,30},{1,7},{2,28},{3,5},{4,2},{5,11},{6,0},{7,9},{8,6},{9,15},{1... | collective-permute-start | bytes 49160 | tf_op jit(solution)/shard_map/ppermute | solution.py:175
  14.9 4.2 %collective-permute-start.7 = (bf16[16,512]{1,0:T(8,128)(2,1)S(1)}, bf16[16,512]{1,0:T(8,128)(2,1)S(1)}, u32[]{:S(2)}, u32[]{:S(2)}) collective-permute-start(bf16[16,512]{1,0:T(8,128)(2,1)S(1)} %apply_factor.1), channel_id=1, source_target_pairs={{0,28},{1,5},{2,30},{3,7},{4,0},{5,9},{6,2},{7,11},{8,4},{9,13},{1... | collective-permute-start | bytes 49160 | tf_op jit(solution)/shard_map/ppermute | solution.py:175
  18.3 1.7 %collective-permute-start.8 = (bf16[16,512]{1,0:T(8,128)(2,1)S(1)}, bf16[16,512]{1,0:T(8,128)(2,1)S(1)}, u32[]{:S(2)}, u32[]{:S(2)}) collective-permute-start(bf16[16,512]{1,0:T(8,128)(2,1)S(1)} %collective-permute-done.6.refs_0_), channel_id=1, source_target_pairs={{0,1},{1,0},{2,3},{3,2},{4,5},{5,4},{6,7},{7,6},{8,9},{9,8},{10,11... | collective-permute-start | bytes 49160 | tf_op jit(solution)/shard_map/ppermute | solution.py:166
  19.1 1.2 %collective-permute-start.9 = (bf16[16,512]{1,0:T(8,128)(2,1)S(1)}, bf16[16,512]{1,0:T(8,128)(2,1)S(1)}, u32[]{:S(2)}, u32[]{:S(2)}) collective-permute-start(bf16[16,512]{1,0:T(8,128)(2,1)S(1)} %collective-permute-done.7.refs_1_), channel_id=1, source_target_pairs={{0,1},{1,0},{2,3},{3,2},{4,5},{5,4},{6,7},{7,6},{8,9},{9,8},{10,11... | collective-permute-start | bytes 49160 | tf_op jit(solution)/shard_map/ppermute | solution.py:166

commit v4 on v3

--- a/solution.py
+++ b/solution.py
@@ -29,27 +29,28 @@
     own = own_ref[:keep_cols, :rows].astype(BF16)
     got = jnp.where(upper, u_got_ref[...], v_got_ref[...])
     both = jnp.concatenate([jnp.where(upper, got, own), jnp.where(upper, own, got)], axis=1)
-    lane = iota((1, LANES), 1)
-    order = own_ref[keep_cols : keep_cols + 1, :LANES]
-    order = jnp.where(lane < states_here, order, 0.0)
-    distance = states_here
-    while distance < LANES:
-        order += pltpu.roll(order, distance, 1)
-        distance *= 2
-    wanted = order.astype(jnp.int32) + lane // states_here * states_here
-    mover = jnp.where(iota((LANES, LANES), 0) == wanted, 1.0, 0.0).astype(BF16)
-    for start in range(0, 2 * rows, LANES):
-        moved = lax.dot_general(
-            both[:, start : start + LANES], mover, (((1,), (1,)), ((), ())), preferred_element_type=F32
-        )
-        out_ref[:, start : start + LANES] = moved.astype(BF16)
-
-
-def half_kernel(ul, ul_got, ur, dl, dl_got, dr, out_ref, *, states_here):
+    shape = (states_here, LANES)
+    order = jnp.broadcast_to(own_ref[keep_cols : keep_cols + 1, :LANES], shape)
+    order = jnp.sum(jnp.where(iota(shape, 0) == iota(shape, 1), order, 0.0), axis=1, keepdims=True)
+    order = jnp.broadcast_to(order, shape).astype(jnp.int32)
+    square = (LANES, LANES)
+    wanted = jnp.concatenate([order] * (LANES // states_here), axis=0) + iota(square, 0) // states_here * states_here
+    mover = jnp.where(iota(square, 1) == wanted, 1.0, 0.0).astype(BF16)
+    starts = range(0, 2 * rows, LANES)
+    stacked = jnp.concatenate([both[:, start : start + LANES] for start in starts], axis=0)
+    moved = jnp.dot(stacked, mover, preferred_element_type=F32).astype(BF16)
+    for i, start in enumerate(starts):
+        out_ref[:, start : start + LANES] = moved[i * keep_cols : (i + 1) * keep_cols]
+
+
+def half_kernel(states_ref, ul, ul_got, ur, dl, dl_got, dr, out_ref, *, states_here):
     rows, width = ul.shape
     step = 2 * LANES
     group = LANES // states_here
     lane = iota((1, LANES), 1)
+    chunk_shape = (states_here, LANES)
+    live_rows = iota(chunk_shape, 0) < states_ref[0]
+    live = live_rows & (iota(chunk_shape, 1) % states_here < states_ref[0])
     odd = {distance: (lane // states_here // distance) % 2 == 1 for distance in range(1, group)}
 
     def regroup(block):
@@ -79,7 +80,8 @@
                     for q in range(0, step, LANES):
                         for i, chunk in enumerate(regroup(full[p : p + LANES, q : q + LANES])):
                             at = column + q + i * states_here
-                            out_ref[at : at + states_here, base + p : base + p + LANES] = chunk.astype(BF16)
+                            chunk = jnp.where(live, chunk, 0.0).astype(BF16)
+                            out_ref[at : at + states_here, base + p : base + p + LANES] = chunk
 
     upper = is_upper()
 
@@ -92,20 +94,18 @@
         work(dl, dl_got, dr)
 
 
-def apply_kernel(states_ref, *refs, states_here):
+def apply_kernel(*refs):
     *factors, half_ref, out_ref = refs
     chips = len(factors)
     chip = lax.axis_index("row") // 2
     depth = factors[0].shape[1]
-    live = iota((1, depth), 1) % states_here < states_ref[...]
     total = jnp.zeros(out_ref.shape, F32)
     first = jnp.where(is_upper(), FACTOR_FIRST[1], FACTOR_FIRST[0])
     for turn in range(chips):
         source = lax.rem(chip - turn - first + 2 * chips, chips)
         part = half_ref[pl.ds(pl.multiple_of(source * depth, depth), depth), :]
-        factor = jnp.where(live, factors[turn][...], jnp.zeros((), BF16))
-        total += jnp.dot(factor, part, preferred_element_type=F32)
-    out_ref[...] = jnp.where(live, total, 0.0).astype(BF16)
+        total += jnp.dot(factors[turn][...], part, preferred_element_type=F32)
+    out_ref[...] = total.astype(BF16)
 
 
 def finish_kernel(weight_ref, *refs, width):
@@ -204,23 +204,23 @@
     half = pl.pallas_call(
         functools.partial(half_kernel, states_here=states_here),
         out_shape=jax.ShapeDtypeStruct((width, 2 * rows), BF16),
-        in_specs=[in_vmem()] * 6,
+        in_specs=[pl.BlockSpec(memory_space=pltpu.SMEM)] + [in_vmem()] * 6,
         out_specs=in_vmem(),
         compiler_params=pltpu.CompilerParams(vmem_limit_bytes=16 * MIB),
         cost_estimate=pl.CostEstimate(
             flops=rows * width, bytes_accessed=rows, transcendentals=0
         ),
         name="half_product",
-    )(ul, ul_got, corner_ur[0], dl, dl_got, corner_dr[0])
+    )(states, ul, ul_got, corner_ur[0], dl, dl_got, corner_dr[0])
 
     applied = pl.pallas_call(
-        functools.partial(apply_kernel, states_here=states_here),
+        apply_kernel,
         out_shape=whole,
-        in_specs=[in_vmem()] * (chips + 2),
+        in_specs=[in_vmem()] * (chips + 1),
         out_specs=in_vmem(),
         compiler_params=pltpu.CompilerParams(vmem_limit_bytes=4 * MIB),
         name="apply_factor",
-    )(states[None], *factors, half)
+    )(*factors, half)
     mine = [to_sector(applied, 1, turn, RESULT_FIRST) for turn in range(chips)]
     theirs = [other_core(value) for value in mine]
 

time: 21.3 us -> 21.1 us (level)
  transfers between devices with their start and end apart: 10 -> 10, of which waited for: 5 -> 5; matrix products, arithmetic and copies ran while one was open for 4% -> 4% of each run, Pallas kernels for 9% -> 8%
where the time goes in v4:
time: 21.1 us; the launch traced here: 20.8 us
  starting transfers between devices  10.7 us (51%)
  waiting for transfers between devices  4.59 us (22%)
  Pallas kernels  2.71 us (13%)
  between operations  2.03 us (10%)
  other arithmetic  0.81 us (4%)
    ppermute x4, starting transfers between devices, to_sector(): return lax.ppermute(value, ('sec', 'row'), pairs)  8.65 us
    ppermute x4, waiting for transfers between devices, to_sector(): return lax.ppermute(value, ('sec', 'row'), pairs)  3.42 us
    ppermute x6, starting transfers between devices, other_core(): return lax.ppermute(value, 'row', [(i, i ^ 1) for i in range(row_devices)])  2.01 us
    pallas_call x1, Pallas kernels, local(): pl.pallas_call(functools.partial(half_kernel, states_here=states_here), o...  1.52 us
    ppermute x6, waiting for transfers between devices, other_core(): return lax.ppermute(value, 'row', [(i, i ^ 1) for i in range(row_devices)])  1.17 us
    select_n x1, other arithmetic, local(): jnp.where(iota(own_shape, 0) < keep_cols, own, placed(joining_map, keep_c...  0.8 us
    pallas_call x1, Pallas kernels, local(): pl.pallas_call(functools.partial(finish_kernel, width=width), out_shape=(...  0.74 us
  transfers between devices with their start and end apart: 10, of which 5 were waited for; matrix products, arithmetic and copies ran while one was open for 4% of the time, Pallas kernels for 8%

profile of v4, /device:TPU:0, one launch (start us, length us, event | category | flops | bytes accessed | tf_op | source)
XLA Modules:
  0.0 20.8 jit_solution(8217383235425186675)
XLA Ops:
  0.6 0.5 %collective-permute-start = (bf16[16,256]{1,0:T(8,128)(2,1)}, bf16[16,256]{1,0:T(8,128)(2,1)S(1)}, u32[]{:S(2)}, u32[]{:S(2)}) collective-permute-start(bf16[16,256]{1,0:T(8,128)(2,1)} %bitcast.25), channel_id=1, source_target_pairs={{0,1},{1,0},{2,3},{3,2},{4,5},{5,4},{6,7},{7,6},{8,9},{9,8},{10,11... | collective-permute-start | bytes 24584 | tf_op jit(solution)/shard_map/ppermute | solution.py:166
  1.1 0.1 collective-permute-start.1
  1.2 0.8 %convert_select_fusion.own_ref = f32[32,256]{1,0:T(8,128)S(1)} fusion(s32[1,16]{1,0:T(1,128)} %param.19, bf16[16,256]{1,0:T(8,128)(2,1)} %bitcast.28, bf16[16,256]{1,0:T(8,128)(2,1)} %bitcast.26, pred[32]{0:T(512)(128)(4,1)S(1)} %iota_compare_fusion, pred[]{:T(512)S(6)} %eq.3), kind=kLoop, calls=%fused_computation | loop fusion | flops 32768 | bytes 49249 | tf_op jit(solution)/shard_map/jit(_where)/select_n | solution.py:189
  2.0 0.0 copy-start
  2.0 0.0 copy-start.1
  2.0 0.0 copy-start.2
  2.0 0.0 copy-start.3
  2.1 0.5 %collective-permute-start.4 = (bf16[256,1024]{1,0:T(8,128)(2,1)}, bf16[256,1024]{1,0:T(8,128)(2,1)S(1)}, u32[]{:S(2)}, u32[]{:S(2)}) collective-permute-start(bf16[256,1024]{1,0:T(8,128)(2,1)} %bitcast.21), channel_id=1, source_target_pairs={{0,1},{1,0},{2,3},{3,2},{4,5},{5,4},{6,7},{7,6},{8,9},{9,8},{10,11... | collective-permute-start | bytes 1572872 | tf_op jit(solution)/shard_map/ppermute | solution.py:166
  2.6 0.1 collective-permute-start.5
  2.6 0.0 collective-permute-done.u_got_ref
  2.6 0.0 collective-permute-done.1.v_got_ref
  2.6 0.2 %join_factor.1 = bf16[16,512]{1,0:T(8,128)(2,1)S(1)} custom-call(f32[32,256]{1,0:T(8,128)S(1)} %convert_select_fusion.own_ref, bf16[16,256]{1,0:T(8,128)(2,1)S(1)} %collective-permute-done.u_got_ref, bf16[16,256]{1,0:T(8,128)(2,1)S(1)} %collective-permute-done.1.v_got_ref), custom_call_target="tpu_custom_call" | custom-call | flops 10000000000 | tf_op jit(solution)/shard_map/join_factor/pallas_call | solution.py:190
  2.9 3.9 %collective-permute-start.2 = (bf16[16,512]{1,0:T(8,128)(2,1)S(1)}, bf16[16,512]{1,0:T(8,128)(2,1)S(1)}, u32[]{:S(2)}, u32[]{:S(2)}) collective-permute-start(bf16[16,512]{1,0:T(8,128)(2,1)S(1)} %join_factor.1), channel_id=1, source_target_pairs={{0,6},{1,31},{2,4},{3,29},{4,10},{5,3},{6,8},{7,1},{8,14},{9,7},{1... | collective-permute-start | bytes 49160 | tf_op jit(solution)/shard_map/ppermute | solution.py:175
  6.7 1.5 %collective-permute-start.3 = (bf16[16,512]{1,0:T(8,128)(2,1)S(1)}, bf16[16,512]{1,0:T(8,128)(2,1)S(1)}, u32[]{:S(2)}, u32[]{:S(2)}) collective-permute-start(bf16[16,512]{1,0:T(8,128)(2,1)S(1)} %join_factor.1), channel_id=1, source_target_pairs={{0,4},{1,29},{2,6},{3,31},{4,8},{5,1},{6,10},{7,3},{8,12},{9,5},{1... | collective-permute-start | bytes 49160 | tf_op jit(solution)/shard_map/ppermute | solution.py:175
  8.9 0.0 collective-permute-done.4.ul_got
  8.9 0.0 collective-permute-done.5.dl_got
  9.0 0.0 copy-done
  9.0 0.0 copy-done.1
  9.0 0.0 copy-done.2
  9.0 0.0 copy-done.3
  9.0 0.0 copy-start.4
  9.0 1.5 %half_product.1.refs_2_ = bf16[1024,512]{1,0:T(8,128)(2,1)S(1)} custom-call(s32[1]{0:T(128)S(6)} %copy.13.states_ref, bf16[256,1024]{1,0:T(8,128)(2,1)S(1)} %bitcast.22, bf16[256,1024]{1,0:T(8,128)(2,1)S(1)} %collective-permute-done.4.ul_got, bf16[1024,1024]{1,0:T(8,128)(2,1)S(1)} %bitcast.19, bf16[256,1024]{1,0:T(8,128)(2,1)S(1)} %bitcast.24, ...), custom_call_target="tpu_custom_call" | custom-call | flops 262144 | bytes 256 | tf_op jit(solution)/shard_map/half_product/pallas_call | solution.py:204
  10.5 1.0 %collective-permute-done.2.refs_0_ = bf16[16,512]{1,0:T(8,128)(2,1)S(1)} collective-permute-done((bf16[16,512]{1,0:T(8,128)(2,1)S(1)}, bf16[16,512]{1,0:T(8,128)(2,1)S(1)}, u32[]{:S(2)}, u32[]{:S(2)}) %collective-permute-start.2) | collective-permute-done | bytes 16416 | tf_op jit(solution)/shard_map/ppermute | solution.py:175
  11.5 1.7 %collective-permute-done.3.refs_1_ = bf16[16,512]{1,0:T(8,128)(2,1)S(1)} collective-permute-done((bf16[16,512]{1,0:T(8,128)(2,1)S(1)}, bf16[16,512]{1,0:T(8,128)(2,1)S(1)}, u32[]{:S(2)}, u32[]{:S(2)}) %collective-permute-start.3) | collective-permute-done | bytes 16416 | tf_op jit(solution)/shard_map/ppermute | solution.py:175
  13.2 0.2 %apply_factor.1 = bf16[16,512]{1,0:T(8,128)(2,1)S(1)} custom-call(bf16[16,512]{1,0:T(8,128)(2,1)S(1)} %collective-permute-done.2.refs_0_, bf16[16,512]{1,0:T(8,128)(2,1)S(1)} %collective-permute-done.3.refs_1_, bf16[1024,512]{1,0:T(8,128)(2,1)S(1)} %half_product.1.refs_2_), custom_call_target="tpu_custom_call" | custom-call | tf_op jit(solution)/shard_map/apply_factor/pallas_call | solution.py:216
  13.4 1.3 %collective-permute-start.6 = (bf16[16,512]{1,0:T(8,128)(2,1)S(1)}, bf16[16,512]{1,0:T(8,128)(2,1)S(1)}, u32[]{:S(2)}, u32[]{:S(2)}) collective-permute-start(bf16[16,512]{1,0:T(8,128)(2,1)S(1)} %apply_factor.1), channel_id=1, source_target_pairs={{0,30},{1,7},{2,28},{3,5},{4,2},{5,11},{6,0},{7,9},{8,6},{9,15},{1... | collective-permute-start | bytes 49160 | tf_op jit(solution)/shard_map/ppermute | solution.py:175
  14.7 2.0 %collective-permute-start.7 = (bf16[16,512]{1,0:T(8,128)(2,1)S(1)}, bf16[16,512]{1,0:T(8,128)(2,1)S(1)}, u32[]{:S(2)}, u32[]{:S(2)}) collective-permute-start(bf16[16,512]{1,0:T(8,128)(2,1)S(1)} %apply_factor.1), channel_id=1, source_target_pairs={{0,28},{1,5},{2,30},{3,7},{4,0},{5,9},{6,2},{7,11},{8,4},{9,13},{1... | collective-permute-start | bytes 49160 | tf_op jit(solution)/shard_map/ppermute | solution.py:175
  17.3 0.8 %collective-permute-done.6.refs_0_ = bf16[16,512]{1,0:T(8,128)(2,1)S(1)} collective-permute-done((bf16[16,512]{1,0:T(8,128)(2,1)S(1)}, bf16[16,512]{1,0:T(8,128)(2,1)S(1)}, u32[]{:S(2)}, u32[]{:S(2)}) %collective-permute-start.6) | collective-permute-done | bytes 16416 | tf_op jit(solution)/shard_map/ppermute | solution.py:175
  18.1 0.8 %collective-permute-start.8 = (bf16[16,512]{1,0:T(8,128)(2,1)S(1)}, bf16[16,512]{1,0:T(8,128)(2,1)S(1)}, u32[]{:S(2)}, u32[]{:S(2)}) collective-permute-start(bf16[16,512]{1,0:T(8,128)(2,1)S(1)} %collective-permute-done.6.refs_0_), channel_id=1, source_target_pairs={{0,1},{1,0},{2,3},{3,2},{4,5},{5,4},{6,7},{7,6},{8,9},{9,8},{10,11... | collective-permute-start | bytes 49160 | tf_op jit(solution)/shard_map/ppermute | solution.py:166
  18.9 0.0 collective-permute-done.7.refs_1_
  18.9 0.0 collective-permute-start.9
  18.9 0.0 copy-done.4
  18.9 0.8 %collective-permute-done.8.refs_2_ = bf16[16,512]{1,0:T(8,128)(2,1)S(1)} collective-permute-done((bf16[16,512]{1,0:T(8,128)(2,1)S(1)}, bf16[16,512]{1,0:T(8,128)(2,1)S(1)}, u32[]{:S(2)}, u32[]{:S(2)}) %collective-permute-start.8) | collective-permute-done | bytes 16416 | tf_op jit(solution)/shard_map/ppermute | solution.py:166
  19.7 0.3 %collective-permute-done.9.refs_3_ = bf16[16,512]{1,0:T(8,128)(2,1)S(1)} collective-permute-done((bf16[16,512]{1,0:T(8,128)(2,1)S(1)}, bf16[16,512]{1,0:T(8,128)(2,1)S(1)}, u32[]{:S(2)}, u32[]{:S(2)}) %collective-permute-start.9) | collective-permute-done | bytes 16416 | tf_op jit(solution)/shard_map/ppermute | solution.py:166
  20.1 0.7 %finish.1 = (bf16[16,256]{1,0:T(8,128)(2,1)}, bf16[16,256]{1,0:T(8,128)(2,1)}, f32[16,16]{1,0:T(8,128)}) custom-call(f32[1,16]{1,0:T(1,128)S(1)} %compare_select_fusion.weight_ref, bf16[16,512]{1,0:T(8,128)(2,1)S(1)} %collective-permute-done.6.refs_0_, bf16[16,512]{1,0:T(8,128)(2,1)S(1)} %collective-permute-done.7.refs_1_, ...), custom_call_target="tpu_custom_call" | custom-call | tf_op jit(solution)/shard_map/finish/pallas_call | solution.py:229
  (2 shorter events, 0.0 us)
Async XLA Ops:
  0.6 2.0 %collective-permute-start = (bf16[16,256]{1,0:T(8,128)(2,1)}, bf16[16,256]{1,0:T(8,128)(2,1)S(1)}, u32[]{:S(2)}, u32[]{:S(2)}) collective-permute-start(bf16[16,256]{1,0:T(8,128)(2,1)} %bitcast.25), channel_id=1, source_target_pairs={{0,1},{1,0},{2,3},{3,2},{4,5},{5,4},{6,7},{7,6},{8,9},{9,8},{10,11... | collective-permute-start | bytes 24584 | tf_op jit(solution)/shard_map/ppermute | solution.py:166
  1.1 1.5 %collective-permute-start.1 = (bf16[16,256]{1,0:T(8,128)(2,1)}, bf16[16,256]{1,0:T(8,128)(2,1)S(1)}, u32[]{:S(2)}, u32[]{:S(2)}) collective-permute-start(bf16[16,256]{1,0:T(8,128)(2,1)} %bitcast.27), channel_id=1, source_target_pairs={{0,1},{1,0},{2,3},{3,2},{4,5},{5,4},{6,7},{7,6},{8,9},{9,8},{10,11... | collective-permute-start | bytes 24584 | tf_op jit(solution)/shard_map/ppermute | solution.py:166
  2.0 6.9 %copy-start = (bf16[1,1024,1024]{2,1,0:T(8,128)(2,1)S(1)}, bf16[1,1024,1024]{2,1,0:T(8,128)(2,1)}, u32[]{:S(2)}) copy-start(bf16[1,1024,1024]{2,1,0:T(8,128)(2,1)} %param.11) | copy-start | bytes 6291460
  2.0 6.9 %copy-start.1 = (bf16[1,1024,1024]{2,1,0:T(8,128)(2,1)S(1)}, bf16[1,1024,1024]{2,1,0:T(8,128)(2,1)}, u32[]{:S(2)}) copy-start(bf16[1,1024,1024]{2,1,0:T(8,128)(2,1)} %param.13) | copy-start | bytes 6291460
  2.0 6.9 %copy-start.2 = (bf16[1,256,1024]{2,1,0:T(8,128)(2,1)S(1)}, bf16[1,256,1024]{2,1,0:T(8,128)(2,1)}, u32[]{:S(2)}) copy-start(bf16[1,256,1024]{2,1,0:T(8,128)(2,1)} %param.10) | copy-start | bytes 1572868
  2.0 6.9 %copy-start.3 = (bf16[1,256,1024]{2,1,0:T(8,128)(2,1)S(1)}, bf16[1,256,1024]{2,1,0:T(8,128)(2,1)}, u32[]{:S(2)}) copy-start(bf16[1,256,1024]{2,1,0:T(8,128)(2,1)} %param.12) | copy-start | bytes 1572868
  2.1 6.9 %collective-permute-start.4 = (bf16[256,1024]{1,0:T(8,128)(2,1)}, bf16[256,1024]{1,0:T(8,128)(2,1)S(1)}, u32[]{:S(2)}, u32[]{:S(2)}) collective-permute-start(bf16[256,1024]{1,0:T(8,128)(2,1)} %bitcast.21), channel_id=1, source_target_pairs={{0,1},{1,0},{2,3},{3,2},{4,5},{5,4},{6,7},{7,6},{8,9},{9,8},{10,11... | collective-permute-start | bytes 1572872 | tf_op jit(solution)/shard_map/ppermute | solution.py:166
  2.6 6.4 %collective-permute-start.5 = (bf16[256,1024]{1,0:T(8,128)(2,1)}, bf16[256,1024]{1,0:T(8,128)(2,1)S(1)}, u32[]{:S(2)}, u32[]{:S(2)}) collective-permute-start(bf16[256,1024]{1,0:T(8,128)(2,1)} %bitcast.23), channel_id=1, source_target_pairs={{0,1},{1,0},{2,3},{3,2},{4,5},{5,4},{6,7},{7,6},{8,9},{9,8},{10,11... | collective-permute-start | bytes 1572872 | tf_op jit(solution)/shard_map/ppermute | solution.py:166
  2.9 8.6 %collective-permute-start.2 = (bf16[16,512]{1,0:T(8,128)(2,1)S(1)}, bf16[16,512]{1,0:T(8,128)(2,1)S(1)}, u32[]{:S(2)}, u32[]{:S(2)}) collective-permute-start(bf16[16,512]{1,0:T(8,128)(2,1)S(1)} %join_factor.1), channel_id=1, source_target_pairs={{0,6},{1,31},{2,4},{3,29},{4,10},{5,3},{6,8},{7,1},{8,14},{9,7},{1... | collective-permute-start | bytes 49160 | tf_op jit(solution)/shard_map/ppermute | solution.py:175
  6.7 6.4 %collective-permute-start.3 = (bf16[16,512]{1,0:T(8,128)(2,1)S(1)}, bf16[16,512]{1,0:T(8,128)(2,1)S(1)}, u32[]{:S(2)}, u32[]{:S(2)}) collective-permute-start(bf16[16,512]{1,0:T(8,128)(2,1)S(1)} %join_factor.1), channel_id=1, source_target_pairs={{0,4},{1,29},{2,6},{3,31},{4,8},{5,1},{6,10},{7,3},{8,12},{9,5},{1... | collective-permute-start | bytes 49160 | tf_op jit(solution)/shard_map/ppermute | solution.py:175
  9.0 9.9 %copy-start.4 = (f32[1,16]{1,0:T(1,128)S(1)}, f32[1,16]{1,0:T(1,128)}, u32[]{:S(2)}) copy-start(f32[1,16]{1,0:T(1,128)} %param.16) | copy-start | bytes 196
  13.4 4.7 %collective-permute-start.6 = (bf16[16,512]{1,0:T(8,128)(2,1)S(1)}, bf16[16,512]{1,0:T(8,128)(2,1)S(1)}, u32[]{:S(2)}, u32[]{:S(2)}) collective-permute-start(bf16[16,512]{1,0:T(8,128)(2,1)S(1)} %apply_factor.1), channel_id=1, source_target_pairs={{0,30},{1,7},{2,28},{3,5},{4,2},{5,11},{6,0},{7,9},{8,6},{9,15},{1... | collective-permute-start | bytes 49160 | tf_op jit(solution)/shard_map/ppermute | solution.py:175
  14.7 4.2 %collective-permute-start.7 = (bf16[16,512]{1,0:T(8,128)(2,1)S(1)}, bf16[16,512]{1,0:T(8,128)(2,1)S(1)}, u32[]{:S(2)}, u32[]{:S(2)}) collective-permute-start(bf16[16,512]{1,0:T(8,128)(2,1)S(1)} %apply_factor.1), channel_id=1, source_target_pairs={{0,28},{1,5},{2,30},{3,7},{4,0},{5,9},{6,2},{7,11},{8,4},{9,13},{1... | collective-permute-start | bytes 49160 | tf_op jit(solution)/shard_map/ppermute | solution.py:175
  18.1 1.7 %collective-permute-start.8 = (bf16[16,512]{1,0:T(8,128)(2,1)S(1)}, bf16[16,512]{1,0:T(8,128)(2,1)S(1)}, u32[]{:S(2)}, u32[]{:S(2)}) collective-permute-start(bf16[16,512]{1,0:T(8,128)(2,1)S(1)} %collective-permute-done.6.refs_0_), channel_id=1, source_target_pairs={{0,1},{1,0},{2,3},{3,2},{4,5},{5,4},{6,7},{7,6},{8,9},{9,8},{10,11... | collective-permute-start | bytes 49160 | tf_op jit(solution)/shard_map/ppermute | solution.py:166
  18.9 1.2 %collective-permute-start.9 = (bf16[16,512]{1,0:T(8,128)(2,1)S(1)}, bf16[16,512]{1,0:T(8,128)(2,1)S(1)}, u32[]{:S(2)}, u32[]{:S(2)}) collective-permute-start(bf16[16,512]{1,0:T(8,128)(2,1)S(1)} %collective-permute-done.7.refs_1_), channel_id=1, source_target_pairs={{0,1},{1,0},{2,3},{3,2},{4,5},{5,4},{6,7},{7,6},{8,9},{9,8},{10,11... | collective-permute-start | bytes 49160 | tf_op jit(solution)/shard_map/ppermute | solution.py:166

commit v5 on v4

--- a/solution.py
+++ b/solution.py
@@ -108,20 +108,18 @@
     out_ref[...] = total.astype(BF16)
 
 
-def finish_kernel(weight_ref, *refs, width):
-    *parts, tilde_ref, proj_ref, inter_ref = refs
-    chips = len(parts) // 2
-    mine, got = parts[:chips], parts[chips:]
+def finish_kernel(kept_ref, singular_ref, mine_ref, got_ref, tilde_ref, proj_ref, inter_ref, *, width, chips):
     keep_cols, rows = tilde_ref.shape
     core = lax.axis_index("row") % 2
     chip = lax.axis_index("row") // 2
     upper = is_upper()
-    weight = weight_ref[...]
+    weight = jnp.where(iota((1, keep_cols), 1) < kept_ref[0], 1.0 / jnp.sqrt(singular_ref[...]), 0.0)
     square = (keep_cols, keep_cols)
     diagonal = iota(square, 0) == iota(square, 1)
     weight_rows = jnp.sum(jnp.where(diagonal, weight, 0.0), axis=1, keepdims=True)
-    lower_parts = [jnp.where(upper, got[turn][...], mine[turn][...]) for turn in range(chips)]
-    upper_parts = [jnp.where(upper, mine[turn][...], got[turn][...]) for turn in range(chips)]
+    turns = [pl.ds(turn * keep_cols, keep_cols) for turn in range(chips)]
+    lower_parts = [jnp.where(upper, got_ref[turn], mine_ref[turn]) for turn in turns]
+    upper_parts = [jnp.where(upper, mine_ref[turn], got_ref[turn]) for turn in turns]
     lower_parts = [lower_parts[(away - RESULT_FIRST[0]) % chips] for away in range(chips)]
     upper_parts = [upper_parts[(away - RESULT_FIRST[1]) % chips] for away in range(chips)]
     for whole, ref in ((upper_parts[0], tilde_ref), (lower_parts[0], proj_ref)):
@@ -222,18 +220,17 @@
         name="apply_factor",
     )(*factors, half)
     mine = [to_sector(applied, 1, turn, RESULT_FIRST) for turn in range(chips)]
-    theirs = [other_core(value) for value in mine]
-
-    columns = jnp.arange(keep_cols, dtype=jnp.int32)
-    weight = jnp.where(columns < kept[0], 1.0 / jnp.sqrt(singular), 0.0)
+    mine = jnp.concatenate(mine, axis=0)
+    theirs = other_core(mine)
+
     tilde, proj, inter = pl.pallas_call(
-        functools.partial(finish_kernel, width=width),
+        functools.partial(finish_kernel, width=width, chips=chips),
         out_shape=(block, block, jax.ShapeDtypeStruct((keep_cols, keep_cols), F32)),
-        in_specs=[in_vmem()] * (2 * chips + 1),
+        in_specs=[pl.BlockSpec(memory_space=pltpu.SMEM)] + [in_vmem()] * 3,
         out_specs=(in_vmem(), in_vmem(), in_vmem()),
         compiler_params=pltpu.CompilerParams(vmem_limit_bytes=MIB),
         name="finish",
-    )(weight, *mine, *theirs)
+    )(kept, singular, mine, theirs)
     return tilde.T[None], proj.T[None], inter[None]
 
 

time: 21.1 us -> 20.8 us (0.986)
  starting transfers between devices: 10.7 us -> 10.4 us
    ppermute x4, waiting for transfers between devices: 3.42 us -> 4.41 us  [to_sector(): return lax.ppermute(value, ('sec', 'row'), pairs)]
    ppermute x6 -> x5, waiting for transfers between devices: 1.17 us -> 0.22 us  [other_core(): return lax.ppermute(value, 'row', [(i, i ^ 1) for i in range(row_devices)])]
    ppermute x6 -> x5, starting transfers between devices: 2.01 us -> 1.74 us  [other_core(): return lax.ppermute(value, 'row', [(i, i ^ 1) for i in range(row_devices)])]
  transfers between devices with their start and end apart: 10 -> 9, of which waited for: 5 -> 5; matrix products, arithmetic and copies ran while one was open for 4% -> 4% of each run, Pallas kernels for 8% -> 8%
where the time goes in v5:
time: 20.8 us; the launch traced here: 20.6 us
  starting transfers between devices  10.4 us (50%)
  waiting for transfers between devices  4.63 us (22%)
  Pallas kernels  2.71 us (13%)
  between operations  2.02 us (10%)
  other arithmetic  0.81 us (4%)
    ppermute x4, starting transfers between devices, to_sector(): return lax.ppermute(value, ('sec', 'row'), pairs)  8.65 us
    ppermute x4, waiting for transfers between devices, to_sector(): return lax.ppermute(value, ('sec', 'row'), pairs)  4.41 us
    ppermute x5, starting transfers between devices, other_core(): return lax.ppermute(value, 'row', [(i, i ^ 1) for i in range(row_devices)])  1.74 us
    pallas_call x1, Pallas kernels, local(): pl.pallas_call(functools.partial(half_kernel, states_here=states_here), o...  1.52 us
    select_n x1, other arithmetic, local(): jnp.where(iota(own_shape, 0) < keep_cols, own, placed(joining_map, keep_c...  0.8 us
    pallas_call x1, Pallas kernels, local(): pl.pallas_call(functools.partial(finish_kernel, width=width, chips=chips)...  0.74 us
  transfers between devices with their start and end apart: 9, of which 5 were waited for; matrix products, arithmetic and copies ran while one was open for 4% of the time, Pallas kernels for 8%

profile of v5, /device:TPU:0, one launch (start us, length us, event | category | flops | bytes accessed | tf_op | source)
XLA Modules:
  0.0 20.6 jit_solution(6794230794938720832)
XLA Ops:
  0.6 0.5 %collective-permute-start = (bf16[16,256]{1,0:T(8,128)(2,1)}, bf16[16,256]{1,0:T(8,128)(2,1)S(1)}, u32[]{:S(2)}, u32[]{:S(2)}) collective-permute-start(bf16[16,256]{1,0:T(8,128)(2,1)} %bitcast.23), channel_id=1, source_target_pairs={{0,1},{1,0},{2,3},{3,2},{4,5},{5,4},{6,7},{7,6},{8,9},{9,8},{10,11... | collective-permute-start | bytes 24584 | tf_op jit(solution)/shard_map/ppermute | solution.py:164
  1.1 0.1 collective-permute-start.1
  1.2 0.8 %convert_select_fusion.own_ref = f32[32,256]{1,0:T(8,128)S(1)} fusion(s32[1,16]{1,0:T(1,128)} %param.19, bf16[16,256]{1,0:T(8,128)(2,1)} %bitcast.26, bf16[16,256]{1,0:T(8,128)(2,1)} %bitcast.24, pred[32]{0:T(512)(128)(4,1)S(1)} %iota_compare_fusion, pred[]{:T(512)S(6)} %eq.3), kind=kLoop, calls=%fused_computation | loop fusion | flops 32768 | bytes 49249 | tf_op jit(solution)/shard_map/jit(_where)/select_n | solution.py:187
  2.0 0.0 copy-start
  2.0 0.0 copy-start.1
  2.0 0.0 copy-start.2
  2.0 0.0 copy-start.3
  2.1 0.5 %collective-permute-start.4 = (bf16[256,1024]{1,0:T(8,128)(2,1)}, bf16[256,1024]{1,0:T(8,128)(2,1)S(1)}, u32[]{:S(2)}, u32[]{:S(2)}) collective-permute-start(bf16[256,1024]{1,0:T(8,128)(2,1)} %bitcast.19), channel_id=1, source_target_pairs={{0,1},{1,0},{2,3},{3,2},{4,5},{5,4},{6,7},{7,6},{8,9},{9,8},{10,11... | collective-permute-start | bytes 1572872 | tf_op jit(solution)/shard_map/ppermute | solution.py:164
  2.6 0.1 collective-permute-start.5
  2.6 0.0 collective-permute-done.u_got_ref
  2.6 0.0 collective-permute-done.1.v_got_ref
  2.6 0.2 %join_factor.1 = bf16[16,512]{1,0:T(8,128)(2,1)S(1)} custom-call(f32[32,256]{1,0:T(8,128)S(1)} %convert_select_fusion.own_ref, bf16[16,256]{1,0:T(8,128)(2,1)S(1)} %collective-permute-done.u_got_ref, bf16[16,256]{1,0:T(8,128)(2,1)S(1)} %collective-permute-done.1.v_got_ref), custom_call_target="tpu_custom_call" | custom-call | flops 10000000000 | tf_op jit(solution)/shard_map/join_factor/pallas_call | solution.py:188
  2.9 3.9 %collective-permute-start.2 = (bf16[16,512]{1,0:T(8,128)(2,1)S(1)}, bf16[16,512]{1,0:T(8,128)(2,1)S(1)}, u32[]{:S(2)}, u32[]{:S(2)}) collective-permute-start(bf16[16,512]{1,0:T(8,128)(2,1)S(1)} %join_factor.1), channel_id=1, source_target_pairs={{0,6},{1,31},{2,4},{3,29},{4,10},{5,3},{6,8},{7,1},{8,14},{9,7},{1... | collective-permute-start | bytes 49160 | tf_op jit(solution)/shard_map/ppermute | solution.py:173
  6.7 1.5 %collective-permute-start.3 = (bf16[16,512]{1,0:T(8,128)(2,1)S(1)}, bf16[16,512]{1,0:T(8,128)(2,1)S(1)}, u32[]{:S(2)}, u32[]{:S(2)}) collective-permute-start(bf16[16,512]{1,0:T(8,128)(2,1)S(1)} %join_factor.1), channel_id=1, source_target_pairs={{0,4},{1,29},{2,6},{3,31},{4,8},{5,1},{6,10},{7,3},{8,12},{9,5},{1... | collective-permute-start | bytes 49160 | tf_op jit(solution)/shard_map/ppermute | solution.py:173
  8.9 0.0 collective-permute-done.4.ul_got
  8.9 0.0 collective-permute-done.5.dl_got
  9.0 0.0 copy-done
  9.0 0.0 copy-done.1
  9.0 0.0 copy-done.2
  9.0 0.0 copy-done.3
  9.0 0.0 copy-start.4
  9.0 1.5 %half_product.1.refs_2_ = bf16[1024,512]{1,0:T(8,128)(2,1)S(1)} custom-call(s32[1]{0:T(128)S(6)} %copy.14.states_ref, bf16[256,1024]{1,0:T(8,128)(2,1)S(1)} %bitcast.20, bf16[256,1024]{1,0:T(8,128)(2,1)S(1)} %collective-permute-done.4.ul_got, bf16[1024,1024]{1,0:T(8,128)(2,1)S(1)} %bitcast.17, bf16[256,1024]{1,0:T(8,128)(2,1)S(1)} %bitcast.22, ...), custom_call_target="tpu_custom_call" | custom-call | flops 262144 | bytes 256 | tf_op jit(solution)/shard_map/half_product/pallas_call | solution.py:202
  10.5 1.0 %collective-permute-done.2.refs_0_ = bf16[16,512]{1,0:T(8,128)(2,1)S(1)} collective-permute-done((bf16[16,512]{1,0:T(8,128)(2,1)S(1)}, bf16[16,512]{1,0:T(8,128)(2,1)S(1)}, u32[]{:S(2)}, u32[]{:S(2)}) %collective-permute-start.2) | collective-permute-done | bytes 16416 | tf_op jit(solution)/shard_map/ppermute | solution.py:173
  11.5 1.7 %collective-permute-done.3.refs_1_ = bf16[16,512]{1,0:T(8,128)(2,1)S(1)} collective-permute-done((bf16[16,512]{1,0:T(8,128)(2,1)S(1)}, bf16[16,512]{1,0:T(8,128)(2,1)S(1)}, u32[]{:S(2)}, u32[]{:S(2)}) %collective-permute-start.3) | collective-permute-done | bytes 16416 | tf_op jit(solution)/shard_map/ppermute | solution.py:173
  13.2 0.2 %apply_factor.1 = bf16[16,512]{1,0:T(8,128)(2,1)S(1)} custom-call(bf16[16,512]{1,0:T(8,128)(2,1)S(1)} %collective-permute-done.2.refs_0_, bf16[16,512]{1,0:T(8,128)(2,1)S(1)} %collective-permute-done.3.refs_1_, bf16[1024,512]{1,0:T(8,128)(2,1)S(1)} %half_product.1.refs_2_), custom_call_target="tpu_custom_call" | custom-call | tf_op jit(solution)/shard_map/apply_factor/pallas_call | solution.py:214
  13.4 1.3 %collective-permute-start.6 = (bf16[16,512]{1,0:T(8,128)(2,1)S(1)}, bf16[16,512]{1,0:T(8,128)(2,1)S(1)}, u32[]{:S(2)}, u32[]{:S(2)}) collective-permute-start(bf16[16,512]{1,0:T(8,128)(2,1)S(1)} %apply_factor.1), channel_id=1, source_target_pairs={{0,30},{1,7},{2,28},{3,5},{4,2},{5,11},{6,0},{7,9},{8,6},{9,15},{1... | collective-permute-start | bytes 49160 | tf_op jit(solution)/shard_map/ppermute | solution.py:173
  14.7 2.0 %collective-permute-start.7 = (bf16[16,512]{1,0:T(8,128)(2,1)S(1)}, bf16[16,512]{1,0:T(8,128)(2,1)S(1)}, u32[]{:S(2)}, u32[]{:S(2)}) collective-permute-start(bf16[16,512]{1,0:T(8,128)(2,1)S(1)} %apply_factor.1), channel_id=1, source_target_pairs={{0,28},{1,5},{2,30},{3,7},{4,0},{5,9},{6,2},{7,11},{8,4},{9,13},{1... | collective-permute-start | bytes 49160 | tf_op jit(solution)/shard_map/ppermute | solution.py:173
  16.6 1.4 %collective-permute-done.6 = bf16[16,512]{1,0:T(8,128)(2,1)S(1)} collective-permute-done((bf16[16,512]{1,0:T(8,128)(2,1)S(1)}, bf16[16,512]{1,0:T(8,128)(2,1)S(1)}, u32[]{:S(2)}, u32[]{:S(2)}) %collective-permute-start.6) | collective-permute-done | bytes 16416 | tf_op jit(solution)/shard_map/ppermute | solution.py:173
  18.1 0.3 %collective-permute-done.7 = bf16[16,512]{1,0:T(8,128)(2,1)S(1)} collective-permute-done((bf16[16,512]{1,0:T(8,128)(2,1)S(1)}, bf16[16,512]{1,0:T(8,128)(2,1)S(1)}, u32[]{:S(2)}, u32[]{:S(2)}) %collective-permute-start.7) | collective-permute-done | bytes 16416 | tf_op jit(solution)/shard_map/ppermute | solution.py:173
  18.4 0.6 %collective-permute-start.8 = (bf16[32,512]{1,0:T(8,128)(2,1)S(1)}, bf16[32,512]{1,0:T(8,128)(2,1)S(1)}, u32[]{:S(2)}, u32[]{:S(2)}) collective-permute-start(bf16[32,512]{1,0:T(8,128)(2,1)S(1)} %constant_dynamic-update-slice_fusion.mine_ref), channel_id=1, source_target_pairs={{0,1},{1,0},{2,3},{3,2},{4,5},{5,4},{6,7},{7,6},{8,9},{9,8},{10,11... | collective-permute-start | bytes 98312 | tf_op jit(solution)/shard_map/ppermute | solution.py:164
  19.6 0.2 %collective-permute-done.8.got_ref = bf16[32,512]{1,0:T(8,128)(2,1)S(1)} collective-permute-done((bf16[32,512]{1,0:T(8,128)(2,1)S(1)}, bf16[32,512]{1,0:T(8,128)(2,1)S(1)}, u32[]{:S(2)}, u32[]{:S(2)}) %collective-permute-start.8) | collective-permute-done | bytes 32800 | tf_op jit(solution)/shard_map/ppermute | solution.py:164
  19.8 0.0 copy-done.4
  19.8 0.7 %finish.1 = (bf16[16,256]{1,0:T(8,128)(2,1)}, bf16[16,256]{1,0:T(8,128)(2,1)}, f32[16,16]{1,0:T(8,128)}) custom-call(s32[1]{0:T(128)S(6)} %copy.15.kept_ref, f32[1,16]{1,0:T(1,128)S(1)} %copy-done.4, bf16[32,512]{1,0:T(8,128)(2,1)S(1)} %constant_dynamic-update-slice_fusion.mine_ref, bf16[32,512]{1,0:T(8,128)(2,1)S(1)} %collective-permute-done.8.got_ref), custom_call_target="tpu_custom_call" | custom-call | tf_op jit(solution)/shard_map/finish/pallas_call | solution.py:226
  (3 shorter events, 0.0 us)
Async XLA Ops:
  0.6 2.0 %collective-permute-start = (bf16[16,256]{1,0:T(8,128)(2,1)}, bf16[16,256]{1,0:T(8,128)(2,1)S(1)}, u32[]{:S(2)}, u32[]{:S(2)}) collective-permute-start(bf16[16,256]{1,0:T(8,128)(2,1)} %bitcast.23), channel_id=1, source_target_pairs={{0,1},{1,0},{2,3},{3,2},{4,5},{5,4},{6,7},{7,6},{8,9},{9,8},{10,11... | collective-permute-start | bytes 24584 | tf_op jit(solution)/shard_map/ppermute | solution.py:164
  1.1 1.5 %collective-permute-start.1 = (bf16[16,256]{1,0:T(8,128)(2,1)}, bf16[16,256]{1,0:T(8,128)(2,1)S(1)}, u32[]{:S(2)}, u32[]{:S(2)}) collective-permute-start(bf16[16,256]{1,0:T(8,128)(2,1)} %bitcast.25), channel_id=1, source_target_pairs={{0,1},{1,0},{2,3},{3,2},{4,5},{5,4},{6,7},{7,6},{8,9},{9,8},{10,11... | collective-permute-start | bytes 24584 | tf_op jit(solution)/shard_map/ppermute | solution.py:164
  2.0 6.9 %copy-start = (bf16[1,1024,1024]{2,1,0:T(8,128)(2,1)S(1)}, bf16[1,1024,1024]{2,1,0:T(8,128)(2,1)}, u32[]{:S(2)}) copy-start(bf16[1,1024,1024]{2,1,0:T(8,128)(2,1)} %param.11) | copy-start | bytes 6291460
  2.0 6.9 %copy-start.1 = (bf16[1,1024,1024]{2,1,0:T(8,128)(2,1)S(1)}, bf16[1,1024,1024]{2,1,0:T(8,128)(2,1)}, u32[]{:S(2)}) copy-start(bf16[1,1024,1024]{2,1,0:T(8,128)(2,1)} %param.13) | copy-start | bytes 6291460
  2.0 6.9 %copy-start.2 = (bf16[1,256,1024]{2,1,0:T(8,128)(2,1)S(1)}, bf16[1,256,1024]{2,1,0:T(8,128)(2,1)}, u32[]{:S(2)}) copy-start(bf16[1,256,1024]{2,1,0:T(8,128)(2,1)} %param.10) | copy-start | bytes 1572868
  2.0 6.9 %copy-start.3 = (bf16[1,256,1024]{2,1,0:T(8,128)(2,1)S(1)}, bf16[1,256,1024]{2,1,0:T(8,128)(2,1)}, u32[]{:S(2)}) copy-start(bf16[1,256,1024]{2,1,0:T(8,128)(2,1)} %param.12) | copy-start | bytes 1572868
  2.1 6.9 %collective-permute-start.4 = (bf16[256,1024]{1,0:T(8,128)(2,1)}, bf16[256,1024]{1,0:T(8,128)(2,1)S(1)}, u32[]{:S(2)}, u32[]{:S(2)}) collective-permute-start(bf16[256,1024]{1,0:T(8,128)(2,1)} %bitcast.19), channel_id=1, source_target_pairs={{0,1},{1,0},{2,3},{3,2},{4,5},{5,4},{6,7},{7,6},{8,9},{9,8},{10,11... | collective-permute-start | bytes 1572872 | tf_op jit(solution)/shard_map/ppermute | solution.py:164
  2.6 6.4 %collective-permute-start.5 = (bf16[256,1024]{1,0:T(8,128)(2,1)}, bf16[256,1024]{1,0:T(8,128)(2,1)S(1)}, u32[]{:S(2)}, u32[]{:S(2)}) collective-permute-start(bf16[256,1024]{1,0:T(8,128)(2,1)} %bitcast.21), channel_id=1, source_target_pairs={{0,1},{1,0},{2,3},{3,2},{4,5},{5,4},{6,7},{7,6},{8,9},{9,8},{10,11... | collective-permute-start | bytes 1572872 | tf_op jit(solution)/shard_map/ppermute | solution.py:164
  2.9 8.6 %collective-permute-start.2 = (bf16[16,512]{1,0:T(8,128)(2,1)S(1)}, bf16[16,512]{1,0:T(8,128)(2,1)S(1)}, u32[]{:S(2)}, u32[]{:S(2)}) collective-permute-start(bf16[16,512]{1,0:T(8,128)(2,1)S(1)} %join_factor.1), channel_id=1, source_target_pairs={{0,6},{1,31},{2,4},{3,29},{4,10},{5,3},{6,8},{7,1},{8,14},{9,7},{1... | collective-permute-start | bytes 49160 | tf_op jit(solution)/shard_map/ppermute | solution.py:173
  6.7 6.4 %collective-permute-start.3 = (bf16[16,512]{1,0:T(8,128)(2,1)S(1)}, bf16[16,512]{1,0:T(8,128)(2,1)S(1)}, u32[]{:S(2)}, u32[]{:S(2)}) collective-permute-start(bf16[16,512]{1,0:T(8,128)(2,1)S(1)} %join_factor.1), channel_id=1, source_target_pairs={{0,4},{1,29},{2,6},{3,31},{4,8},{5,1},{6,10},{7,3},{8,12},{9,5},{1... | collective-permute-start | bytes 49160 | tf_op jit(solution)/shard_map/ppermute | solution.py:173
  9.0 10.8 %copy-start.4 = (f32[1,16]{1,0:T(1,128)S(1)}, f32[1,16]{1,0:T(1,128)}, u32[]{:S(2)}) copy-start(f32[1,16]{1,0:T(1,128)} %singular_ref.1) | copy-start | bytes 196
  13.4 4.7 %collective-permute-start.6 = (bf16[16,512]{1,0:T(8,128)(2,1)S(1)}, bf16[16,512]{1,0:T(8,128)(2,1)S(1)}, u32[]{:S(2)}, u32[]{:S(2)}) collective-permute-start(bf16[16,512]{1,0:T(8,128)(2,1)S(1)} %apply_factor.1), channel_id=1, source_target_pairs={{0,30},{1,7},{2,28},{3,5},{4,2},{5,11},{6,0},{7,9},{8,6},{9,15},{1... | collective-permute-start | bytes 49160 | tf_op jit(solution)/shard_map/ppermute | solution.py:173
  14.7 3.7 %collective-permute-start.7 = (bf16[16,512]{1,0:T(8,128)(2,1)S(1)}, bf16[16,512]{1,0:T(8,128)(2,1)S(1)}, u32[]{:S(2)}, u32[]{:S(2)}) collective-permute-start(bf16[16,512]{1,0:T(8,128)(2,1)S(1)} %apply_factor.1), channel_id=1, source_target_pairs={{0,28},{1,5},{2,30},{3,7},{4,0},{5,9},{6,2},{7,11},{8,4},{9,13},{1... | collective-permute-start | bytes 49160 | tf_op jit(solution)/shard_map/ppermute | solution.py:173
  18.4 1.4 %collective-permute-start.8 = (bf16[32,512]{1,0:T(8,128)(2,1)S(1)}, bf16[32,512]{1,0:T(8,128)(2,1)S(1)}, u32[]{:S(2)}, u32[]{:S(2)}) collective-permute-start(bf16[32,512]{1,0:T(8,128)(2,1)S(1)} %constant_dynamic-update-slice_fusion.mine_ref), channel_id=1, source_target_pairs={{0,1},{1,0},{2,3},{3,2},{4,5},{5,4},{6,7},{7,6},{8,9},{9,8},{10,11... | collective-permute-start | bytes 98312 | tf_op jit(solution)/shard_map/ppermute | solution.py:164

commit v6 on v5

--- a/solution.py
+++ b/solution.py
@@ -10,6 +10,7 @@
 LANES = 128
 F32, BF16 = jnp.float32, jnp.bfloat16
 MIB = 1024 * 1024
+START_FLOPS = 2 * 10**9
 JOIN_FLOPS = 10**10
 FACTOR_FIRST = (1, 1)
 RESULT_FIRST = (1, 1)
@@ -23,22 +24,31 @@
     return lax.axis_index("row") & 1 == 1
 
 
-def join_kernel(own_ref, u_got_ref, v_got_ref, out_ref, *, states_here):
+def start_kernel(out_ref):
+    out_ref[...] = jnp.zeros(out_ref.shape, F32)
+
+
+def own_kernel(after_ref, map_ref, u_ref, v_ref, own_ref, mover_ref):
+    states_here = map_ref.shape[1]
+    own_ref[...] = jnp.where(is_upper(), u_ref[...], v_ref[...])
+    small = (states_here, states_here)
+    entries = jnp.where(iota(small, 0) == iota(small, 1), map_ref[...].astype(F32), 0.0)
+    entries = jnp.sum(entries, axis=1, keepdims=True).astype(jnp.int32)
+    entries = jnp.broadcast_to(entries, (states_here, LANES))
+    square = (LANES, LANES)
+    wanted = jnp.concatenate([entries] * (LANES // states_here), axis=0) + iota(square, 0) // states_here * states_here
+    mover_ref[...] = jnp.where(iota(square, 1) == wanted, 1.0, 0.0).astype(BF16)
+
+
+def join_kernel(own_ref, mover_ref, u_got_ref, v_got_ref, out_ref):
     keep_cols, rows = u_got_ref.shape
     upper = is_upper()
-    own = own_ref[:keep_cols, :rows].astype(BF16)
+    own = own_ref[...]
     got = jnp.where(upper, u_got_ref[...], v_got_ref[...])
     both = jnp.concatenate([jnp.where(upper, got, own), jnp.where(upper, own, got)], axis=1)
-    shape = (states_here, LANES)
-    order = jnp.broadcast_to(own_ref[keep_cols : keep_cols + 1, :LANES], shape)
-    order = jnp.sum(jnp.where(iota(shape, 0) == iota(shape, 1), order, 0.0), axis=1, keepdims=True)
-    order = jnp.broadcast_to(order, shape).astype(jnp.int32)
-    square = (LANES, LANES)
-    wanted = jnp.concatenate([order] * (LANES // states_here), axis=0) + iota(square, 0) // states_here * states_here
-    mover = jnp.where(iota(square, 1) == wanted, 1.0, 0.0).astype(BF16)
     starts = range(0, 2 * rows, LANES)
     stacked = jnp.concatenate([both[:, start : start + LANES] for start in starts], axis=0)
-    moved = jnp.dot(stacked, mover, preferred_element_type=F32).astype(BF16)
+    moved = jnp.dot(stacked, mover_ref[...], preferred_element_type=F32).astype(BF16)
     for i, start in enumerate(starts):
         out_ref[:, start : start + LANES] = moved[i * keep_cols : (i + 1) * keep_cols]
 
@@ -176,29 +186,36 @@
     whole = jax.ShapeDtypeStruct((keep_cols, 2 * rows), BF16)
     u, v = left_factor[0].T, right_factor[0].T
     u_got, v_got = other_core(u), other_core(v)
-    own_shape = (2 * keep_cols, max(rows, LANES))
-
-    def placed(value, row):
-        height, across = value.shape
-        spare = (row, own_shape[0] - row - height, 0), (0, own_shape[1] - across, 0)
-        return lax.pad(value, jnp.zeros((), value.dtype), spare)
-
-    own = jnp.where(is_upper(), placed(u, 0), placed(v, 0)).astype(F32)
-    own = jnp.where(iota(own_shape, 0) < keep_cols, own, placed(joining_map, keep_cols).astype(F32))
+    waited = pl.pallas_call(
+        start_kernel,
+        out_shape=jax.ShapeDtypeStruct((8, LANES), F32),
+        in_specs=[],
+        out_specs=in_vmem(),
+        compiler_params=pltpu.CompilerParams(vmem_limit_bytes=MIB),
+        cost_estimate=pl.CostEstimate(flops=START_FLOPS, bytes_accessed=0, transcendentals=0),
+        name="start",
+    )()
+    own, mover = pl.pallas_call(
+        own_kernel,
+        out_shape=(block, jax.ShapeDtypeStruct((LANES, LANES), BF16)),
+        in_specs=[in_vmem()] * 4,
+        out_specs=(in_vmem(), in_vmem()),
+        compiler_params=pltpu.CompilerParams(vmem_limit_bytes=MIB),
+        name="own_factor",
+    )(waited, joining_map, u, v)
     joined = pl.pallas_call(
-        functools.partial(join_kernel, states_here=states_here),
+        join_kernel,
         out_shape=whole,
-        in_specs=[in_vmem()] * 3,
+        in_specs=[in_vmem()] * 4,
         out_specs=in_vmem(),
         compiler_params=pltpu.CompilerParams(vmem_limit_bytes=MIB),
         cost_estimate=pl.CostEstimate(flops=JOIN_FLOPS, bytes_accessed=0, transcendentals=0),
         name="join_factor",
-    )(own, u_got, v_got)
+    )(own, mover, u_got, v_got)
     factors = [to_sector(joined, -1, turn, FACTOR_FIRST) for turn in range(chips)]
 
     ul, dl = corner_ul[0], corner_dl[0]
-    ul_later, dl_later, _ = lax.optimization_barrier((ul, dl, own))
-    ul_got, dl_got = other_core(ul_later), other_core(dl_later)
+    ul_got, dl_got = other_core(ul), other_core(dl)
     half = pl.pallas_call(
         functools.partial(half_kernel, states_here=states_here),
         out_shape=jax.ShapeDtypeStruct((width, 2 * rows), BF16),

time: 20.8 us -> 20.6 us (level)
  other arithmetic: 0.81 us -> 0 us
  local copies, waits for them, and re-layouts: 0.03 us -> 0.65 us
    select_n x1 -> x0, other arithmetic: 0.8 us -> none  [local(): jnp.where(iota(own_shape, 0) < keep_cols, own, placed(joining_map, keep_c...]
    unnamed x11 -> x17, local copies, waits for them, and re-layouts: 0.03 us -> 0.65 us
    ppermute x4, starting transfers between devices: 8.65 us -> 8.38 us  [to_sector(): return lax.ppermute(value, ('sec', 'row'), pairs)]
  transfers between devices with their start and end apart: 9 -> 9, of which waited for: 5 -> 5; matrix products, arithmetic and copies ran while one was open for 4% -> 0% of each run, Pallas kernels for 8% -> 9%
where the time goes in v6:
time: 20.6 us; the launch traced here: 20.4 us
  starting transfers between devices  10.2 us (50%)
  waiting for transfers between devices  4.83 us (23%)
  Pallas kernels  2.73 us (13%)
  between operations  2.02 us (10%)
  local copies, waits for them, and re-layouts  0.65 us (3%)
    ppermute x4, starting transfers between devices, to_sector(): return lax.ppermute(value, ('sec', 'row'), pairs)  8.38 us
    ppermute x4, waiting for transfers between devices, to_sector(): return lax.ppermute(value, ('sec', 'row'), pairs)  4.56 us
    ppermute x5, starting transfers between devices, other_core(): return lax.ppermute(value, 'row', [(i, i ^ 1) for i in range(row_devices)])  1.79 us
    pallas_call x1, Pallas kernels, local(): pl.pallas_call(functools.partial(half_kernel, states_here=states_here), o...  1.53 us
    pallas_call x1, Pallas kernels, local(): pl.pallas_call(functools.partial(finish_kernel, width=width, chips=chips)...  0.74 us
    unnamed x17, local copies, waits for them, and re-layouts  0.65 us
  transfers between devices with their start and end apart: 9, of which 5 were waited for; matrix products, arithmetic and copies ran while one was open for 0% of the time, Pallas kernels for 9%

profile of v6, /device:TPU:0, one launch (start us, length us, event | category | flops | bytes accessed | tf_op | source)
XLA Modules:
  0.0 20.4 jit_solution(14270215772963311116)
XLA Ops:
  0.6 0.5 %collective-permute-start = (bf16[16,256]{1,0:T(8,128)(2,1)}, bf16[16,256]{1,0:T(8,128)(2,1)S(1)}, u32[]{:S(2)}, u32[]{:S(2)}) collective-permute-start(bf16[16,256]{1,0:T(8,128)(2,1)} %bitcast.23), channel_id=1, source_target_pairs={{0,1},{1,0},{2,3},{3,2},{4,5},{5,4},{6,7},{7,6},{8,9},{9,8},{10,11... | collective-permute-start | bytes 24584 | tf_op jit(solution)/shard_map/ppermute | solution.py:174
  1.1 0.1 collective-permute-start.1
  1.2 0.4 %collective-permute-start.4 = (bf16[256,1024]{1,0:T(8,128)(2,1)}, bf16[256,1024]{1,0:T(8,128)(2,1)S(1)}, u32[]{:S(2)}, u32[]{:S(2)}) collective-permute-start(bf16[256,1024]{1,0:T(8,128)(2,1)} %bitcast.19), channel_id=1, source_target_pairs={{0,1},{1,0},{2,3},{3,2},{4,5},{5,4},{6,7},{7,6},{8,9},{9,8},{10,11... | collective-permute-start | bytes 1572872 | tf_op jit(solution)/shard_map/ppermute | solution.py:174
  1.7 0.0 copy-start.4
  1.7 0.0 copy-start.5
  1.7 0.0 copy-start.7
  1.7 0.1 collective-permute-start.5
  1.8 0.6 %copy-done.4 = bf16[1,256,16]{1,2,0:T(8,128)(2,1)S(1)} copy-done((bf16[1,256,16]{1,2,0:T(8,128)(2,1)S(1)}, bf16[1,256,16]{1,2,0:T(8,128)(2,1)}, u32[]{:S(2)}) %copy-start.4) | copy-done | bytes 8216
  2.4 0.0 copy-done.5
  2.4 0.0 copy-done.7
  2.4 0.1 own_factor.1
  2.5 0.0 collective-permute-done.u_got_ref
  2.5 0.1 collective-permute-done.1.v_got_ref
  2.5 0.0 copy-start
  2.5 0.0 copy-start.1
  2.5 0.0 copy-start.2
  2.5 0.0 copy-start.3
  2.5 0.1 join_factor.1
  2.7 3.6 %collective-permute-start.2 = (bf16[16,512]{1,0:T(8,128)(2,1)S(1)}, bf16[16,512]{1,0:T(8,128)(2,1)S(1)}, u32[]{:S(2)}, u32[]{:S(2)}) collective-permute-start(bf16[16,512]{1,0:T(8,128)(2,1)S(1)} %join_factor.1), channel_id=1, source_target_pairs={{0,6},{1,31},{2,4},{3,29},{4,10},{5,3},{6,8},{7,1},{8,14},{9,7},{1... | collective-permute-start | bytes 49160 | tf_op jit(solution)/shard_map/ppermute | solution.py:183
  6.3 1.5 %collective-permute-start.3 = (bf16[16,512]{1,0:T(8,128)(2,1)S(1)}, bf16[16,512]{1,0:T(8,128)(2,1)S(1)}, u32[]{:S(2)}, u32[]{:S(2)}) collective-permute-start(bf16[16,512]{1,0:T(8,128)(2,1)S(1)} %join_factor.1), channel_id=1, source_target_pairs={{0,4},{1,29},{2,6},{3,31},{4,8},{5,1},{6,10},{7,3},{8,12},{9,5},{1... | collective-permute-start | bytes 49160 | tf_op jit(solution)/shard_map/ppermute | solution.py:183
  8.5 0.0 collective-permute-done.4.ul_got
  8.5 0.0 collective-permute-done.5.dl_got
  8.5 0.0 copy-done
  8.5 0.0 copy-done.1
  8.5 0.0 copy-done.2
  8.5 0.0 copy-done.3
  8.5 0.0 copy-start.6
  8.6 1.5 %half_product.1.refs_2_ = bf16[1024,512]{1,0:T(8,128)(2,1)S(1)} custom-call(s32[1]{0:T(128)S(6)} %copy.14.states_ref, bf16[256,1024]{1,0:T(8,128)(2,1)S(1)} %bitcast.20, bf16[256,1024]{1,0:T(8,128)(2,1)S(1)} %collective-permute-done.4.ul_got, bf16[1024,1024]{1,0:T(8,128)(2,1)S(1)} %bitcast.17, bf16[256,1024]{1,0:T(8,128)(2,1)S(1)} %bitcast.22, ...), custom_call_target="tpu_custom_call" | custom-call | flops 262144 | bytes 256 | tf_op jit(solution)/shard_map/half_product/pallas_call | solution.py:219
  10.1 0.9 %collective-permute-done.2.refs_0_ = bf16[16,512]{1,0:T(8,128)(2,1)S(1)} collective-permute-done((bf16[16,512]{1,0:T(8,128)(2,1)S(1)}, bf16[16,512]{1,0:T(8,128)(2,1)S(1)}, u32[]{:S(2)}, u32[]{:S(2)}) %collective-permute-start.2) | collective-permute-done | bytes 16416 | tf_op jit(solution)/shard_map/ppermute | solution.py:183
  11.0 1.7 %collective-permute-done.3.refs_1_ = bf16[16,512]{1,0:T(8,128)(2,1)S(1)} collective-permute-done((bf16[16,512]{1,0:T(8,128)(2,1)S(1)}, bf16[16,512]{1,0:T(8,128)(2,1)S(1)}, u32[]{:S(2)}, u32[]{:S(2)}) %collective-permute-start.3) | collective-permute-done | bytes 16416 | tf_op jit(solution)/shard_map/ppermute | solution.py:183
  12.7 0.2 %apply_factor.1 = bf16[16,512]{1,0:T(8,128)(2,1)S(1)} custom-call(bf16[16,512]{1,0:T(8,128)(2,1)S(1)} %collective-permute-done.2.refs_0_, bf16[16,512]{1,0:T(8,128)(2,1)S(1)} %collective-permute-done.3.refs_1_, bf16[1024,512]{1,0:T(8,128)(2,1)S(1)} %half_product.1.refs_2_), custom_call_target="tpu_custom_call" | custom-call | tf_op jit(solution)/shard_map/apply_factor/pallas_call | solution.py:231
  13.0 1.3 %collective-permute-start.6 = (bf16[16,512]{1,0:T(8,128)(2,1)S(1)}, bf16[16,512]{1,0:T(8,128)(2,1)S(1)}, u32[]{:S(2)}, u32[]{:S(2)}) collective-permute-start(bf16[16,512]{1,0:T(8,128)(2,1)S(1)} %apply_factor.1), channel_id=1, source_target_pairs={{0,30},{1,7},{2,28},{3,5},{4,2},{5,11},{6,0},{7,9},{8,6},{9,15},{1... | collective-permute-start | bytes 49160 | tf_op jit(solution)/shard_map/ppermute | solution.py:183
  14.2 2.0 %collective-permute-start.7 = (bf16[16,512]{1,0:T(8,128)(2,1)S(1)}, bf16[16,512]{1,0:T(8,128)(2,1)S(1)}, u32[]{:S(2)}, u32[]{:S(2)}) collective-permute-start(bf16[16,512]{1,0:T(8,128)(2,1)S(1)} %apply_factor.1), channel_id=1, source_target_pairs={{0,28},{1,5},{2,30},{3,7},{4,0},{5,9},{6,2},{7,11},{8,4},{9,13},{1... | collective-permute-start | bytes 49160 | tf_op jit(solution)/shard_map/ppermute | solution.py:183
  16.2 1.4 %collective-permute-done.6 = bf16[16,512]{1,0:T(8,128)(2,1)S(1)} collective-permute-done((bf16[16,512]{1,0:T(8,128)(2,1)S(1)}, bf16[16,512]{1,0:T(8,128)(2,1)S(1)}, u32[]{:S(2)}, u32[]{:S(2)}) %collective-permute-start.6) | collective-permute-done | bytes 16416 | tf_op jit(solution)/shard_map/ppermute | solution.py:183
  17.6 0.5 %collective-permute-done.7 = bf16[16,512]{1,0:T(8,128)(2,1)S(1)} collective-permute-done((bf16[16,512]{1,0:T(8,128)(2,1)S(1)}, bf16[16,512]{1,0:T(8,128)(2,1)S(1)}, u32[]{:S(2)}, u32[]{:S(2)}) %collective-permute-start.7) | collective-permute-done | bytes 16416 | tf_op jit(solution)/shard_map/ppermute | solution.py:183
  18.1 0.7 %collective-permute-start.8 = (bf16[32,512]{1,0:T(8,128)(2,1)S(1)}, bf16[32,512]{1,0:T(8,128)(2,1)S(1)}, u32[]{:S(2)}, u32[]{:S(2)}) collective-permute-start(bf16[32,512]{1,0:T(8,128)(2,1)S(1)} %constant_dynamic-update-slice_fusion.mine_ref), channel_id=1, source_target_pairs={{0,1},{1,0},{2,3},{3,2},{4,5},{5,4},{6,7},{7,6},{8,9},{9,8},{10,11... | collective-permute-start | bytes 98312 | tf_op jit(solution)/shard_map/ppermute | solution.py:174
  19.4 0.2 %collective-permute-done.8.got_ref = bf16[32,512]{1,0:T(8,128)(2,1)S(1)} collective-permute-done((bf16[32,512]{1,0:T(8,128)(2,1)S(1)}, bf16[32,512]{1,0:T(8,128)(2,1)S(1)}, u32[]{:S(2)}, u32[]{:S(2)}) %collective-permute-start.8) | collective-permute-done | bytes 32800 | tf_op jit(solution)/shard_map/ppermute | solution.py:174
  19.7 0.0 copy-done.6
  19.7 0.7 %finish.1 = (bf16[16,256]{1,0:T(8,128)(2,1)}, bf16[16,256]{1,0:T(8,128)(2,1)}, f32[16,16]{1,0:T(8,128)}) custom-call(s32[1]{0:T(128)S(6)} %copy.15.kept_ref, f32[1,16]{1,0:T(1,128)S(1)} %copy-done.6, bf16[32,512]{1,0:T(8,128)(2,1)S(1)} %constant_dynamic-update-slice_fusion.mine_ref, bf16[32,512]{1,0:T(8,128)(2,1)S(1)} %collective-permute-done.8.got_ref), custom_call_target="tpu_custom_call" | custom-call | tf_op jit(solution)/shard_map/finish/pallas_call | solution.py:243
  (3 shorter events, 0.0 us)
Async XLA Ops:
  0.6 1.8 %collective-permute-start = (bf16[16,256]{1,0:T(8,128)(2,1)}, bf16[16,256]{1,0:T(8,128)(2,1)S(1)}, u32[]{:S(2)}, u32[]{:S(2)}) collective-permute-start(bf16[16,256]{1,0:T(8,128)(2,1)} %bitcast.23), channel_id=1, source_target_pairs={{0,1},{1,0},{2,3},{3,2},{4,5},{5,4},{6,7},{7,6},{8,9},{9,8},{10,11... | collective-permute-start | bytes 24584 | tf_op jit(solution)/shard_map/ppermute | solution.py:174
  1.1 1.4 %collective-permute-start.1 = (bf16[16,256]{1,0:T(8,128)(2,1)}, bf16[16,256]{1,0:T(8,128)(2,1)S(1)}, u32[]{:S(2)}, u32[]{:S(2)}) collective-permute-start(bf16[16,256]{1,0:T(8,128)(2,1)} %bitcast.25), channel_id=1, source_target_pairs={{0,1},{1,0},{2,3},{3,2},{4,5},{5,4},{6,7},{7,6},{8,9},{9,8},{10,11... | collective-permute-start | bytes 24584 | tf_op jit(solution)/shard_map/ppermute | solution.py:174
  1.2 7.3 %collective-permute-start.4 = (bf16[256,1024]{1,0:T(8,128)(2,1)}, bf16[256,1024]{1,0:T(8,128)(2,1)S(1)}, u32[]{:S(2)}, u32[]{:S(2)}) collective-permute-start(bf16[256,1024]{1,0:T(8,128)(2,1)} %bitcast.19), channel_id=1, source_target_pairs={{0,1},{1,0},{2,3},{3,2},{4,5},{5,4},{6,7},{7,6},{8,9},{9,8},{10,11... | collective-permute-start | bytes 1572872 | tf_op jit(solution)/shard_map/ppermute | solution.py:174
  1.7 0.7 %copy-start.4 = (bf16[1,256,16]{1,2,0:T(8,128)(2,1)S(1)}, bf16[1,256,16]{1,2,0:T(8,128)(2,1)}, u32[]{:S(2)}) copy-start(bf16[1,256,16]{1,2,0:T(8,128)(2,1)} %param.14) | copy-start | bytes 24580
  1.7 0.7 %copy-start.5 = (bf16[1,256,16]{1,2,0:T(8,128)(2,1)S(1)}, bf16[1,256,16]{1,2,0:T(8,128)(2,1)}, u32[]{:S(2)}) copy-start(bf16[1,256,16]{1,2,0:T(8,128)(2,1)} %param.15) | copy-start | bytes 24580
  1.7 0.7 %copy-start.7 = (s32[1,16]{1,0:T(1,128)S(1)}, s32[1,16]{1,0:T(1,128)}, u32[]{:S(2)}) copy-start(s32[1,16]{1,0:T(1,128)} %map_ref.1) | copy-start | bytes 196
  1.7 6.8 %collective-permute-start.5 = (bf16[256,1024]{1,0:T(8,128)(2,1)}, bf16[256,1024]{1,0:T(8,128)(2,1)S(1)}, u32[]{:S(2)}, u32[]{:S(2)}) collective-permute-start(bf16[256,1024]{1,0:T(8,128)(2,1)} %bitcast.21), channel_id=1, source_target_pairs={{0,1},{1,0},{2,3},{3,2},{4,5},{5,4},{6,7},{7,6},{8,9},{9,8},{10,11... | collective-permute-start | bytes 1572872 | tf_op jit(solution)/shard_map/ppermute | solution.py:174
  2.5 6.0 %copy-start = (bf16[1,1024,1024]{2,1,0:T(8,128)(2,1)S(1)}, bf16[1,1024,1024]{2,1,0:T(8,128)(2,1)}, u32[]{:S(2)}) copy-start(bf16[1,1024,1024]{2,1,0:T(8,128)(2,1)} %param.11) | copy-start | bytes 6291460
  2.5 6.0 %copy-start.1 = (bf16[1,1024,1024]{2,1,0:T(8,128)(2,1)S(1)}, bf16[1,1024,1024]{2,1,0:T(8,128)(2,1)}, u32[]{:S(2)}) copy-start(bf16[1,1024,1024]{2,1,0:T(8,128)(2,1)} %param.13) | copy-start | bytes 6291460
  2.5 6.0 %copy-start.2 = (bf16[1,256,1024]{2,1,0:T(8,128)(2,1)S(1)}, bf16[1,256,1024]{2,1,0:T(8,128)(2,1)}, u32[]{:S(2)}) copy-start(bf16[1,256,1024]{2,1,0:T(8,128)(2,1)} %param.10) | copy-start | bytes 1572868
  2.5 6.0 %copy-start.3 = (bf16[1,256,1024]{2,1,0:T(8,128)(2,1)S(1)}, bf16[1,256,1024]{2,1,0:T(8,128)(2,1)}, u32[]{:S(2)}) copy-start(bf16[1,256,1024]{2,1,0:T(8,128)(2,1)} %param.12) | copy-start | bytes 1572868
  2.7 8.4 %collective-permute-start.2 = (bf16[16,512]{1,0:T(8,128)(2,1)S(1)}, bf16[16,512]{1,0:T(8,128)(2,1)S(1)}, u32[]{:S(2)}, u32[]{:S(2)}) collective-permute-start(bf16[16,512]{1,0:T(8,128)(2,1)S(1)} %join_factor.1), channel_id=1, source_target_pairs={{0,6},{1,31},{2,4},{3,29},{4,10},{5,3},{6,8},{7,1},{8,14},{9,7},{1... | collective-permute-start | bytes 49160 | tf_op jit(solution)/shard_map/ppermute | solution.py:183
  6.3 6.4 %collective-permute-start.3 = (bf16[16,512]{1,0:T(8,128)(2,1)S(1)}, bf16[16,512]{1,0:T(8,128)(2,1)S(1)}, u32[]{:S(2)}, u32[]{:S(2)}) collective-permute-start(bf16[16,512]{1,0:T(8,128)(2,1)S(1)} %join_factor.1), channel_id=1, source_target_pairs={{0,4},{1,29},{2,6},{3,31},{4,8},{5,1},{6,10},{7,3},{8,12},{9,5},{1... | collective-permute-start | bytes 49160 | tf_op jit(solution)/shard_map/ppermute | solution.py:183
  8.5 11.1 %copy-start.6 = (f32[1,16]{1,0:T(1,128)S(1)}, f32[1,16]{1,0:T(1,128)}, u32[]{:S(2)}) copy-start(f32[1,16]{1,0:T(1,128)} %singular_ref.1) | copy-start | bytes 196
  13.0 4.7 %collective-permute-start.6 = (bf16[16,512]{1,0:T(8,128)(2,1)S(1)}, bf16[16,512]{1,0:T(8,128)(2,1)S(1)}, u32[]{:S(2)}, u32[]{:S(2)}) collective-permute-start(bf16[16,512]{1,0:T(8,128)(2,1)S(1)} %apply_factor.1), channel_id=1, source_target_pairs={{0,30},{1,7},{2,28},{3,5},{4,2},{5,11},{6,0},{7,9},{8,6},{9,15},{1... | collective-permute-start | bytes 49160 | tf_op jit(solution)/shard_map/ppermute | solution.py:183
  14.2 3.9 %collective-permute-start.7 = (bf16[16,512]{1,0:T(8,128)(2,1)S(1)}, bf16[16,512]{1,0:T(8,128)(2,1)S(1)}, u32[]{:S(2)}, u32[]{:S(2)}) collective-permute-start(bf16[16,512]{1,0:T(8,128)(2,1)S(1)} %apply_factor.1), channel_id=1, source_target_pairs={{0,28},{1,5},{2,30},{3,7},{4,0},{5,9},{6,2},{7,11},{8,4},{9,13},{1... | collective-permute-start | bytes 49160 | tf_op jit(solution)/shard_map/ppermute | solution.py:183
  18.1 1.5 %collective-permute-start.8 = (bf16[32,512]{1,0:T(8,128)(2,1)S(1)}, bf16[32,512]{1,0:T(8,128)(2,1)S(1)}, u32[]{:S(2)}, u32[]{:S(2)}) collective-permute-start(bf16[32,512]{1,0:T(8,128)(2,1)S(1)} %constant_dynamic-update-slice_fusion.mine_ref), channel_id=1, source_target_pairs={{0,1},{1,0},{2,3},{3,2},{4,5},{5,4},{6,7},{7,6},{8,9},{9,8},{10,11... | collective-permute-start | bytes 98312 | tf_op jit(solution)/shard_map/ppermute | solution.py:174

commit v7 on v6

--- a/solution.py
+++ b/solution.py
@@ -14,6 +14,8 @@
 JOIN_FLOPS = 10**10
 FACTOR_FIRST = (1, 1)
 RESULT_FIRST = (1, 1)
+FACTOR_WRAP = (1, 0)
+RESULT_WRAP = (1, 1)
 
 
 def iota(shape, dim):
@@ -110,7 +112,12 @@
     chip = lax.axis_index("row") // 2
     depth = factors[0].shape[1]
     total = jnp.zeros(out_ref.shape, F32)
-    first = jnp.where(is_upper(), FACTOR_FIRST[1], FACTOR_FIRST[0])
+    sector, last = lax.axis_index("sec"), lax.axis_size("sec") - 1
+    first = jnp.where(
+        is_upper(),
+        jnp.where(sector == last, FACTOR_WRAP[1], FACTOR_FIRST[1]),
+        jnp.where(sector == 0, FACTOR_WRAP[0], FACTOR_FIRST[0]),
+    )
     for turn in range(chips):
         source = lax.rem(chip - turn - first + 2 * chips, chips)
         part = half_ref[pl.ds(pl.multiple_of(source * depth, depth), depth), :]
@@ -130,8 +137,18 @@
     turns = [pl.ds(turn * keep_cols, keep_cols) for turn in range(chips)]
     lower_parts = [jnp.where(upper, got_ref[turn], mine_ref[turn]) for turn in turns]
     upper_parts = [jnp.where(upper, mine_ref[turn], got_ref[turn]) for turn in turns]
-    lower_parts = [lower_parts[(away - RESULT_FIRST[0]) % chips] for away in range(chips)]
-    upper_parts = [upper_parts[(away - RESULT_FIRST[1]) % chips] for away in range(chips)]
+    sector, last = lax.axis_index("sec"), lax.axis_size("sec") - 1
+
+    def ordered(parts, core, wraps):
+        found = []
+        for away in range(chips):
+            usual = parts[(away - RESULT_FIRST[core]) % chips]
+            wrapped = parts[(away - RESULT_WRAP[core]) % chips]
+            found.append(jnp.where(wraps, wrapped, usual))
+        return found
+
+    lower_parts = ordered(lower_parts, 0, sector == last)
+    upper_parts = ordered(upper_parts, 1, sector == 0)
     for whole, ref in ((upper_parts[0], tilde_ref), (lower_parts[0], proj_ref)):
         own = jnp.where(core == 0, whole[:, :rows], whole[:, rows:])
         ref[...] = (own.astype(F32) * weight_rows).astype(BF16)
@@ -173,13 +190,13 @@
     def other_core(value):
         return lax.ppermute(value, "row", [(i, i ^ 1) for i in range(row_devices)])
 
-    def to_sector(value, upper_step, turn, first):
+    def to_sector(value, upper_step, turn, first, wrap):
         pairs = []
         for s in range(sectors):
             for r in range(row_devices):
-                t = (s + (upper_step if r % 2 else -upper_step)) % sectors
-                away = (turn + first[r % 2]) % chips
-                pairs.append((s * row_devices + r, t * row_devices + (r + 2 * away) % row_devices))
+                t = s + (upper_step if r % 2 else -upper_step)
+                away = (turn + (first if 0 <= t < sectors else wrap)[r % 2]) % chips
+                pairs.append((s * row_devices + r, t % sectors * row_devices + (r + 2 * away) % row_devices))
         return lax.ppermute(value, ("sec", "row"), pairs)
 
     block = jax.ShapeDtypeStruct((keep_cols, rows), BF16)
@@ -212,7 +229,7 @@
         cost_estimate=pl.CostEstimate(flops=JOIN_FLOPS, bytes_accessed=0, transcendentals=0),
         name="join_factor",
     )(own, mover, u_got, v_got)
-    factors = [to_sector(joined, -1, turn, FACTOR_FIRST) for turn in range(chips)]
+    factors = [to_sector(joined, -1, turn, FACTOR_FIRST, FACTOR_WRAP) for turn in range(chips)]
 
     ul, dl = corner_ul[0], corner_dl[0]
     ul_got, dl_got = other_core(ul), other_core(dl)
@@ -236,7 +253,7 @@
         compiler_params=pltpu.CompilerParams(vmem_limit_bytes=4 * MIB),
         name="apply_factor",
     )(*factors, half)
-    mine = [to_sector(applied, 1, turn, RESULT_FIRST) for turn in range(chips)]
+    mine = [to_sector(applied, 1, turn, RESULT_FIRST, RESULT_WRAP) for turn in range(chips)]
     mine = jnp.concatenate(mine, axis=0)
     theirs = other_core(mine)
 

time: 20.6 us -> 20.6 us (level)
  no operation moved by 1% of the time
where the time goes in v7:
time: 20.6 us; the launch traced here: 20.3 us
  starting transfers between devices  10.2 us (50%)
  waiting for transfers between devices  4.67 us (23%)
  Pallas kernels  2.73 us (13%)
  between operations  2.02 us (10%)
  local copies, waits for them, and re-layouts  0.65 us (3%)
    ppermute x4, starting transfers between devices, to_sector(): return lax.ppermute(value, ('sec', 'row'), pairs)  8.38 us
    ppermute x4, waiting for transfers between devices, to_sector(): return lax.ppermute(value, ('sec', 'row'), pairs)  4.4 us
    ppermute x5, starting transfers between devices, other_core(): return lax.ppermute(value, 'row', [(i, i ^ 1) for i in range(row_devices)])  1.85 us
    pallas_call x1, Pallas kernels, local(): pl.pallas_call(functools.partial(half_kernel, states_here=states_here), o...  1.53 us
    pallas_call x1, Pallas kernels, local(): pl.pallas_call(functools.partial(finish_kernel, width=width, chips=chips)...  0.74 us
    unnamed x17, local copies, waits for them, and re-layouts  0.65 us
  transfers between devices with their start and end apart: 9, of which 5 were waited for; matrix products, arithmetic and copies ran while one was open for 0% of the time, Pallas kernels for 9%

profile of v7, /device:TPU:0, one launch (start us, length us, event | category | flops | bytes accessed | tf_op | source)
XLA Modules:
  0.0 20.3 jit_solution(10318348725980124925)
XLA Ops:
  0.6 0.5 %collective-permute-start = (bf16[16,256]{1,0:T(8,128)(2,1)}, bf16[16,256]{1,0:T(8,128)(2,1)S(1)}, u32[]{:S(2)}, u32[]{:S(2)}) collective-permute-start(bf16[16,256]{1,0:T(8,128)(2,1)} %bitcast.23), channel_id=1, source_target_pairs={{0,1},{1,0},{2,3},{3,2},{4,5},{5,4},{6,7},{7,6},{8,9},{9,8},{10,11... | collective-permute-start | bytes 24584 | tf_op jit(solution)/shard_map/ppermute | solution.py:191
  1.1 0.1 collective-permute-start.1
  1.2 0.4 %collective-permute-start.4 = (bf16[256,1024]{1,0:T(8,128)(2,1)}, bf16[256,1024]{1,0:T(8,128)(2,1)S(1)}, u32[]{:S(2)}, u32[]{:S(2)}) collective-permute-start(bf16[256,1024]{1,0:T(8,128)(2,1)} %bitcast.19), channel_id=1, source_target_pairs={{0,1},{1,0},{2,3},{3,2},{4,5},{5,4},{6,7},{7,6},{8,9},{9,8},{10,11... | collective-permute-start | bytes 1572872 | tf_op jit(solution)/shard_map/ppermute | solution.py:191
  1.7 0.0 copy-start.4
  1.7 0.0 copy-start.5
  1.7 0.0 copy-start.7
  1.7 0.1 collective-permute-start.5
  1.8 0.6 %copy-done.4 = bf16[1,256,16]{1,2,0:T(8,128)(2,1)S(1)} copy-done((bf16[1,256,16]{1,2,0:T(8,128)(2,1)S(1)}, bf16[1,256,16]{1,2,0:T(8,128)(2,1)}, u32[]{:S(2)}) %copy-start.4) | copy-done | bytes 8216
  2.4 0.0 copy-done.5
  2.4 0.0 copy-done.7
  2.4 0.1 own_factor.1
  2.5 0.0 collective-permute-done.u_got_ref
  2.5 0.1 collective-permute-done.1.v_got_ref
  2.5 0.0 copy-start
  2.5 0.0 copy-start.1
  2.5 0.0 copy-start.2
  2.5 0.0 copy-start.3
  2.5 0.1 join_factor.1
  2.7 3.6 %collective-permute-start.2 = (bf16[16,512]{1,0:T(8,128)(2,1)S(1)}, bf16[16,512]{1,0:T(8,128)(2,1)S(1)}, u32[]{:S(2)}, u32[]{:S(2)}) collective-permute-start(bf16[16,512]{1,0:T(8,128)(2,1)S(1)} %join_factor.1), channel_id=1, source_target_pairs={{0,6},{1,29},{2,4},{3,31},{4,10},{5,3},{6,8},{7,1},{8,14},{9,7},{1... | collective-permute-start | bytes 49160 | tf_op jit(solution)/shard_map/ppermute | solution.py:200
  6.3 1.5 %collective-permute-start.3 = (bf16[16,512]{1,0:T(8,128)(2,1)S(1)}, bf16[16,512]{1,0:T(8,128)(2,1)S(1)}, u32[]{:S(2)}, u32[]{:S(2)}) collective-permute-start(bf16[16,512]{1,0:T(8,128)(2,1)S(1)} %join_factor.1), channel_id=1, source_target_pairs={{0,4},{1,31},{2,6},{3,29},{4,8},{5,1},{6,10},{7,3},{8,12},{9,5},{1... | collective-permute-start | bytes 49160 | tf_op jit(solution)/shard_map/ppermute | solution.py:200
  8.5 0.0 collective-permute-done.4.ul_got
  8.5 0.0 collective-permute-done.5.dl_got
  8.5 0.0 copy-done
  8.5 0.0 copy-done.1
  8.5 0.0 copy-done.2
  8.5 0.0 copy-done.3
  8.5 0.0 copy-start.6
  8.6 1.5 %half_product.1.refs_2_ = bf16[1024,512]{1,0:T(8,128)(2,1)S(1)} custom-call(s32[1]{0:T(128)S(6)} %copy.14.states_ref, bf16[256,1024]{1,0:T(8,128)(2,1)S(1)} %bitcast.20, bf16[256,1024]{1,0:T(8,128)(2,1)S(1)} %collective-permute-done.4.ul_got, bf16[1024,1024]{1,0:T(8,128)(2,1)S(1)} %bitcast.17, bf16[256,1024]{1,0:T(8,128)(2,1)S(1)} %bitcast.22, ...), custom_call_target="tpu_custom_call" | custom-call | flops 262144 | bytes 256 | tf_op jit(solution)/shard_map/half_product/pallas_call | solution.py:236
  10.1 0.9 %collective-permute-done.2.refs_0_ = bf16[16,512]{1,0:T(8,128)(2,1)S(1)} collective-permute-done((bf16[16,512]{1,0:T(8,128)(2,1)S(1)}, bf16[16,512]{1,0:T(8,128)(2,1)S(1)}, u32[]{:S(2)}, u32[]{:S(2)}) %collective-permute-start.2) | collective-permute-done | bytes 16416 | tf_op jit(solution)/shard_map/ppermute | solution.py:200
  11.0 1.7 %collective-permute-done.3.refs_1_ = bf16[16,512]{1,0:T(8,128)(2,1)S(1)} collective-permute-done((bf16[16,512]{1,0:T(8,128)(2,1)S(1)}, bf16[16,512]{1,0:T(8,128)(2,1)S(1)}, u32[]{:S(2)}, u32[]{:S(2)}) %collective-permute-start.3) | collective-permute-done | bytes 16416 | tf_op jit(solution)/shard_map/ppermute | solution.py:200
  12.7 0.2 %apply_factor.1 = bf16[16,512]{1,0:T(8,128)(2,1)S(1)} custom-call(bf16[16,512]{1,0:T(8,128)(2,1)S(1)} %collective-permute-done.2.refs_0_, bf16[16,512]{1,0:T(8,128)(2,1)S(1)} %collective-permute-done.3.refs_1_, bf16[1024,512]{1,0:T(8,128)(2,1)S(1)} %half_product.1.refs_2_), custom_call_target="tpu_custom_call" | custom-call | tf_op jit(solution)/shard_map/apply_factor/pallas_call | solution.py:248
  13.0 1.3 %collective-permute-start.6 = (bf16[16,512]{1,0:T(8,128)(2,1)S(1)}, bf16[16,512]{1,0:T(8,128)(2,1)S(1)}, u32[]{:S(2)}, u32[]{:S(2)}) collective-permute-start(bf16[16,512]{1,0:T(8,128)(2,1)S(1)} %apply_factor.1), channel_id=1, source_target_pairs={{0,30},{1,7},{2,28},{3,5},{4,2},{5,11},{6,0},{7,9},{8,6},{9,15},{1... | collective-permute-start | bytes 49160 | tf_op jit(solution)/shard_map/ppermute | solution.py:200
  14.2 2.0 %collective-permute-start.7 = (bf16[16,512]{1,0:T(8,128)(2,1)S(1)}, bf16[16,512]{1,0:T(8,128)(2,1)S(1)}, u32[]{:S(2)}, u32[]{:S(2)}) collective-permute-start(bf16[16,512]{1,0:T(8,128)(2,1)S(1)} %apply_factor.1), channel_id=1, source_target_pairs={{0,28},{1,5},{2,30},{3,7},{4,0},{5,9},{6,2},{7,11},{8,4},{9,13},{1... | collective-permute-start | bytes 49160 | tf_op jit(solution)/shard_map/ppermute | solution.py:200
  16.2 1.4 %collective-permute-done.6 = bf16[16,512]{1,0:T(8,128)(2,1)S(1)} collective-permute-done((bf16[16,512]{1,0:T(8,128)(2,1)S(1)}, bf16[16,512]{1,0:T(8,128)(2,1)S(1)}, u32[]{:S(2)}, u32[]{:S(2)}) %collective-permute-start.6) | collective-permute-done | bytes 16416 | tf_op jit(solution)/shard_map/ppermute | solution.py:200
  17.6 0.3 %collective-permute-done.7 = bf16[16,512]{1,0:T(8,128)(2,1)S(1)} collective-permute-done((bf16[16,512]{1,0:T(8,128)(2,1)S(1)}, bf16[16,512]{1,0:T(8,128)(2,1)S(1)}, u32[]{:S(2)}, u32[]{:S(2)}) %collective-permute-start.7) | collective-permute-done | bytes 16416 | tf_op jit(solution)/shard_map/ppermute | solution.py:200
  18.0 0.7 %collective-permute-start.8 = (bf16[32,512]{1,0:T(8,128)(2,1)S(1)}, bf16[32,512]{1,0:T(8,128)(2,1)S(1)}, u32[]{:S(2)}, u32[]{:S(2)}) collective-permute-start(bf16[32,512]{1,0:T(8,128)(2,1)S(1)} %constant_dynamic-update-slice_fusion.mine_ref), channel_id=1, source_target_pairs={{0,1},{1,0},{2,3},{3,2},{4,5},{5,4},{6,7},{7,6},{8,9},{9,8},{10,11... | collective-permute-start | bytes 98312 | tf_op jit(solution)/shard_map/ppermute | solution.py:191
  19.3 0.2 %collective-permute-done.8.got_ref = bf16[32,512]{1,0:T(8,128)(2,1)S(1)} collective-permute-done((bf16[32,512]{1,0:T(8,128)(2,1)S(1)}, bf16[32,512]{1,0:T(8,128)(2,1)S(1)}, u32[]{:S(2)}, u32[]{:S(2)}) %collective-permute-start.8) | collective-permute-done | bytes 32800 | tf_op jit(solution)/shard_map/ppermute | solution.py:191
  19.6 0.0 copy-done.6
  19.6 0.7 %finish.1 = (bf16[16,256]{1,0:T(8,128)(2,1)}, bf16[16,256]{1,0:T(8,128)(2,1)}, f32[16,16]{1,0:T(8,128)}) custom-call(s32[1]{0:T(128)S(6)} %copy.15.kept_ref, f32[1,16]{1,0:T(1,128)S(1)} %copy-done.6, bf16[32,512]{1,0:T(8,128)(2,1)S(1)} %constant_dynamic-update-slice_fusion.mine_ref, bf16[32,512]{1,0:T(8,128)(2,1)S(1)} %collective-permute-done.8.got_ref), custom_call_target="tpu_custom_call" | custom-call | tf_op jit(solution)/shard_map/finish/pallas_call | solution.py:260
  (3 shorter events, 0.0 us)
Async XLA Ops:
  0.6 1.8 %collective-permute-start = (bf16[16,256]{1,0:T(8,128)(2,1)}, bf16[16,256]{1,0:T(8,128)(2,1)S(1)}, u32[]{:S(2)}, u32[]{:S(2)}) collective-permute-start(bf16[16,256]{1,0:T(8,128)(2,1)} %bitcast.23), channel_id=1, source_target_pairs={{0,1},{1,0},{2,3},{3,2},{4,5},{5,4},{6,7},{7,6},{8,9},{9,8},{10,11... | collective-permute-start | bytes 24584 | tf_op jit(solution)/shard_map/ppermute | solution.py:191
  1.1 1.4 %collective-permute-start.1 = (bf16[16,256]{1,0:T(8,128)(2,1)}, bf16[16,256]{1,0:T(8,128)(2,1)S(1)}, u32[]{:S(2)}, u32[]{:S(2)}) collective-permute-start(bf16[16,256]{1,0:T(8,128)(2,1)} %bitcast.25), channel_id=1, source_target_pairs={{0,1},{1,0},{2,3},{3,2},{4,5},{5,4},{6,7},{7,6},{8,9},{9,8},{10,11... | collective-permute-start | bytes 24584 | tf_op jit(solution)/shard_map/ppermute | solution.py:191
  1.2 7.3 %collective-permute-start.4 = (bf16[256,1024]{1,0:T(8,128)(2,1)}, bf16[256,1024]{1,0:T(8,128)(2,1)S(1)}, u32[]{:S(2)}, u32[]{:S(2)}) collective-permute-start(bf16[256,1024]{1,0:T(8,128)(2,1)} %bitcast.19), channel_id=1, source_target_pairs={{0,1},{1,0},{2,3},{3,2},{4,5},{5,4},{6,7},{7,6},{8,9},{9,8},{10,11... | collective-permute-start | bytes 1572872 | tf_op jit(solution)/shard_map/ppermute | solution.py:191
  1.7 0.7 %copy-start.4 = (bf16[1,256,16]{1,2,0:T(8,128)(2,1)S(1)}, bf16[1,256,16]{1,2,0:T(8,128)(2,1)}, u32[]{:S(2)}) copy-start(bf16[1,256,16]{1,2,0:T(8,128)(2,1)} %param.14) | copy-start | bytes 24580
  1.7 0.7 %copy-start.5 = (bf16[1,256,16]{1,2,0:T(8,128)(2,1)S(1)}, bf16[1,256,16]{1,2,0:T(8,128)(2,1)}, u32[]{:S(2)}) copy-start(bf16[1,256,16]{1,2,0:T(8,128)(2,1)} %param.15) | copy-start | bytes 24580
  1.7 0.7 %copy-start.7 = (s32[1,16]{1,0:T(1,128)S(1)}, s32[1,16]{1,0:T(1,128)}, u32[]{:S(2)}) copy-start(s32[1,16]{1,0:T(1,128)} %map_ref.1) | copy-start | bytes 196
  1.7 6.8 %collective-permute-start.5 = (bf16[256,1024]{1,0:T(8,128)(2,1)}, bf16[256,1024]{1,0:T(8,128)(2,1)S(1)}, u32[]{:S(2)}, u32[]{:S(2)}) collective-permute-start(bf16[256,1024]{1,0:T(8,128)(2,1)} %bitcast.21), channel_id=1, source_target_pairs={{0,1},{1,0},{2,3},{3,2},{4,5},{5,4},{6,7},{7,6},{8,9},{9,8},{10,11... | collective-permute-start | bytes 1572872 | tf_op jit(solution)/shard_map/ppermute | solution.py:191
  2.5 6.0 %copy-start = (bf16[1,1024,1024]{2,1,0:T(8,128)(2,1)S(1)}, bf16[1,1024,1024]{2,1,0:T(8,128)(2,1)}, u32[]{:S(2)}) copy-start(bf16[1,1024,1024]{2,1,0:T(8,128)(2,1)} %param.11) | copy-start | bytes 6291460
  2.5 6.0 %copy-start.1 = (bf16[1,1024,1024]{2,1,0:T(8,128)(2,1)S(1)}, bf16[1,1024,1024]{2,1,0:T(8,128)(2,1)}, u32[]{:S(2)}) copy-start(bf16[1,1024,1024]{2,1,0:T(8,128)(2,1)} %param.13) | copy-start | bytes 6291460
  2.5 6.0 %copy-start.2 = (bf16[1,256,1024]{2,1,0:T(8,128)(2,1)S(1)}, bf16[1,256,1024]{2,1,0:T(8,128)(2,1)}, u32[]{:S(2)}) copy-start(bf16[1,256,1024]{2,1,0:T(8,128)(2,1)} %param.10) | copy-start | bytes 1572868
  2.5 6.0 %copy-start.3 = (bf16[1,256,1024]{2,1,0:T(8,128)(2,1)S(1)}, bf16[1,256,1024]{2,1,0:T(8,128)(2,1)}, u32[]{:S(2)}) copy-start(bf16[1,256,1024]{2,1,0:T(8,128)(2,1)} %param.12) | copy-start | bytes 1572868
  2.7 8.4 %collective-permute-start.2 = (bf16[16,512]{1,0:T(8,128)(2,1)S(1)}, bf16[16,512]{1,0:T(8,128)(2,1)S(1)}, u32[]{:S(2)}, u32[]{:S(2)}) collective-permute-start(bf16[16,512]{1,0:T(8,128)(2,1)S(1)} %join_factor.1), channel_id=1, source_target_pairs={{0,6},{1,29},{2,4},{3,31},{4,10},{5,3},{6,8},{7,1},{8,14},{9,7},{1... | collective-permute-start | bytes 49160 | tf_op jit(solution)/shard_map/ppermute | solution.py:200
  6.3 6.4 %collective-permute-start.3 = (bf16[16,512]{1,0:T(8,128)(2,1)S(1)}, bf16[16,512]{1,0:T(8,128)(2,1)S(1)}, u32[]{:S(2)}, u32[]{:S(2)}) collective-permute-start(bf16[16,512]{1,0:T(8,128)(2,1)S(1)} %join_factor.1), channel_id=1, source_target_pairs={{0,4},{1,31},{2,6},{3,29},{4,8},{5,1},{6,10},{7,3},{8,12},{9,5},{1... | collective-permute-start | bytes 49160 | tf_op jit(solution)/shard_map/ppermute | solution.py:200
  8.5 11.0 %copy-start.6 = (f32[1,16]{1,0:T(1,128)S(1)}, f32[1,16]{1,0:T(1,128)}, u32[]{:S(2)}) copy-start(f32[1,16]{1,0:T(1,128)} %singular_ref.1) | copy-start | bytes 196
  13.0 4.7 %collective-permute-start.6 = (bf16[16,512]{1,0:T(8,128)(2,1)S(1)}, bf16[16,512]{1,0:T(8,128)(2,1)S(1)}, u32[]{:S(2)}, u32[]{:S(2)}) collective-permute-start(bf16[16,512]{1,0:T(8,128)(2,1)S(1)} %apply_factor.1), channel_id=1, source_target_pairs={{0,30},{1,7},{2,28},{3,5},{4,2},{5,11},{6,0},{7,9},{8,6},{9,15},{1... | collective-permute-start | bytes 49160 | tf_op jit(solution)/shard_map/ppermute | solution.py:200
  14.2 3.7 %collective-permute-start.7 = (bf16[16,512]{1,0:T(8,128)(2,1)S(1)}, bf16[16,512]{1,0:T(8,128)(2,1)S(1)}, u32[]{:S(2)}, u32[]{:S(2)}) collective-permute-start(bf16[16,512]{1,0:T(8,128)(2,1)S(1)} %apply_factor.1), channel_id=1, source_target_pairs={{0,28},{1,5},{2,30},{3,7},{4,0},{5,9},{6,2},{7,11},{8,4},{9,13},{1... | collective-permute-start | bytes 49160 | tf_op jit(solution)/shard_map/ppermute | solution.py:200
  18.0 1.6 %collective-permute-start.8 = (bf16[32,512]{1,0:T(8,128)(2,1)S(1)}, bf16[32,512]{1,0:T(8,128)(2,1)S(1)}, u32[]{:S(2)}, u32[]{:S(2)}) collective-permute-start(bf16[32,512]{1,0:T(8,128)(2,1)S(1)} %constant_dynamic-update-slice_fusion.mine_ref), channel_id=1, source_target_pairs={{0,1},{1,0},{2,3},{3,2},{4,5},{5,4},{6,7},{7,6},{8,9},{9,8},{10,11... | collective-permute-start | bytes 98312 | tf_op jit(solution)/shard_map/ppermute | solution.py:191

commit v8 on v6

--- a/solution.py
+++ b/solution.py
@@ -139,12 +139,16 @@
         lax.dot_general(a, b, (((1,), (1,)), ((), ())), preferred_element_type=F32)
         for a, b in zip(upper_parts, lower_parts)
     ]
-    total = jnp.zeros(square, F32)
-    for source in range(chips):
-        for away in range(chips):
-            here = lax.rem(chip - away + chips, chips) == source
-            total += jnp.where(here, products[away], 0.0)
-    inter_ref[...] = total * weight_rows * weight / jnp.sqrt(jnp.float32(width))
+    total = products[0]
+    if chips == 2:
+        total = products[0] + products[1]
+    elif chips > 2:
+        total = jnp.zeros(square, F32)
+        for source in range(chips):
+            for away in range(chips):
+                here = lax.rem(chip - away + chips, chips) == source
+                total += jnp.where(here, products[away], 0.0)
+    inter_ref[...] = total * (weight_rows * weight / jnp.sqrt(jnp.float32(width)))
 
 
 def in_vmem():

time: 20.6 us -> 20.6 us (level)
  no operation moved by 1% of the time
where the time goes in v8:
time: 20.6 us; the launch traced here: 20.4 us
  starting transfers between devices  10.2 us (50%)
  waiting for transfers between devices  4.83 us (23%)
  Pallas kernels  2.72 us (13%)
  between operations  2.02 us (10%)
  local copies, waits for them, and re-layouts  0.65 us (3%)
    ppermute x4, starting transfers between devices, to_sector(): return lax.ppermute(value, ('sec', 'row'), pairs)  8.38 us
    ppermute x4, waiting for transfers between devices, to_sector(): return lax.ppermute(value, ('sec', 'row'), pairs)  4.56 us
    ppermute x5, starting transfers between devices, other_core(): return lax.ppermute(value, 'row', [(i, i ^ 1) for i in range(row_devices)])  1.79 us
    pallas_call x1, Pallas kernels, local(): pl.pallas_call(functools.partial(half_kernel, states_here=states_here), o...  1.53 us
    pallas_call x1, Pallas kernels, local(): pl.pallas_call(functools.partial(finish_kernel, width=width, chips=chips)...  0.73 us
    unnamed x17, local copies, waits for them, and re-layouts  0.65 us
  transfers between devices with their start and end apart: 9, of which 5 were waited for; matrix products, arithmetic and copies ran while one was open for 0% of the time, Pallas kernels for 9%

profile of v8, /device:TPU:0, one launch (start us, length us, event | category | flops | bytes accessed | tf_op | source)
XLA Modules:
  0.0 20.4 jit_solution(2894391753069724446)
XLA Ops:
  0.6 0.5 %collective-permute-start = (bf16[16,256]{1,0:T(8,128)(2,1)}, bf16[16,256]{1,0:T(8,128)(2,1)S(1)}, u32[]{:S(2)}, u32[]{:S(2)}) collective-permute-start(bf16[16,256]{1,0:T(8,128)(2,1)} %bitcast.23), channel_id=1, source_target_pairs={{0,1},{1,0},{2,3},{3,2},{4,5},{5,4},{6,7},{7,6},{8,9},{9,8},{10,11... | collective-permute-start | bytes 24584 | tf_op jit(solution)/shard_map/ppermute | solution.py:178
  1.1 0.1 collective-permute-start.1
  1.2 0.4 %collective-permute-start.4 = (bf16[256,1024]{1,0:T(8,128)(2,1)}, bf16[256,1024]{1,0:T(8,128)(2,1)S(1)}, u32[]{:S(2)}, u32[]{:S(2)}) collective-permute-start(bf16[256,1024]{1,0:T(8,128)(2,1)} %bitcast.19), channel_id=1, source_target_pairs={{0,1},{1,0},{2,3},{3,2},{4,5},{5,4},{6,7},{7,6},{8,9},{9,8},{10,11... | collective-permute-start | bytes 1572872 | tf_op jit(solution)/shard_map/ppermute | solution.py:178
  1.7 0.0 copy-start.4
  1.7 0.0 copy-start.5
  1.7 0.0 copy-start.7
  1.7 0.1 collective-permute-start.5
  1.8 0.6 %copy-done.4 = bf16[1,256,16]{1,2,0:T(8,128)(2,1)S(1)} copy-done((bf16[1,256,16]{1,2,0:T(8,128)(2,1)S(1)}, bf16[1,256,16]{1,2,0:T(8,128)(2,1)}, u32[]{:S(2)}) %copy-start.4) | copy-done | bytes 8216
  2.4 0.0 copy-done.5
  2.4 0.0 copy-done.7
  2.4 0.1 own_factor.1
  2.5 0.0 collective-permute-done.u_got_ref
  2.5 0.1 collective-permute-done.1.v_got_ref
  2.5 0.0 copy-start
  2.5 0.0 copy-start.1
  2.5 0.0 copy-start.2
  2.5 0.0 copy-start.3
  2.5 0.1 join_factor.1
  2.7 3.6 %collective-permute-start.2 = (bf16[16,512]{1,0:T(8,128)(2,1)S(1)}, bf16[16,512]{1,0:T(8,128)(2,1)S(1)}, u32[]{:S(2)}, u32[]{:S(2)}) collective-permute-start(bf16[16,512]{1,0:T(8,128)(2,1)S(1)} %join_factor.1), channel_id=1, source_target_pairs={{0,6},{1,31},{2,4},{3,29},{4,10},{5,3},{6,8},{7,1},{8,14},{9,7},{1... | collective-permute-start | bytes 49160 | tf_op jit(solution)/shard_map/ppermute | solution.py:187
  6.3 1.5 %collective-permute-start.3 = (bf16[16,512]{1,0:T(8,128)(2,1)S(1)}, bf16[16,512]{1,0:T(8,128)(2,1)S(1)}, u32[]{:S(2)}, u32[]{:S(2)}) collective-permute-start(bf16[16,512]{1,0:T(8,128)(2,1)S(1)} %join_factor.1), channel_id=1, source_target_pairs={{0,4},{1,29},{2,6},{3,31},{4,8},{5,1},{6,10},{7,3},{8,12},{9,5},{1... | collective-permute-start | bytes 49160 | tf_op jit(solution)/shard_map/ppermute | solution.py:187
  8.5 0.0 collective-permute-done.4.ul_got
  8.5 0.0 collective-permute-done.5.dl_got
  8.5 0.0 copy-done
  8.5 0.0 copy-done.1
  8.5 0.0 copy-done.2
  8.5 0.0 copy-done.3
  8.5 0.0 copy-start.6
  8.6 1.5 %half_product.1.refs_2_ = bf16[1024,512]{1,0:T(8,128)(2,1)S(1)} custom-call(s32[1]{0:T(128)S(6)} %copy.14.states_ref, bf16[256,1024]{1,0:T(8,128)(2,1)S(1)} %bitcast.20, bf16[256,1024]{1,0:T(8,128)(2,1)S(1)} %collective-permute-done.4.ul_got, bf16[1024,1024]{1,0:T(8,128)(2,1)S(1)} %bitcast.17, bf16[256,1024]{1,0:T(8,128)(2,1)S(1)} %bitcast.22, ...), custom_call_target="tpu_custom_call" | custom-call | flops 262144 | bytes 256 | tf_op jit(solution)/shard_map/half_product/pallas_call | solution.py:223
  10.1 0.9 %collective-permute-done.2.refs_0_ = bf16[16,512]{1,0:T(8,128)(2,1)S(1)} collective-permute-done((bf16[16,512]{1,0:T(8,128)(2,1)S(1)}, bf16[16,512]{1,0:T(8,128)(2,1)S(1)}, u32[]{:S(2)}, u32[]{:S(2)}) %collective-permute-start.2) | collective-permute-done | bytes 16416 | tf_op jit(solution)/shard_map/ppermute | solution.py:187
  11.0 1.7 %collective-permute-done.3.refs_1_ = bf16[16,512]{1,0:T(8,128)(2,1)S(1)} collective-permute-done((bf16[16,512]{1,0:T(8,128)(2,1)S(1)}, bf16[16,512]{1,0:T(8,128)(2,1)S(1)}, u32[]{:S(2)}, u32[]{:S(2)}) %collective-permute-start.3) | collective-permute-done | bytes 16416 | tf_op jit(solution)/shard_map/ppermute | solution.py:187
  12.7 0.2 %apply_factor.1 = bf16[16,512]{1,0:T(8,128)(2,1)S(1)} custom-call(bf16[16,512]{1,0:T(8,128)(2,1)S(1)} %collective-permute-done.2.refs_0_, bf16[16,512]{1,0:T(8,128)(2,1)S(1)} %collective-permute-done.3.refs_1_, bf16[1024,512]{1,0:T(8,128)(2,1)S(1)} %half_product.1.refs_2_), custom_call_target="tpu_custom_call" | custom-call | tf_op jit(solution)/shard_map/apply_factor/pallas_call | solution.py:235
  13.0 1.3 %collective-permute-start.6 = (bf16[16,512]{1,0:T(8,128)(2,1)S(1)}, bf16[16,512]{1,0:T(8,128)(2,1)S(1)}, u32[]{:S(2)}, u32[]{:S(2)}) collective-permute-start(bf16[16,512]{1,0:T(8,128)(2,1)S(1)} %apply_factor.1), channel_id=1, source_target_pairs={{0,30},{1,7},{2,28},{3,5},{4,2},{5,11},{6,0},{7,9},{8,6},{9,15},{1... | collective-permute-start | bytes 49160 | tf_op jit(solution)/shard_map/ppermute | solution.py:187
  14.2 2.0 %collective-permute-start.7 = (bf16[16,512]{1,0:T(8,128)(2,1)S(1)}, bf16[16,512]{1,0:T(8,128)(2,1)S(1)}, u32[]{:S(2)}, u32[]{:S(2)}) collective-permute-start(bf16[16,512]{1,0:T(8,128)(2,1)S(1)} %apply_factor.1), channel_id=1, source_target_pairs={{0,28},{1,5},{2,30},{3,7},{4,0},{5,9},{6,2},{7,11},{8,4},{9,13},{1... | collective-permute-start | bytes 49160 | tf_op jit(solution)/shard_map/ppermute | solution.py:187
  16.2 1.4 %collective-permute-done.6 = bf16[16,512]{1,0:T(8,128)(2,1)S(1)} collective-permute-done((bf16[16,512]{1,0:T(8,128)(2,1)S(1)}, bf16[16,512]{1,0:T(8,128)(2,1)S(1)}, u32[]{:S(2)}, u32[]{:S(2)}) %collective-permute-start.6) | collective-permute-done | bytes 16416 | tf_op jit(solution)/shard_map/ppermute | solution.py:187
  17.6 0.5 %collective-permute-done.7 = bf16[16,512]{1,0:T(8,128)(2,1)S(1)} collective-permute-done((bf16[16,512]{1,0:T(8,128)(2,1)S(1)}, bf16[16,512]{1,0:T(8,128)(2,1)S(1)}, u32[]{:S(2)}, u32[]{:S(2)}) %collective-permute-start.7) | collective-permute-done | bytes 16416 | tf_op jit(solution)/shard_map/ppermute | solution.py:187
  18.1 0.7 %collective-permute-start.8 = (bf16[32,512]{1,0:T(8,128)(2,1)S(1)}, bf16[32,512]{1,0:T(8,128)(2,1)S(1)}, u32[]{:S(2)}, u32[]{:S(2)}) collective-permute-start(bf16[32,512]{1,0:T(8,128)(2,1)S(1)} %constant_dynamic-update-slice_fusion.mine_ref), channel_id=1, source_target_pairs={{0,1},{1,0},{2,3},{3,2},{4,5},{5,4},{6,7},{7,6},{8,9},{9,8},{10,11... | collective-permute-start | bytes 98312 | tf_op jit(solution)/shard_map/ppermute | solution.py:178
  19.4 0.2 %collective-permute-done.8.got_ref = bf16[32,512]{1,0:T(8,128)(2,1)S(1)} collective-permute-done((bf16[32,512]{1,0:T(8,128)(2,1)S(1)}, bf16[32,512]{1,0:T(8,128)(2,1)S(1)}, u32[]{:S(2)}, u32[]{:S(2)}) %collective-permute-start.8) | collective-permute-done | bytes 32800 | tf_op jit(solution)/shard_map/ppermute | solution.py:178
  19.7 0.0 copy-done.6
  19.7 0.7 %finish.1 = (bf16[16,256]{1,0:T(8,128)(2,1)}, bf16[16,256]{1,0:T(8,128)(2,1)}, f32[16,16]{1,0:T(8,128)}) custom-call(s32[1]{0:T(128)S(6)} %copy.15.kept_ref, f32[1,16]{1,0:T(1,128)S(1)} %copy-done.6, bf16[32,512]{1,0:T(8,128)(2,1)S(1)} %constant_dynamic-update-slice_fusion.mine_ref, bf16[32,512]{1,0:T(8,128)(2,1)S(1)} %collective-permute-done.8.got_ref), custom_call_target="tpu_custom_call" | custom-call | tf_op jit(solution)/shard_map/finish/pallas_call | solution.py:247
  (3 shorter events, 0.0 us)
Async XLA Ops:
  0.6 1.8 %collective-permute-start = (bf16[16,256]{1,0:T(8,128)(2,1)}, bf16[16,256]{1,0:T(8,128)(2,1)S(1)}, u32[]{:S(2)}, u32[]{:S(2)}) collective-permute-start(bf16[16,256]{1,0:T(8,128)(2,1)} %bitcast.23), channel_id=1, source_target_pairs={{0,1},{1,0},{2,3},{3,2},{4,5},{5,4},{6,7},{7,6},{8,9},{9,8},{10,11... | collective-permute-start | bytes 24584 | tf_op jit(solution)/shard_map/ppermute | solution.py:178
  1.1 1.4 %collective-permute-start.1 = (bf16[16,256]{1,0:T(8,128)(2,1)}, bf16[16,256]{1,0:T(8,128)(2,1)S(1)}, u32[]{:S(2)}, u32[]{:S(2)}) collective-permute-start(bf16[16,256]{1,0:T(8,128)(2,1)} %bitcast.25), channel_id=1, source_target_pairs={{0,1},{1,0},{2,3},{3,2},{4,5},{5,4},{6,7},{7,6},{8,9},{9,8},{10,11... | collective-permute-start | bytes 24584 | tf_op jit(solution)/shard_map/ppermute | solution.py:178
  1.2 7.3 %collective-permute-start.4 = (bf16[256,1024]{1,0:T(8,128)(2,1)}, bf16[256,1024]{1,0:T(8,128)(2,1)S(1)}, u32[]{:S(2)}, u32[]{:S(2)}) collective-permute-start(bf16[256,1024]{1,0:T(8,128)(2,1)} %bitcast.19), channel_id=1, source_target_pairs={{0,1},{1,0},{2,3},{3,2},{4,5},{5,4},{6,7},{7,6},{8,9},{9,8},{10,11... | collective-permute-start | bytes 1572872 | tf_op jit(solution)/shard_map/ppermute | solution.py:178
  1.7 0.7 %copy-start.4 = (bf16[1,256,16]{1,2,0:T(8,128)(2,1)S(1)}, bf16[1,256,16]{1,2,0:T(8,128)(2,1)}, u32[]{:S(2)}) copy-start(bf16[1,256,16]{1,2,0:T(8,128)(2,1)} %param.14) | copy-start | bytes 24580
  1.7 0.7 %copy-start.5 = (bf16[1,256,16]{1,2,0:T(8,128)(2,1)S(1)}, bf16[1,256,16]{1,2,0:T(8,128)(2,1)}, u32[]{:S(2)}) copy-start(bf16[1,256,16]{1,2,0:T(8,128)(2,1)} %param.15) | copy-start | bytes 24580
  1.7 0.7 %copy-start.7 = (s32[1,16]{1,0:T(1,128)S(1)}, s32[1,16]{1,0:T(1,128)}, u32[]{:S(2)}) copy-start(s32[1,16]{1,0:T(1,128)} %map_ref.1) | copy-start | bytes 196
  1.7 6.8 %collective-permute-start.5 = (bf16[256,1024]{1,0:T(8,128)(2,1)}, bf16[256,1024]{1,0:T(8,128)(2,1)S(1)}, u32[]{:S(2)}, u32[]{:S(2)}) collective-permute-start(bf16[256,1024]{1,0:T(8,128)(2,1)} %bitcast.21), channel_id=1, source_target_pairs={{0,1},{1,0},{2,3},{3,2},{4,5},{5,4},{6,7},{7,6},{8,9},{9,8},{10,11... | collective-permute-start | bytes 1572872 | tf_op jit(solution)/shard_map/ppermute | solution.py:178
  2.5 6.0 %copy-start = (bf16[1,1024,1024]{2,1,0:T(8,128)(2,1)S(1)}, bf16[1,1024,1024]{2,1,0:T(8,128)(2,1)}, u32[]{:S(2)}) copy-start(bf16[1,1024,1024]{2,1,0:T(8,128)(2,1)} %param.11) | copy-start | bytes 6291460
  2.5 6.0 %copy-start.1 = (bf16[1,1024,1024]{2,1,0:T(8,128)(2,1)S(1)}, bf16[1,1024,1024]{2,1,0:T(8,128)(2,1)}, u32[]{:S(2)}) copy-start(bf16[1,1024,1024]{2,1,0:T(8,128)(2,1)} %param.13) | copy-start | bytes 6291460
  2.5 6.0 %copy-start.2 = (bf16[1,256,1024]{2,1,0:T(8,128)(2,1)S(1)}, bf16[1,256,1024]{2,1,0:T(8,128)(2,1)}, u32[]{:S(2)}) copy-start(bf16[1,256,1024]{2,1,0:T(8,128)(2,1)} %param.10) | copy-start | bytes 1572868
  2.5 6.0 %copy-start.3 = (bf16[1,256,1024]{2,1,0:T(8,128)(2,1)S(1)}, bf16[1,256,1024]{2,1,0:T(8,128)(2,1)}, u32[]{:S(2)}) copy-start(bf16[1,256,1024]{2,1,0:T(8,128)(2,1)} %param.12) | copy-start | bytes 1572868
  2.7 8.4 %collective-permute-start.2 = (bf16[16,512]{1,0:T(8,128)(2,1)S(1)}, bf16[16,512]{1,0:T(8,128)(2,1)S(1)}, u32[]{:S(2)}, u32[]{:S(2)}) collective-permute-start(bf16[16,512]{1,0:T(8,128)(2,1)S(1)} %join_factor.1), channel_id=1, source_target_pairs={{0,6},{1,31},{2,4},{3,29},{4,10},{5,3},{6,8},{7,1},{8,14},{9,7},{1... | collective-permute-start | bytes 49160 | tf_op jit(solution)/shard_map/ppermute | solution.py:187
  6.3 6.4 %collective-permute-start.3 = (bf16[16,512]{1,0:T(8,128)(2,1)S(1)}, bf16[16,512]{1,0:T(8,128)(2,1)S(1)}, u32[]{:S(2)}, u32[]{:S(2)}) collective-permute-start(bf16[16,512]{1,0:T(8,128)(2,1)S(1)} %join_factor.1), channel_id=1, source_target_pairs={{0,4},{1,29},{2,6},{3,31},{4,8},{5,1},{6,10},{7,3},{8,12},{9,5},{1... | collective-permute-start | bytes 49160 | tf_op jit(solution)/shard_map/ppermute | solution.py:187
  8.5 11.1 %copy-start.6 = (f32[1,16]{1,0:T(1,128)S(1)}, f32[1,16]{1,0:T(1,128)}, u32[]{:S(2)}) copy-start(f32[1,16]{1,0:T(1,128)} %singular_ref.1) | copy-start | bytes 196
  13.0 4.7 %collective-permute-start.6 = (bf16[16,512]{1,0:T(8,128)(2,1)S(1)}, bf16[16,512]{1,0:T(8,128)(2,1)S(1)}, u32[]{:S(2)}, u32[]{:S(2)}) collective-permute-start(bf16[16,512]{1,0:T(8,128)(2,1)S(1)} %apply_factor.1), channel_id=1, source_target_pairs={{0,30},{1,7},{2,28},{3,5},{4,2},{5,11},{6,0},{7,9},{8,6},{9,15},{1... | collective-permute-start | bytes 49160 | tf_op jit(solution)/shard_map/ppermute | solution.py:187
  14.2 3.9 %collective-permute-start.7 = (bf16[16,512]{1,0:T(8,128)(2,1)S(1)}, bf16[16,512]{1,0:T(8,128)(2,1)S(1)}, u32[]{:S(2)}, u32[]{:S(2)}) collective-permute-start(bf16[16,512]{1,0:T(8,128)(2,1)S(1)} %apply_factor.1), channel_id=1, source_target_pairs={{0,28},{1,5},{2,30},{3,7},{4,0},{5,9},{6,2},{7,11},{8,4},{9,13},{1... | collective-permute-start | bytes 49160 | tf_op jit(solution)/shard_map/ppermute | solution.py:187
  18.1 1.5 %collective-permute-start.8 = (bf16[32,512]{1,0:T(8,128)(2,1)S(1)}, bf16[32,512]{1,0:T(8,128)(2,1)S(1)}, u32[]{:S(2)}, u32[]{:S(2)}) collective-permute-start(bf16[32,512]{1,0:T(8,128)(2,1)S(1)} %constant_dynamic-update-slice_fusion.mine_ref), channel_id=1, source_target_pairs={{0,1},{1,0},{2,3},{3,2},{4,5},{5,4},{6,7},{7,6},{8,9},{9,8},{10,11... | collective-permute-start | bytes 98312 | tf_op jit(solution)/shard_map/ppermute | solution.py:178

commit v9 on v7

--- a/solution.py
+++ b/solution.py
@@ -156,12 +156,16 @@
         lax.dot_general(a, b, (((1,), (1,)), ((), ())), preferred_element_type=F32)
         for a, b in zip(upper_parts, lower_parts)
     ]
-    total = jnp.zeros(square, F32)
-    for source in range(chips):
-        for away in range(chips):
-            here = lax.rem(chip - away + chips, chips) == source
-            total += jnp.where(here, products[away], 0.0)
-    inter_ref[...] = total * weight_rows * weight / jnp.sqrt(jnp.float32(width))
+    total = products[0]
+    if chips == 2:
+        total = products[0] + products[1]
+    elif chips > 2:
+        total = jnp.zeros(square, F32)
+        for source in range(chips):
+            for away in range(chips):
+                here = lax.rem(chip - away + chips, chips) == source
+                total += jnp.where(here, products[away], 0.0)
+    inter_ref[...] = total * (weight_rows * weight / jnp.sqrt(jnp.float32(width)))
 
 
 def in_vmem():

time: 20.6 us -> 20.5 us (level)
  no operation moved by 1% of the time
where the time goes in v9:
time: 20.5 us; the launch traced here: 20.3 us
  starting transfers between devices  10.2 us (50%)
  waiting for transfers between devices  4.67 us (23%)
  Pallas kernels  2.72 us (13%)
  between operations  2.02 us (10%)
  local copies, waits for them, and re-layouts  0.65 us (3%)
    ppermute x4, starting transfers between devices, to_sector(): return lax.ppermute(value, ('sec', 'row'), pairs)  8.38 us
    ppermute x4, waiting for transfers between devices, to_sector(): return lax.ppermute(value, ('sec', 'row'), pairs)  4.4 us
    ppermute x5, starting transfers between devices, other_core(): return lax.ppermute(value, 'row', [(i, i ^ 1) for i in range(row_devices)])  1.85 us
    pallas_call x1, Pallas kernels, local(): pl.pallas_call(functools.partial(half_kernel, states_here=states_here), o...  1.53 us
    pallas_call x1, Pallas kernels, local(): pl.pallas_call(functools.partial(finish_kernel, width=width, chips=chips)...  0.73 us
    unnamed x17, local copies, waits for them, and re-layouts  0.65 us
  transfers between devices with their start and end apart: 9, of which 5 were waited for; matrix products, arithmetic and copies ran while one was open for 0% of the time, Pallas kernels for 9%

profile of v9, /device:TPU:0, one launch (start us, length us, event | category | flops | bytes accessed | tf_op | source)
XLA Modules:
  0.0 20.3 jit_solution(10551783348642781064)
XLA Ops:
  0.6 0.5 %collective-permute-start = (bf16[16,256]{1,0:T(8,128)(2,1)}, bf16[16,256]{1,0:T(8,128)(2,1)S(1)}, u32[]{:S(2)}, u32[]{:S(2)}) collective-permute-start(bf16[16,256]{1,0:T(8,128)(2,1)} %bitcast.23), channel_id=1, source_target_pairs={{0,1},{1,0},{2,3},{3,2},{4,5},{5,4},{6,7},{7,6},{8,9},{9,8},{10,11... | collective-permute-start | bytes 24584 | tf_op jit(solution)/shard_map/ppermute | solution.py:195
  1.1 0.1 collective-permute-start.1
  1.2 0.4 %collective-permute-start.4 = (bf16[256,1024]{1,0:T(8,128)(2,1)}, bf16[256,1024]{1,0:T(8,128)(2,1)S(1)}, u32[]{:S(2)}, u32[]{:S(2)}) collective-permute-start(bf16[256,1024]{1,0:T(8,128)(2,1)} %bitcast.19), channel_id=1, source_target_pairs={{0,1},{1,0},{2,3},{3,2},{4,5},{5,4},{6,7},{7,6},{8,9},{9,8},{10,11... | collective-permute-start | bytes 1572872 | tf_op jit(solution)/shard_map/ppermute | solution.py:195
  1.7 0.0 copy-start.4
  1.7 0.0 copy-start.5
  1.7 0.0 copy-start.7
  1.7 0.1 collective-permute-start.5
  1.8 0.6 %copy-done.4 = bf16[1,256,16]{1,2,0:T(8,128)(2,1)S(1)} copy-done((bf16[1,256,16]{1,2,0:T(8,128)(2,1)S(1)}, bf16[1,256,16]{1,2,0:T(8,128)(2,1)}, u32[]{:S(2)}) %copy-start.4) | copy-done | bytes 8216
  2.4 0.0 copy-done.5
  2.4 0.0 copy-done.7
  2.4 0.1 own_factor.1
  2.5 0.0 collective-permute-done.u_got_ref
  2.5 0.1 collective-permute-done.1.v_got_ref
  2.5 0.0 copy-start
  2.5 0.0 copy-start.1
  2.5 0.0 copy-start.2
  2.5 0.0 copy-start.3
  2.5 0.1 join_factor.1
  2.7 3.6 %collective-permute-start.2 = (bf16[16,512]{1,0:T(8,128)(2,1)S(1)}, bf16[16,512]{1,0:T(8,128)(2,1)S(1)}, u32[]{:S(2)}, u32[]{:S(2)}) collective-permute-start(bf16[16,512]{1,0:T(8,128)(2,1)S(1)} %join_factor.1), channel_id=1, source_target_pairs={{0,6},{1,29},{2,4},{3,31},{4,10},{5,3},{6,8},{7,1},{8,14},{9,7},{1... | collective-permute-start | bytes 49160 | tf_op jit(solution)/shard_map/ppermute | solution.py:204
  6.3 1.5 %collective-permute-start.3 = (bf16[16,512]{1,0:T(8,128)(2,1)S(1)}, bf16[16,512]{1,0:T(8,128)(2,1)S(1)}, u32[]{:S(2)}, u32[]{:S(2)}) collective-permute-start(bf16[16,512]{1,0:T(8,128)(2,1)S(1)} %join_factor.1), channel_id=1, source_target_pairs={{0,4},{1,31},{2,6},{3,29},{4,8},{5,1},{6,10},{7,3},{8,12},{9,5},{1... | collective-permute-start | bytes 49160 | tf_op jit(solution)/shard_map/ppermute | solution.py:204
  8.5 0.0 collective-permute-done.4.ul_got
  8.5 0.0 collective-permute-done.5.dl_got
  8.5 0.0 copy-done
  8.5 0.0 copy-done.1
  8.5 0.0 copy-done.2
  8.5 0.0 copy-done.3
  8.5 0.0 copy-start.6
  8.6 1.5 %half_product.1.refs_2_ = bf16[1024,512]{1,0:T(8,128)(2,1)S(1)} custom-call(s32[1]{0:T(128)S(6)} %copy.14.states_ref, bf16[256,1024]{1,0:T(8,128)(2,1)S(1)} %bitcast.20, bf16[256,1024]{1,0:T(8,128)(2,1)S(1)} %collective-permute-done.4.ul_got, bf16[1024,1024]{1,0:T(8,128)(2,1)S(1)} %bitcast.17, bf16[256,1024]{1,0:T(8,128)(2,1)S(1)} %bitcast.22, ...), custom_call_target="tpu_custom_call" | custom-call | flops 262144 | bytes 256 | tf_op jit(solution)/shard_map/half_product/pallas_call | solution.py:240
  10.1 0.9 %collective-permute-done.2.refs_0_ = bf16[16,512]{1,0:T(8,128)(2,1)S(1)} collective-permute-done((bf16[16,512]{1,0:T(8,128)(2,1)S(1)}, bf16[16,512]{1,0:T(8,128)(2,1)S(1)}, u32[]{:S(2)}, u32[]{:S(2)}) %collective-permute-start.2) | collective-permute-done | bytes 16416 | tf_op jit(solution)/shard_map/ppermute | solution.py:204
  11.0 1.7 %collective-permute-done.3.refs_1_ = bf16[16,512]{1,0:T(8,128)(2,1)S(1)} collective-permute-done((bf16[16,512]{1,0:T(8,128)(2,1)S(1)}, bf16[16,512]{1,0:T(8,128)(2,1)S(1)}, u32[]{:S(2)}, u32[]{:S(2)}) %collective-permute-start.3) | collective-permute-done | bytes 16416 | tf_op jit(solution)/shard_map/ppermute | solution.py:204
  12.7 0.2 %apply_factor.1 = bf16[16,512]{1,0:T(8,128)(2,1)S(1)} custom-call(bf16[16,512]{1,0:T(8,128)(2,1)S(1)} %collective-permute-done.2.refs_0_, bf16[16,512]{1,0:T(8,128)(2,1)S(1)} %collective-permute-done.3.refs_1_, bf16[1024,512]{1,0:T(8,128)(2,1)S(1)} %half_product.1.refs_2_), custom_call_target="tpu_custom_call" | custom-call | tf_op jit(solution)/shard_map/apply_factor/pallas_call | solution.py:252
  13.0 1.3 %collective-permute-start.6 = (bf16[16,512]{1,0:T(8,128)(2,1)S(1)}, bf16[16,512]{1,0:T(8,128)(2,1)S(1)}, u32[]{:S(2)}, u32[]{:S(2)}) collective-permute-start(bf16[16,512]{1,0:T(8,128)(2,1)S(1)} %apply_factor.1), channel_id=1, source_target_pairs={{0,30},{1,7},{2,28},{3,5},{4,2},{5,11},{6,0},{7,9},{8,6},{9,15},{1... | collective-permute-start | bytes 49160 | tf_op jit(solution)/shard_map/ppermute | solution.py:204
  14.2 2.0 %collective-permute-start.7 = (bf16[16,512]{1,0:T(8,128)(2,1)S(1)}, bf16[16,512]{1,0:T(8,128)(2,1)S(1)}, u32[]{:S(2)}, u32[]{:S(2)}) collective-permute-start(bf16[16,512]{1,0:T(8,128)(2,1)S(1)} %apply_factor.1), channel_id=1, source_target_pairs={{0,28},{1,5},{2,30},{3,7},{4,0},{5,9},{6,2},{7,11},{8,4},{9,13},{1... | collective-permute-start | bytes 49160 | tf_op jit(solution)/shard_map/ppermute | solution.py:204
  16.2 1.4 %collective-permute-done.6 = bf16[16,512]{1,0:T(8,128)(2,1)S(1)} collective-permute-done((bf16[16,512]{1,0:T(8,128)(2,1)S(1)}, bf16[16,512]{1,0:T(8,128)(2,1)S(1)}, u32[]{:S(2)}, u32[]{:S(2)}) %collective-permute-start.6) | collective-permute-done | bytes 16416 | tf_op jit(solution)/shard_map/ppermute | solution.py:204
  17.6 0.3 %collective-permute-done.7 = bf16[16,512]{1,0:T(8,128)(2,1)S(1)} collective-permute-done((bf16[16,512]{1,0:T(8,128)(2,1)S(1)}, bf16[16,512]{1,0:T(8,128)(2,1)S(1)}, u32[]{:S(2)}, u32[]{:S(2)}) %collective-permute-start.7) | collective-permute-done | bytes 16416 | tf_op jit(solution)/shard_map/ppermute | solution.py:204
  18.0 0.7 %collective-permute-start.8 = (bf16[32,512]{1,0:T(8,128)(2,1)S(1)}, bf16[32,512]{1,0:T(8,128)(2,1)S(1)}, u32[]{:S(2)}, u32[]{:S(2)}) collective-permute-start(bf16[32,512]{1,0:T(8,128)(2,1)S(1)} %constant_dynamic-update-slice_fusion.mine_ref), channel_id=1, source_target_pairs={{0,1},{1,0},{2,3},{3,2},{4,5},{5,4},{6,7},{7,6},{8,9},{9,8},{10,11... | collective-permute-start | bytes 98312 | tf_op jit(solution)/shard_map/ppermute | solution.py:195
  19.3 0.2 %collective-permute-done.8.got_ref = bf16[32,512]{1,0:T(8,128)(2,1)S(1)} collective-permute-done((bf16[32,512]{1,0:T(8,128)(2,1)S(1)}, bf16[32,512]{1,0:T(8,128)(2,1)S(1)}, u32[]{:S(2)}, u32[]{:S(2)}) %collective-permute-start.8) | collective-permute-done | bytes 32800 | tf_op jit(solution)/shard_map/ppermute | solution.py:195
  19.6 0.0 copy-done.6
  19.6 0.7 %finish.1 = (bf16[16,256]{1,0:T(8,128)(2,1)}, bf16[16,256]{1,0:T(8,128)(2,1)}, f32[16,16]{1,0:T(8,128)}) custom-call(s32[1]{0:T(128)S(6)} %copy.15.kept_ref, f32[1,16]{1,0:T(1,128)S(1)} %copy-done.6, bf16[32,512]{1,0:T(8,128)(2,1)S(1)} %constant_dynamic-update-slice_fusion.mine_ref, bf16[32,512]{1,0:T(8,128)(2,1)S(1)} %collective-permute-done.8.got_ref), custom_call_target="tpu_custom_call" | custom-call | tf_op jit(solution)/shard_map/finish/pallas_call | solution.py:264
  (3 shorter events, 0.0 us)
Async XLA Ops:
  0.6 1.8 %collective-permute-start = (bf16[16,256]{1,0:T(8,128)(2,1)}, bf16[16,256]{1,0:T(8,128)(2,1)S(1)}, u32[]{:S(2)}, u32[]{:S(2)}) collective-permute-start(bf16[16,256]{1,0:T(8,128)(2,1)} %bitcast.23), channel_id=1, source_target_pairs={{0,1},{1,0},{2,3},{3,2},{4,5},{5,4},{6,7},{7,6},{8,9},{9,8},{10,11... | collective-permute-start | bytes 24584 | tf_op jit(solution)/shard_map/ppermute | solution.py:195
  1.1 1.4 %collective-permute-start.1 = (bf16[16,256]{1,0:T(8,128)(2,1)}, bf16[16,256]{1,0:T(8,128)(2,1)S(1)}, u32[]{:S(2)}, u32[]{:S(2)}) collective-permute-start(bf16[16,256]{1,0:T(8,128)(2,1)} %bitcast.25), channel_id=1, source_target_pairs={{0,1},{1,0},{2,3},{3,2},{4,5},{5,4},{6,7},{7,6},{8,9},{9,8},{10,11... | collective-permute-start | bytes 24584 | tf_op jit(solution)/shard_map/ppermute | solution.py:195
  1.2 7.3 %collective-permute-start.4 = (bf16[256,1024]{1,0:T(8,128)(2,1)}, bf16[256,1024]{1,0:T(8,128)(2,1)S(1)}, u32[]{:S(2)}, u32[]{:S(2)}) collective-permute-start(bf16[256,1024]{1,0:T(8,128)(2,1)} %bitcast.19), channel_id=1, source_target_pairs={{0,1},{1,0},{2,3},{3,2},{4,5},{5,4},{6,7},{7,6},{8,9},{9,8},{10,11... | collective-permute-start | bytes 1572872 | tf_op jit(solution)/shard_map/ppermute | solution.py:195
  1.7 0.7 %copy-start.4 = (bf16[1,256,16]{1,2,0:T(8,128)(2,1)S(1)}, bf16[1,256,16]{1,2,0:T(8,128)(2,1)}, u32[]{:S(2)}) copy-start(bf16[1,256,16]{1,2,0:T(8,128)(2,1)} %param.14) | copy-start | bytes 24580
  1.7 0.7 %copy-start.5 = (bf16[1,256,16]{1,2,0:T(8,128)(2,1)S(1)}, bf16[1,256,16]{1,2,0:T(8,128)(2,1)}, u32[]{:S(2)}) copy-start(bf16[1,256,16]{1,2,0:T(8,128)(2,1)} %param.15) | copy-start | bytes 24580
  1.7 0.7 %copy-start.7 = (s32[1,16]{1,0:T(1,128)S(1)}, s32[1,16]{1,0:T(1,128)}, u32[]{:S(2)}) copy-start(s32[1,16]{1,0:T(1,128)} %map_ref.1) | copy-start | bytes 196
  1.7 6.8 %collective-permute-start.5 = (bf16[256,1024]{1,0:T(8,128)(2,1)}, bf16[256,1024]{1,0:T(8,128)(2,1)S(1)}, u32[]{:S(2)}, u32[]{:S(2)}) collective-permute-start(bf16[256,1024]{1,0:T(8,128)(2,1)} %bitcast.21), channel_id=1, source_target_pairs={{0,1},{1,0},{2,3},{3,2},{4,5},{5,4},{6,7},{7,6},{8,9},{9,8},{10,11... | collective-permute-start | bytes 1572872 | tf_op jit(solution)/shard_map/ppermute | solution.py:195
  2.5 6.0 %copy-start = (bf16[1,1024,1024]{2,1,0:T(8,128)(2,1)S(1)}, bf16[1,1024,1024]{2,1,0:T(8,128)(2,1)}, u32[]{:S(2)}) copy-start(bf16[1,1024,1024]{2,1,0:T(8,128)(2,1)} %param.11) | copy-start | bytes 6291460
  2.5 6.0 %copy-start.1 = (bf16[1,1024,1024]{2,1,0:T(8,128)(2,1)S(1)}, bf16[1,1024,1024]{2,1,0:T(8,128)(2,1)}, u32[]{:S(2)}) copy-start(bf16[1,1024,1024]{2,1,0:T(8,128)(2,1)} %param.13) | copy-start | bytes 6291460
  2.5 6.0 %copy-start.2 = (bf16[1,256,1024]{2,1,0:T(8,128)(2,1)S(1)}, bf16[1,256,1024]{2,1,0:T(8,128)(2,1)}, u32[]{:S(2)}) copy-start(bf16[1,256,1024]{2,1,0:T(8,128)(2,1)} %param.10) | copy-start | bytes 1572868
  2.5 6.0 %copy-start.3 = (bf16[1,256,1024]{2,1,0:T(8,128)(2,1)S(1)}, bf16[1,256,1024]{2,1,0:T(8,128)(2,1)}, u32[]{:S(2)}) copy-start(bf16[1,256,1024]{2,1,0:T(8,128)(2,1)} %param.12) | copy-start | bytes 1572868
  2.7 8.4 %collective-permute-start.2 = (bf16[16,512]{1,0:T(8,128)(2,1)S(1)}, bf16[16,512]{1,0:T(8,128)(2,1)S(1)}, u32[]{:S(2)}, u32[]{:S(2)}) collective-permute-start(bf16[16,512]{1,0:T(8,128)(2,1)S(1)} %join_factor.1), channel_id=1, source_target_pairs={{0,6},{1,29},{2,4},{3,31},{4,10},{5,3},{6,8},{7,1},{8,14},{9,7},{1... | collective-permute-start | bytes 49160 | tf_op jit(solution)/shard_map/ppermute | solution.py:204
  6.3 6.4 %collective-permute-start.3 = (bf16[16,512]{1,0:T(8,128)(2,1)S(1)}, bf16[16,512]{1,0:T(8,128)(2,1)S(1)}, u32[]{:S(2)}, u32[]{:S(2)}) collective-permute-start(bf16[16,512]{1,0:T(8,128)(2,1)S(1)} %join_factor.1), channel_id=1, source_target_pairs={{0,4},{1,31},{2,6},{3,29},{4,8},{5,1},{6,10},{7,3},{8,12},{9,5},{1... | collective-permute-start | bytes 49160 | tf_op jit(solution)/shard_map/ppermute | solution.py:204
  8.5 11.0 %copy-start.6 = (f32[1,16]{1,0:T(1,128)S(1)}, f32[1,16]{1,0:T(1,128)}, u32[]{:S(2)}) copy-start(f32[1,16]{1,0:T(1,128)} %singular_ref.1) | copy-start | bytes 196
  13.0 4.7 %collective-permute-start.6 = (bf16[16,512]{1,0:T(8,128)(2,1)S(1)}, bf16[16,512]{1,0:T(8,128)(2,1)S(1)}, u32[]{:S(2)}, u32[]{:S(2)}) collective-permute-start(bf16[16,512]{1,0:T(8,128)(2,1)S(1)} %apply_factor.1), channel_id=1, source_target_pairs={{0,30},{1,7},{2,28},{3,5},{4,2},{5,11},{6,0},{7,9},{8,6},{9,15},{1... | collective-permute-start | bytes 49160 | tf_op jit(solution)/shard_map/ppermute | solution.py:204
  14.2 3.7 %collective-permute-start.7 = (bf16[16,512]{1,0:T(8,128)(2,1)S(1)}, bf16[16,512]{1,0:T(8,128)(2,1)S(1)}, u32[]{:S(2)}, u32[]{:S(2)}) collective-permute-start(bf16[16,512]{1,0:T(8,128)(2,1)S(1)} %apply_factor.1), channel_id=1, source_target_pairs={{0,28},{1,5},{2,30},{3,7},{4,0},{5,9},{6,2},{7,11},{8,4},{9,13},{1... | collective-permute-start | bytes 49160 | tf_op jit(solution)/shard_map/ppermute | solution.py:204
  18.0 1.6 %collective-permute-start.8 = (bf16[32,512]{1,0:T(8,128)(2,1)S(1)}, bf16[32,512]{1,0:T(8,128)(2,1)S(1)}, u32[]{:S(2)}, u32[]{:S(2)}) collective-permute-start(bf16[32,512]{1,0:T(8,128)(2,1)S(1)} %constant_dynamic-update-slice_fusion.mine_ref), channel_id=1, source_target_pairs={{0,1},{1,0},{2,3},{3,2},{4,5},{5,4},{6,7},{7,6},{8,9},{9,8},{10,11... | collective-permute-start | bytes 98312 | tf_op jit(solution)/shard_map/ppermute | solution.py:195
